TPU v7x, 32 devices: a whole 2x2x4 slice. The times are simulated.
32 devices in a mesh: parts: 2 (over x), bins: 8 (over z, y), pix: 2 (over core).
Axes of the slice: x: 2, y: 2, z: 4, core: 2. Of those that a mesh axis runs over, the one named last changes fastest.
Arguments:
- spectra: bfloat16 [16384, 8192], P(('parts', 'pix'), 'bins'), parts along dimension 0, may hold values from -45 to 45
- probes: bfloat16 [16384, 256], P(('parts', 'pix')), parts along dimension 0, may hold values from -6 to 6
Outputs:
- basis: float32 [4, 4096, 256], P(('parts', 'pix'), 'bins'), parts along dimension 0
There are 2 independent parts, one for each index of `parts`. A program takes and returns all parts, laid end to end along the dimension named above; each array names one. Nothing has to cross between parts.
All inputs are finite; a program needn't handle non-finite values.
Results may differ from a plain program's by a relative error of at most 0.0025.
Values may be sent and summed in bfloat16 or wider, within the bound.
No kernel may reach another device: no remote copies, remote signals or barrier semaphores. Data moves between devices by JAX's collectives and lax.ppermute only.
A program may use at most 64 MiB of HBM per device.

v0:
```python
import jax
import jax.numpy as jnp
from jax import lax
from jax.sharding import PartitionSpec as P


def on_device(spectra, probes):
    rows_dev = spectra.shape[0]
    width_cols = probes.shape[1]
    bin_terms = lax.dot_general(
        spectra, probes, (((0,), (0,)), ((), ())), preferred_element_type=jnp.float32
    )
    loadings = lax.psum(bin_terms, "pix").astype(jnp.bfloat16)
    own_rows = rows_dev // lax.axis_size("bins")
    image_full = lax.psum(jnp.dot(spectra, loadings, preferred_element_type=jnp.float32), "bins")
    gram_local = lax.dot_general(
        image_full, image_full, (((0,), (0,)), ((), ())), precision=lax.Precision.HIGHEST
    )
    gram_matrix = lax.psum(gram_local, "pix")
    image_rows = lax.dynamic_slice_in_dim(
        image_full, lax.axis_index("bins") * own_rows, own_rows, 0
    )
    gram_matrix = gram_matrix / jnp.float32(rows_dev * lax.axis_size("pix"))
    factor = jnp.linalg.cholesky(gram_matrix)
    basis = jax.scipy.linalg.solve_triangular(factor, image_rows.T, lower=True).T
    return basis.reshape(1, own_rows, width_cols)


def solution(mesh):
    return jax.shard_map(
        on_device,
        mesh=mesh,
        in_specs=(P(("parts", "pix"), "bins"), P(("parts", "pix"), None)),
        out_specs=P(("parts", "pix"), "bins", None),
        check_vma=False,
    )
```

profile of v0, /device:TPU:0, one launch (start us, length us, event | category | flops | bytes accessed | tf_op | source)
XLA Modules:
  0.0 284.0 jit_solution(13907273541797249808)
XLA Ops:
  6.5 0.0 copy-start
  6.5 1.6 copy-done
  8.1 5.7 %fusion.10 = f32[1024,256]{1,0:T(8,128)S(1)} fusion(bf16[4096,1024]{1,0:T(8,128)(2,1)} %param.2, bf16[4096,256]{1,0:T(8,128)(2,1)S(1)} %copy-done), kind=kOutput, calls=%fused_computation.33 | convolution fusion | flops 2147483648 | bytes 11534336 | tf_op jit(solution)/shard_map/dot_general | solution.py:10
  13.9 6.9 %all-reduce.8 = bf16[1024,256]{1,0:T(8,128)(2,1)} all-reduce(f32[1024,256]{1,0:T(8,128)S(1)} %fusion.10), channel_id=1, replica_groups=mesh['parts'=2,'bins'=8,'pix'=2] {'pix'}, use_global_device_ids=true, to_apply=%region_0.0 | all-reduce | flops 262144 | bytes 1572864 | tf_op jit(solution)/shard_map/psum | solution.py:13
  20.8 7.9 %convolution_bitcast_fusion = f32[4096,256]{0,1:T(8,128)} fusion(bf16[4096,1024]{1,0:T(8,128)(2,1)} %param.2, bf16[1024,256]{1,0:T(8,128)(2,1)} %all-reduce.8), kind=kOutput, calls=%fused_computation.2 | convolution fusion | flops 2147483648 | bytes 13107200 | tf_op jit(solution)/shard_map/dot_general | solution.py:15
  28.7 0.0 all-reduce.5.cloned.1.call-update
  28.8 0.2 all-reduce.7.cloned.1.call-start
  29.0 158.7 %all-reduce.5.cloned.1.call-done = f32[4096,256]{0,1:T(8,128)} async-done(((f32[4096,256]{0,1:T(8,128)}), f32[4096,256]{0,1:T(8,128)}) %all-reduce.5.cloned.1.call-update) | async-done | bytes 4194320 | tf_op jit(solution)/shard_map/psum | solution.py:15
  187.6 7.7 %fusion.11 = f32[256,256]{0,1:T(8,128)} fusion(f32[4096,256]{0,1:T(8,128)} %all-reduce.5.cloned.1.call-done), kind=kOutput, calls=%fused_computation.34 | convolution fusion | flops 3221225472 | bytes 4456448 | tf_op jit(solution)/shard_map/dot_general | solution.py:16
  195.3 0.0 all-reduce.7.cloned.1.call-update
  195.4 1.1 dynamic-slice_bitcast_fusion
  196.5 16.3 %all-reduce.7.cloned.1.call-done = f32[256,256]{0,1:T(8,128)} async-done(((f32[256,256]{0,1:T(8,128)}), f32[256,256]{0,1:T(8,128)}) %all-reduce.7.cloned.1.call-update) | async-done | bytes 262160 | tf_op jit(solution)/shard_map/psum | solution.py:19
  212.8 1.0 broadcast_multiply_fusion
  213.8 0.1 copy.4
  213.9 1.0 fusion.3
  214.9 11.7 %cholesky.50 = f32[128,128]{1,0:T(8,128)S(1)} custom-call(f32[128,128]{1,0:T(8,128)S(1)} %cholesky.118), custom_call_target="Cholesky" | custom-call | tf_op jit(solution)/shard_map/jit(cholesky)/cholesky | solution.py:24
  226.6 9.8 %custom-call.15 = f32[1,128,128]{1,2,0:T(8,128)S(1)} custom-call(f32[1,128,128]{2,1,0:T(8,128)S(1)} %get-tuple-element.26), custom_call_target="InvertDiagBlocksLowerTriangular" | custom-call | tf_op jit(solution)/shard_map/jit(cholesky)/cholesky | solution.py:24
  236.5 0.2 constant_dynamic-update-slice_fusion
  236.7 0.3 convolution_subtract_fusion.1
  237.0 11.9 %cholesky.105 = f32[128,128]{1,0:T(8,128)S(1)} custom-call(f32[128,128]{1,0:T(8,128)S(1)} %convolution_subtract_fusion.1), custom_call_target="Cholesky" | custom-call | tf_op jit(solution)/shard_map/jit(cholesky)/cholesky | solution.py:24
  248.9 0.7 compare_reduce_fusion
  251.0 0.1 triangular_solve.57
  251.1 4.1 %while.1 = (s32[]{:T(128)}, f32[256,256]{1,0:T(8,128)S(1)}, s32[2,2]{1,0:T(2,128)S(1)}, f32[2,128,128]{2,1,0:T(8,128)S(1)}, s32[]{:T(128)}) while((s32[]{:T(128)}, f32[256,256]{1,0:T(8,128)S(1)}, s32[2,2]{1,0:T(2,128)S(1)}, f32[2,128,128]{2,1,0:T(8,128)S(1)}, s32[]{:T(128)}) %tuple.23), condition=%wide.while_cond, body=%wide.while_body.sunk | while | flops 2 | bytes 131181 | solution.py:25
  251.1 0.6 fusion.23
  251.7 1.4 bitcast_dynamic-update-slice_fusion.2
  253.2 0.6 fusion.23
  253.8 1.4 bitcast_dynamic-update-slice_fusion.2
  255.2 19.7 %custom-call.16 = f32[2,128,128]{1,2,0:T(8,128)S(1)} custom-call(f32[2,128,128]{2,1,0:T(8,128)S(1)} %get-tuple-element.12), custom_call_target="InvertDiagBlocksLowerTriangular" | custom-call | tf_op jit(solution)/shard_map/jit(_solve_triangular)/triangular_solve | solution.py:25
  274.9 0.4 fusion.1
  275.3 0.4 convolution_subtract_fusion
  275.7 0.4 fusion.5
  276.2 1.0 copy.5
  (11 shorter events, 0.2 us)
Async XLA Ops:
  6.5 1.6 copy-start
  6.5 181.1 %all-reduce.5.cloned.1.call-start = ((), (), s32[]{:S(2)}) async-start(), calls=%async_computation | async-start | bytes 8388608 | tf_op jit(solution)/shard_map/psum | solution.py:15
  28.8 184.0 %all-reduce.7.cloned.1.call-start = ((), (), s32[]{:S(2)}) async-start(), calls=%async_computation.1 | async-start | bytes 524288 | tf_op jit(solution)/shard_map/psum | solution.py:19
Sparse Core Ops, SparseCore 0:
  28.9 158.7 all-reduce.4
  195.5 17.2 all-reduce.6
where the time goes:
time: 284 us
  waiting for transfers between devices  175 us (62%)
  other arithmetic  55.9 us (20%)
  matrix products  23 us (8%)
  between operations  14.9 us (5%)
  local copies, waits for them, and re-layouts  7.95 us (3%)
  blocking collectives  6.94 us (2%)
    psum x1, waiting for transfers between devices, on_device(): lax.psum(jnp.dot(spectra, loadings, preferred_element_type=jnp.float32),...  159 us
    another operation x6, other arithmetic, on_device(): factor = jnp.linalg.cholesky(gram_matrix)  34.2 us
    another operation x3, other arithmetic, on_device(): jax.scipy.linalg.solve_triangular(factor, image_rows.T, lower=True)  19.7 us
    psum x1, waiting for transfers between devices, on_device(): gram_matrix = lax.psum(gram_local, 'pix')  16.3 us
    dot_general x1, matrix products, on_device(): jnp.dot(spectra, loadings, preferred_element_type=jnp.float32)  7.93 us
    dot_general x1, matrix products, on_device(): lax.dot_general(image_full, image_full, (((0,), (0,)), ((), ())), precisi...  7.69 us
    psum x1, blocking collectives, on_device(): loadings = lax.psum(bin_terms, 'pix').astype(jnp.bfloat16)  6.94 us
    dot_general x1, matrix products, on_device(): lax.dot_general(spectra, probes, (((0,), (0,)), ((), ())), preferred_elem...  5.73 us
  transfers between devices with their start and end apart: 2, of which 2 were waited for; matrix products, arithmetic and copies ran while one was open for 0% of the time, Pallas kernels for 0%

commit v1 on v0

v1 whole, which is shorter than its diff:
```python
import functools
import jax
import jax.numpy as jnp
from jax import lax
from jax.experimental import pallas as pl
from jax.experimental.pallas import tpu as pltpu
from jax.sharding import PartitionSpec as P

CHUNKS = 4
F32 = jnp.float32
BF16 = jnp.bfloat16
MIB = 1 << 20


def params(mib=32):
    return pltpu.CompilerParams(vmem_limit_bytes=mib * MIB)


def image_kernel(idx_ref, spectra_ref, loadings_ref, *out_refs):
    rows = out_refs[0].shape[1]
    for c, out in enumerate(out_refs):
        out[0] = jnp.dot(
            spectra_ref[0, 0, c * rows:(c + 1) * rows, :], loadings_ref[...], preferred_element_type=F32
        ).astype(out.dtype)


def image_half(idx, spectra, loadings, own, dtype):
    outer, _, rows, bins = spectra.shape
    cols = loadings.shape[1]
    piece = rows // CHUNKS
    side = (lambda i, idx: (i, idx[0], 0, 0)) if own else (lambda i, idx: (i, 1 - idx[0], 0, 0))
    return pl.pallas_call(
        image_kernel,
        grid_spec=pltpu.PrefetchScalarGridSpec(
            num_scalar_prefetch=1,
            grid=(outer,),
            in_specs=[
                pl.BlockSpec((1, 1, rows, bins), side),
                pl.BlockSpec((bins, cols), lambda i, idx: (0, 0)),
            ],
            out_specs=[pl.BlockSpec((1, piece, cols), lambda i, idx: (i, 0, 0))] * CHUNKS,
        ),
        out_shape=[jax.ShapeDtypeStruct((outer, piece, cols), dtype)] * CHUNKS,
        compiler_params=params(),
        cost_estimate=pl.CostEstimate(
            flops=2 * outer * rows * bins * cols, bytes_accessed=outer * rows * (bins * 2 + cols * 4), transcendentals=0
        ),
    )(idx, spectra, loadings)


def add_kernel(idx_ref, got_ref, kept_ref, own_ref, *send_refs):
    me = idx_ref[1]
    own_ref[...] = got_ref[me].astype(F32) + kept_ref[me]
    for d, send in enumerate(send_refs):
        other = lax.bitwise_xor(me, d + 1)
        send[...] = (got_ref[other].astype(F32) + kept_ref[other]).astype(send.dtype)


def add_chunk(idx, got, kept):
    outer, piece, cols = got.shape
    vmem = pl.BlockSpec(memory_space=pltpu.VMEM)
    return pl.pallas_call(
        add_kernel,
        in_specs=[pl.BlockSpec(memory_space=pltpu.SMEM), vmem, vmem],
        out_specs=[vmem] * outer,
        out_shape=[jax.ShapeDtypeStruct((piece, cols), F32)]
        + [jax.ShapeDtypeStruct((piece, cols), BF16)] * (outer - 1),
        compiler_params=params(),
        cost_estimate=pl.CostEstimate(
            flops=outer * piece * cols, bytes_accessed=outer * piece * cols * 8, transcendentals=0
        ),
    )(idx, got, kept)


def gram_kernel(n, *refs):
    own_ref, got, (gram_in, x_ref, gram_ref) = refs[0], refs[1:n], refs[n:]
    x = own_ref[...]
    for g in got:
        x = x + g[...].astype(F32)
    x_ref[...] = x
    gram_ref[...] = gram_in[...] + lax.dot_general(
        x, x, (((0,), (0,)), ((), ())), precision=lax.Precision.HIGHEST, preferred_element_type=F32
    )


def gram_chunk(own, got, gram):
    piece, cols = own.shape
    n = 1 + len(got)
    vmem = pl.BlockSpec(memory_space=pltpu.VMEM)
    return pl.pallas_call(
        functools.partial(gram_kernel, n),
        in_specs=[vmem] * (n + 1),
        out_specs=[vmem] * 2,
        out_shape=[jax.ShapeDtypeStruct((piece, cols), F32), jax.ShapeDtypeStruct((cols, cols), F32)],
        compiler_params=params(),
        cost_estimate=pl.CostEstimate(
            flops=12 * piece * cols * cols, bytes_accessed=n * piece * cols * 4, transcendentals=0
        ),
    )(own, *got, gram)


def xor_pairs(n, d):
    return [(i, i ^ d) for i in range(n)]


def on_device(n_bins, spectra, probes):
    rows_dev, bins = spectra.shape
    cols = probes.shape[1]
    outer = n_bins // 2
    rows = rows_dev // n_bins
    half = cols // 2
    me = lax.axis_index("bins")
    pix = lax.axis_index("pix")
    idx = jnp.stack([me % 2, me // 2]).astype(jnp.int32)

    terms = lax.dot_general(spectra, probes, (((0,), (0,)), ((), ())), preferred_element_type=F32)
    loadings = (terms + lax.ppermute(terms, "pix", xor_pairs(2, 1))).astype(BF16)

    blocks = spectra.reshape(outer, 2, rows, bins)
    away = image_half(idx, blocks, loadings, False, BF16)
    kept = image_half(idx, blocks, loadings, True, F32)
    gram = jnp.zeros((cols, cols), F32)
    image = []
    for c in range(CHUNKS):
        got = lax.ppermute(away[c], "bins", xor_pairs(n_bins, 1))
        own, *sends = add_chunk(idx, got, kept[c])
        arrived = [lax.ppermute(s, "bins", xor_pairs(n_bins, 2 * (d + 1))) for d, s in enumerate(sends)]
        x, gram = gram_chunk(own, arrived, gram)
        image.append(x)
    image_rows = jnp.concatenate(image, 0)

    corner = gram[half:, half:]
    lower = lax.broadcasted_iota(jnp.int32, (half, half), 0) >= lax.broadcasted_iota(jnp.int32, (half, half), 1)
    diag = jnp.sum(jnp.where(jnp.eye(half, dtype=bool), corner, 0.0), 0)
    packed = [
        jnp.concatenate([gram[half:, :half], jnp.zeros((8, half), F32)], 0),
        jnp.concatenate([jnp.where(lower, gram[:half, :half], corner), jnp.broadcast_to(diag, (8, half))], 0),
    ]
    mine = jnp.where(pix == 0, packed[0], packed[1])
    other = jnp.where(pix == 0, packed[1], packed[0])
    mine = mine + lax.ppermute(other, "pix", xor_pairs(2, 1))
    d = 1
    while d < n_bins:
        mine = mine + lax.ppermute(mine, "bins", xor_pairs(n_bins, d))
        d *= 2
    other = lax.ppermute(mine, "pix", xor_pairs(2, 1))
    below = jnp.where(pix == 0, mine, other)[:half]
    diags = jnp.where(pix == 0, other, mine)
    strict = jnp.where(lower, 0.0, diags[:half])
    first = jnp.where(lower, diags[:half], diags[:half].T)
    corner = strict + strict.T + jnp.where(jnp.eye(half, dtype=bool), diags[half], 0.0)
    gram_matrix = jnp.concatenate(
        [jnp.concatenate([first, below.T], 1), jnp.concatenate([below, corner], 1)], 0
    ) / F32(rows_dev * 2)

    factor = jnp.linalg.cholesky(gram_matrix)
    basis = jax.scipy.linalg.solve_triangular(factor, image_rows.T, lower=True).T
    return basis.reshape(1, rows, cols)


def solution(mesh):
    return jax.shard_map(
        functools.partial(on_device, mesh.shape["bins"]),
        mesh=mesh,
        in_specs=(P(("parts", "pix"), "bins"), P(("parts", "pix"), None)),
        out_specs=P(("parts", "pix"), "bins", None),
        check_vma=False,
    )
```

time: 284 us -> 156 us (0.55)
  waiting for transfers between devices: 175 us -> 28.5 us
  starting transfers between devices: 0.22 us -> 33.7 us
  matrix products: 23 us -> 9.31 us
  between operations: 14.9 us -> 1.61 us
  Pallas kernels: 0 us -> 10.2 us
  blocking collectives: 6.94 us -> 0 us
  local copies, waits for them, and re-layouts: 7.95 us -> 14 us
    psum x2 -> x0, waiting for transfers between devices: 175 us -> none  [the longest x1 159 us: on_device(): lax.psum(jnp.dot(spectra, loadings, preferred_element_type=jnp.float32),...]
    ppermute x0 -> x22, starting transfers between devices: none -> 33.7 us  [the longest x12 24.5 us: on_device(): lax.ppermute(s, 'bins', xor_pairs(n_bins, 2 * (d + 1)))]
    ppermute x0 -> x22, waiting for transfers between devices: none -> 28.5 us  [the longest x3 13.5 us: on_device(): mine = mine + lax.ppermute(mine, 'bins', xor_pairs(n_bins, d))]
    dot_general x2 -> x0, matrix products: 15.6 us -> none  [the longest x1 7.93 us: on_device(): jnp.dot(spectra, loadings, preferred_element_type=jnp.float32)]
    pallas_call x0 -> x10, Pallas kernels: none -> 10.2 us  [the longest x2 4.94 us: image_half(): pl.pallas_call(image_kernel, grid_spec=pltpu.PrefetchScalarGridSpec(num_s...]
    psum x1 -> x0, blocking collectives: 6.94 us -> none  [on_device(): loadings = lax.psum(bin_terms, 'pix').astype(jnp.bfloat16)]
    unnamed x2 -> x4, local copies, waits for them, and re-layouts: 1.59 us -> 4.97 us
    another operation x6 -> x7, other arithmetic: 34.2 us -> 34.9 us  [on_device(): factor = jnp.linalg.cholesky(gram_matrix)]
  transfers between devices with their start and end apart: 2 -> 22, of which waited for: 2 -> 12; matrix products, arithmetic and copies ran while one was open for 0% -> 1% of each run, Pallas kernels for 0% -> 5%
where the time goes in v1:
time: 156 us
  other arithmetic  58.6 us (38%)
  starting transfers between devices  33.7 us (22%)
  waiting for transfers between devices  28.5 us (18%)
  local copies, waits for them, and re-layouts  14 us (9%)
  Pallas kernels  10.2 us (7%)
  matrix products  9.31 us (6%)
  between operations  1.61 us (1%)
    another operation x7, other arithmetic, on_device(): factor = jnp.linalg.cholesky(gram_matrix)  34.9 us
    ppermute x12, starting transfers between devices, on_device(): lax.ppermute(s, 'bins', xor_pairs(n_bins, 2 * (d + 1)))  24.5 us
    another operation x3, other arithmetic, on_device(): jax.scipy.linalg.solve_triangular(factor, image_rows.T, lower=True)  21.1 us
    ppermute x3, waiting for transfers between devices, on_device(): mine = mine + lax.ppermute(mine, 'bins', xor_pairs(n_bins, d))  13.5 us
    dot_general x1, matrix products, on_device(): lax.dot_general(spectra, probes, (((0,), (0,)), ((), ())), preferred_elem...  5.73 us
    ppermute x4, waiting for transfers between devices, on_device(): got = lax.ppermute(away[c], 'bins', xor_pairs(n_bins, 1))  5.32 us
    another operation x6, local copies, waits for them, and re-layouts  5.3 us
    ppermute x4, starting transfers between devices, on_device(): got = lax.ppermute(away[c], 'bins', xor_pairs(n_bins, 1))  5.06 us
  transfers between devices with their start and end apart: 22, of which 12 were waited for; matrix products, arithmetic and copies ran while one was open for 1% of the time, Pallas kernels for 5%

profile of v1, /device:TPU:0, one launch (start us, length us, event | category | flops | bytes accessed | tf_op | source)
XLA Modules:
  0.0 156.0 jit_solution(17978559023964740232)
XLA Ops:
  0.0 1.6 %copy-done = bf16[4096,256]{1,0:T(8,128)(2,1)S(1)} copy-done((bf16[4096,256]{1,0:T(8,128)(2,1)S(1)}, bf16[4096,256]{1,0:T(8,128)(2,1)}, u32[]{:S(2)}) %copy-start) | copy-done | bytes 2097176
  1.6 5.7 %fusion.13 = f32[1024,256]{1,0:T(8,128)S(1)} fusion(bf16[4096,1024]{1,0:T(8,128)(2,1)} %param.2, bf16[4096,256]{1,0:T(8,128)(2,1)S(1)} %copy-done), kind=kOutput, calls=%fused_computation.48 | convolution fusion | flops 2147483648 | bytes 11534336 | tf_op jit(solution)/shard_map/dot_general | solution.py:116
  7.9 2.3 %collective-permute-done = f32[1024,256]{1,0:T(8,128)} collective-permute-done((f32[1024,256]{1,0:T(8,128)S(1)}, f32[1024,256]{1,0:T(8,128)}, u32[]{:S(2)}, u32[]{:S(2)}) %collective-permute-start) | collective-permute-done | bytes 1048608 | tf_op jit(solution)/shard_map/ppermute | solution.py:117
  11.6 3.4 %copy-done.1 = bf16[4096,1024]{1,0:T(8,128)(2,1)S(1)} copy-done((bf16[4096,1024]{1,0:T(8,128)(2,1)S(1)}, bf16[4096,1024]{1,0:T(8,128)(2,1)}, u32[]{:S(2)}) %copy-start.1) | copy-done | bytes 8388632
  15.0 2.4 %shard_map.28 = (bf16[4,128,256]{2,1,0:T(8,128)(2,1)S(1)}, bf16[4,128,256]{2,1,0:T(8,128)(2,1)S(1)}, bf16[4,128,256]{2,1,0:T(8,128)(2,1)S(1)}, bf16[4,128,256]{2,1,0:T(8,128)(2,1)S(1)}) custom-call(s32[2]{0:T(128)S(1)} %pad_add_fusion.idx_ref, bf16[4,2,512,1024]{3,2,1,0:T(8,128)(2,1)S(1)} %bitcast.49, bf16[1024,256]{1,0:T(8,128)(2,1)S(1)} %add_convert_fusion.loadings_ref), custom_call_target="tpu_custom_call" | custom-call | flops 1073741824 | bytes 6291456 | tf_op jit(solution)/shard_map/pallas_call | solution.py:32
  17.4 3.0 %collective-permute-start.13 = (bf16[4,128,256]{2,1,0:T(8,128)(2,1)S(1)}, bf16[4,128,256]{2,1,0:T(8,128)(2,1)S(1)}, u32[]{:S(2)}, u32[]{:S(2)}) collective-permute-start(bf16[4,128,256]{2,1,0:T(8,128)(2,1)S(1)} %get-tuple-element.55), channel_id=1, source_target_pairs={{0,2},{2,0},{4,6},{6,4},{8,10},{10,8},{12,14},{14,12},{1,3},{3,1},... | collective-permute-start | bytes 786440 | tf_op jit(solution)/shard_map/ppermute | solution.py:125
  20.4 1.9 %collective-permute-start.5 = (bf16[4,128,256]{2,1,0:T(8,128)(2,1)S(1)}, bf16[4,128,256]{2,1,0:T(8,128)(2,1)S(1)}, u32[]{:S(2)}, u32[]{:S(2)}) collective-permute-start(bf16[4,128,256]{2,1,0:T(8,128)(2,1)S(1)} %get-tuple-element.43), channel_id=1, source_target_pairs={{0,2},{2,0},{4,6},{6,4},{8,10},{10,8},{12,14},{14,12},{1,3},{3,1},... | collective-permute-start | bytes 786440 | tf_op jit(solution)/shard_map/ppermute | solution.py:125
  22.4 2.6 %shard_map.29 = (f32[4,128,256]{2,1,0:T(8,128)S(1)}, f32[4,128,256]{2,1,0:T(8,128)S(1)}, f32[4,128,256]{2,1,0:T(8,128)S(1)}, f32[4,128,256]{2,1,0:T(8,128)S(1)}) custom-call(s32[2]{0:T(128)S(1)} %pad_add_fusion.idx_ref, bf16[4,2,512,1024]{3,2,1,0:T(8,128)(2,1)S(1)} %bitcast.50, bf16[1024,256]{1,0:T(8,128)(2,1)S(1)} %add_convert_fusion.loadings_ref), custom_call_target="tpu_custom_call" | custom-call | flops 1073741824 | bytes 6291456 | tf_op jit(solution)/shard_map/pallas_call | solution.py:32
  25.0 2.4 %collective-permute-done.13.got_ref = bf16[4,128,256]{2,1,0:T(8,128)(2,1)S(1)} collective-permute-done((bf16[4,128,256]{2,1,0:T(8,128)(2,1)S(1)}, bf16[4,128,256]{2,1,0:T(8,128)(2,1)S(1)}, u32[]{:S(2)}, u32[]{:S(2)}) %collective-permute-start.13) | collective-permute-done | bytes 262176 | tf_op jit(solution)/shard_map/ppermute | solution.py:125
  28.0 2.2 %collective-permute-start.14 = (bf16[128,256]{1,0:T(8,128)(2,1)S(1)}, bf16[128,256]{1,0:T(8,128)(2,1)S(1)}, u32[]{:S(2)}, u32[]{:S(2)}) collective-permute-start(bf16[128,256]{1,0:T(8,128)(2,1)S(1)} %get-tuple-element.58), channel_id=1, source_target_pairs={{0,4},{2,6},{4,0},{6,2},{8,12},{10,14},{12,8},{14,10},{1,5},{3,7},... | collective-permute-start | bytes 196616 | tf_op jit(solution)/shard_map/ppermute | solution.py:127
  30.2 2.6 %collective-permute-start.15 = (bf16[128,256]{1,0:T(8,128)(2,1)S(1)}, bf16[128,256]{1,0:T(8,128)(2,1)S(1)}, u32[]{:S(2)}, u32[]{:S(2)}) collective-permute-start(bf16[128,256]{1,0:T(8,128)(2,1)S(1)} %get-tuple-element.59), channel_id=1, source_target_pairs={{0,8},{2,10},{4,12},{6,14},{8,0},{10,2},{12,4},{14,6},{1,9},{3,11}... | collective-permute-start | bytes 196616 | tf_op jit(solution)/shard_map/ppermute | solution.py:127
  33.0 4.1 %collective-permute-start.16 = (bf16[128,256]{1,0:T(8,128)(2,1)S(1)}, bf16[128,256]{1,0:T(8,128)(2,1)S(1)}, u32[]{:S(2)}, u32[]{:S(2)}) collective-permute-start(bf16[128,256]{1,0:T(8,128)(2,1)S(1)} %get-tuple-element.60), channel_id=1, source_target_pairs={{0,12},{2,14},{4,8},{6,10},{8,4},{10,6},{12,0},{14,2},{1,13},{3,15... | collective-permute-start | bytes 196616 | tf_op jit(solution)/shard_map/ppermute | solution.py:127
  38.7 2.1 %collective-permute-start.10 = (bf16[128,256]{1,0:T(8,128)(2,1)S(1)}, bf16[128,256]{1,0:T(8,128)(2,1)S(1)}, u32[]{:S(2)}, u32[]{:S(2)}) collective-permute-start(bf16[128,256]{1,0:T(8,128)(2,1)S(1)} %get-tuple-element.52), channel_id=1, source_target_pairs={{0,4},{2,6},{4,0},{6,2},{8,12},{10,14},{12,8},{14,10},{1,5},{3,7},... | collective-permute-start | bytes 196616 | tf_op jit(solution)/shard_map/ppermute | solution.py:127
  42.0 1.8 %collective-permute-done.1.got_ref = bf16[4,128,256]{2,1,0:T(8,128)(2,1)S(1)} collective-permute-done((bf16[4,128,256]{2,1,0:T(8,128)(2,1)S(1)}, bf16[4,128,256]{2,1,0:T(8,128)(2,1)S(1)}, u32[]{:S(2)}, u32[]{:S(2)}) %collective-permute-start.1) | collective-permute-done | bytes 262176 | tf_op jit(solution)/shard_map/ppermute | solution.py:125
  43.8 2.8 %collective-permute-start.11 = (bf16[128,256]{1,0:T(8,128)(2,1)S(1)}, bf16[128,256]{1,0:T(8,128)(2,1)S(1)}, u32[]{:S(2)}, u32[]{:S(2)}) collective-permute-start(bf16[128,256]{1,0:T(8,128)(2,1)S(1)} %get-tuple-element.53), channel_id=1, source_target_pairs={{0,8},{2,10},{4,12},{6,14},{8,0},{10,2},{12,4},{14,6},{1,9},{3,11}... | collective-permute-start | bytes 196616 | tf_op jit(solution)/shard_map/ppermute | solution.py:127
  46.6 1.3 collective-permute-start.12
  48.3 2.7 %collective-permute-start.7 = (bf16[128,256]{1,0:T(8,128)(2,1)}, bf16[128,256]{1,0:T(8,128)(2,1)S(1)}, u32[]{:S(2)}, u32[]{:S(2)}) collective-permute-start(bf16[128,256]{1,0:T(8,128)(2,1)} %get-tuple-element.47), channel_id=1, source_target_pairs={{0,8},{2,10},{4,12},{6,14},{8,0},{10,2},{12,4},{14,6},{1,9},{3,11}... | collective-permute-start | bytes 196616 | tf_op jit(solution)/shard_map/ppermute | solution.py:127
  53.6 4.7 %collective-permute-start.3 = (bf16[128,256]{1,0:T(8,128)(2,1)}, bf16[128,256]{1,0:T(8,128)(2,1)S(1)}, u32[]{:S(2)}, u32[]{:S(2)}) collective-permute-start(bf16[128,256]{1,0:T(8,128)(2,1)} %get-tuple-element.41), channel_id=1, source_target_pairs={{0,8},{2,10},{4,12},{6,14},{8,0},{10,2},{12,4},{14,6},{1,9},{3,11}... | collective-permute-start | bytes 196616 | tf_op jit(solution)/shard_map/ppermute | solution.py:127
  59.9 2.7 %collective-permute-done.3.refs_2_ = bf16[128,256]{1,0:T(8,128)(2,1)S(1)} collective-permute-done((bf16[128,256]{1,0:T(8,128)(2,1)}, bf16[128,256]{1,0:T(8,128)(2,1)S(1)}, u32[]{:S(2)}, u32[]{:S(2)}) %collective-permute-start.3) | collective-permute-done | bytes 65568 | tf_op jit(solution)/shard_map/ppermute | solution.py:127
  62.6 2.0 %collective-permute-done.4.refs_3_ = bf16[128,256]{1,0:T(8,128)(2,1)S(1)} collective-permute-done((bf16[128,256]{1,0:T(8,128)(2,1)}, bf16[128,256]{1,0:T(8,128)(2,1)S(1)}, u32[]{:S(2)}, u32[]{:S(2)}) %collective-permute-start.4) | collective-permute-done | bytes 65568 | tf_op jit(solution)/shard_map/ppermute | solution.py:127
  66.8 1.6 %collective-permute-start.18 = (f32[136,128]{0,1:T(8,128)S(1)}, f32[136,128]{0,1:T(8,128)S(1)}, u32[]{:S(2)}, u32[]{:S(2)}) collective-permute-start(f32[136,128]{0,1:T(8,128)S(1)} %fusion.3), channel_id=1, source_target_pairs={{0,2},{2,0},{4,6},{6,4},{8,10},{10,8},{12,14},{14,12},{1,3},{3,1},... | collective-permute-start | bytes 208904 | tf_op jit(solution)/shard_map/ppermute | solution.py:144
  68.3 4.0 %collective-permute-done.18 = f32[136,128]{0,1:T(8,128)S(1)} collective-permute-done((f32[136,128]{0,1:T(8,128)S(1)}, f32[136,128]{0,1:T(8,128)S(1)}, u32[]{:S(2)}, u32[]{:S(2)}) %collective-permute-start.18) | collective-permute-done | bytes 69664 | tf_op jit(solution)/shard_map/ppermute | solution.py:144
  72.6 4.8 %collective-permute-done.19 = f32[136,128]{0,1:T(8,128)S(1)} collective-permute-done((f32[136,128]{0,1:T(8,128)S(1)}, f32[136,128]{0,1:T(8,128)S(1)}, u32[]{:S(2)}, u32[]{:S(2)}) %collective-permute-start.19) | collective-permute-done | bytes 69664 | tf_op jit(solution)/shard_map/ppermute | solution.py:144
  77.4 1.8 %collective-permute-start.20 = (f32[136,128]{0,1:T(8,128)S(1)}, f32[136,128]{0,1:T(8,128)S(1)}, u32[]{:S(2)}, u32[]{:S(2)}) collective-permute-start(f32[136,128]{0,1:T(8,128)S(1)} %add.55), channel_id=1, source_target_pairs={{0,8},{2,10},{4,12},{6,14},{8,0},{10,2},{12,4},{14,6},{1,9},{3,11}... | collective-permute-start | bytes 208904 | tf_op jit(solution)/shard_map/ppermute | solution.py:144
  79.8 4.7 %collective-permute-done.20 = f32[136,128]{0,1:T(8,128)S(1)} collective-permute-done((f32[136,128]{0,1:T(8,128)S(1)}, f32[136,128]{0,1:T(8,128)S(1)}, u32[]{:S(2)}, u32[]{:S(2)}) %collective-permute-start.20) | collective-permute-done | bytes 69664 | tf_op jit(solution)/shard_map/ppermute | solution.py:144
  88.3 11.7 %cholesky.56 = f32[128,128]{1,0:T(8,128)S(1)} custom-call(f32[128,128]{1,0:T(8,128)S(1)} %cholesky.124), custom_call_target="Cholesky" | custom-call | tf_op jit(solution)/shard_map/jit(cholesky)/cholesky | solution.py:156
  100.3 9.8 %custom-call.15 = f32[1,128,128]{1,2,0:T(8,128)S(1)} custom-call(f32[1,128,128]{2,1,0:T(8,128)S(1)} %copy.26), custom_call_target="InvertDiagBlocksLowerTriangular" | custom-call | tf_op jit(solution)/shard_map/jit(cholesky)/cholesky | solution.py:156
  112.3 11.9 %cholesky.112 = f32[128,128]{1,0:T(8,128)S(1)} custom-call(f32[128,128]{1,0:T(8,128)S(1)} %convolution_subtract_fusion.1), custom_call_target="Cholesky" | custom-call | tf_op jit(solution)/shard_map/jit(cholesky)/cholesky | solution.py:156
  127.7 5.3 %while.1 = (s32[]{:T(128)}, f32[256,256]{1,0:T(8,128)S(1)}, s32[2,2]{1,0:T(2,128)S(1)}, f32[2,128,128]{2,1,0:T(8,128)}, s32[]{:T(128)}) while((s32[]{:T(128)}, f32[256,256]{1,0:T(8,128)S(1)}, s32[2,2]{1,0:T(2,128)S(1)}, f32[2,128,128]{2,1,0:T(8,128)}, s32[]{:T(128)}) %tuple.25), condition=%wide.while_cond, body=%wide.while_body.sunk | while | flops 2 | bytes 132705 | solution.py:157
  128.3 2.0 %bitcast_dynamic-update-slice_fusion.2 = f32[2,128,128]{2,1,0:T(8,128)} fusion(f32[2,128,128]{2,1,0:T(8,128)} %get-tuple-element.135, s32[]{:T(128)} %get-tuple-element.132, f32[256,256]{1,0:T(8,128)S(1)} %get-tuple-element.138, s32[]{:T(128)} %bitcast.47, s32[]{:T(128)} %bitcast.48), kind=kLoop, calls=%fused_computation.clone.1 | loop fusion | bytes 132608 | tf_op jit(solution)/shard_map/jit(_solve_triangular)/triangular_solve
  131.0 2.0 %bitcast_dynamic-update-slice_fusion.2 = f32[2,128,128]{2,1,0:T(8,128)} fusion(f32[2,128,128]{2,1,0:T(8,128)} %get-tuple-element.135, s32[]{:T(128)} %get-tuple-element.132, f32[256,256]{1,0:T(8,128)S(1)} %get-tuple-element.138, s32[]{:T(128)} %bitcast.47, s32[]{:T(128)} %bitcast.48), kind=kLoop, calls=%fused_computation.clone.1 | loop fusion | bytes 132608 | tf_op jit(solution)/shard_map/jit(_solve_triangular)/triangular_solve
  133.0 20.5 %custom-call.16 = f32[2,128,128]{1,2,0:T(8,128)S(1)} custom-call(f32[2,128,128]{2,1,0:T(8,128)} %get-tuple-element.76), custom_call_target="InvertDiagBlocksLowerTriangular" | custom-call | tf_op jit(solution)/shard_map/jit(_solve_triangular)/triangular_solve | solution.py:157
  (85 shorter events, 25.2 us)
Async XLA Ops:
  0.0 1.6 %copy-start = (bf16[4096,256]{1,0:T(8,128)(2,1)S(1)}, bf16[4096,256]{1,0:T(8,128)(2,1)}, u32[]{:S(2)}) copy-start(bf16[4096,256]{1,0:T(8,128)(2,1)} %param.3) | copy-start | bytes 6291460
  7.3 2.9 %collective-permute-start = (f32[1024,256]{1,0:T(8,128)S(1)}, f32[1024,256]{1,0:T(8,128)}, u32[]{:S(2)}, u32[]{:S(2)}) collective-permute-start(f32[1024,256]{1,0:T(8,128)S(1)} %fusion.13), channel_id=1, source_target_pairs={{0,1},{1,0},{2,3},{3,2},{4,5},{5,4},{6,7},{7,6},{8,9},{9,8},{10,11... | collective-permute-start | bytes 3145736 | tf_op jit(solution)/shard_map/ppermute | solution.py:117
  11.6 3.4 %copy-start.1 = (bf16[4096,1024]{1,0:T(8,128)(2,1)S(1)}, bf16[4096,1024]{1,0:T(8,128)(2,1)}, u32[]{:S(2)}) copy-start(bf16[4096,1024]{1,0:T(8,128)(2,1)} %param.2) | copy-start | bytes 25165828
  17.4 10.0 %collective-permute-start.13 = (bf16[4,128,256]{2,1,0:T(8,128)(2,1)S(1)}, bf16[4,128,256]{2,1,0:T(8,128)(2,1)S(1)}, u32[]{:S(2)}, u32[]{:S(2)}) collective-permute-start(bf16[4,128,256]{2,1,0:T(8,128)(2,1)S(1)} %get-tuple-element.55), channel_id=1, source_target_pairs={{0,2},{2,0},{4,6},{6,4},{8,10},{10,8},{12,14},{14,12},{1,3},{3,1},... | collective-permute-start | bytes 786440 | tf_op jit(solution)/shard_map/ppermute | solution.py:125
  20.3 12.7 %collective-permute-start.9 = (bf16[4,128,256]{2,1,0:T(8,128)(2,1)S(1)}, bf16[4,128,256]{2,1,0:T(8,128)(2,1)S(1)}, u32[]{:S(2)}, u32[]{:S(2)}) collective-permute-start(bf16[4,128,256]{2,1,0:T(8,128)(2,1)S(1)} %get-tuple-element.49), channel_id=1, source_target_pairs={{0,2},{2,0},{4,6},{6,4},{8,10},{10,8},{12,14},{14,12},{1,3},{3,1},... | collective-permute-start | bytes 786440 | tf_op jit(solution)/shard_map/ppermute | solution.py:125
  20.4 18.2 %collective-permute-start.5 = (bf16[4,128,256]{2,1,0:T(8,128)(2,1)S(1)}, bf16[4,128,256]{2,1,0:T(8,128)(2,1)S(1)}, u32[]{:S(2)}, u32[]{:S(2)}) collective-permute-start(bf16[4,128,256]{2,1,0:T(8,128)(2,1)S(1)} %get-tuple-element.43), channel_id=1, source_target_pairs={{0,2},{2,0},{4,6},{6,4},{8,10},{10,8},{12,14},{14,12},{1,3},{3,1},... | collective-permute-start | bytes 786440 | tf_op jit(solution)/shard_map/ppermute | solution.py:125
  22.4 21.4 %collective-permute-start.1 = (bf16[4,128,256]{2,1,0:T(8,128)(2,1)S(1)}, bf16[4,128,256]{2,1,0:T(8,128)(2,1)S(1)}, u32[]{:S(2)}, u32[]{:S(2)}) collective-permute-start(bf16[4,128,256]{2,1,0:T(8,128)(2,1)S(1)} %get-tuple-element.37), channel_id=1, source_target_pairs={{0,2},{2,0},{4,6},{6,4},{8,10},{10,8},{12,14},{14,12},{1,3},{3,1},... | collective-permute-start | bytes 786440 | tf_op jit(solution)/shard_map/ppermute | solution.py:125
  28.0 18.6 %collective-permute-start.14 = (bf16[128,256]{1,0:T(8,128)(2,1)S(1)}, bf16[128,256]{1,0:T(8,128)(2,1)S(1)}, u32[]{:S(2)}, u32[]{:S(2)}) collective-permute-start(bf16[128,256]{1,0:T(8,128)(2,1)S(1)} %get-tuple-element.58), channel_id=1, source_target_pairs={{0,4},{2,6},{4,0},{6,2},{8,12},{10,14},{12,8},{14,10},{1,5},{3,7},... | collective-permute-start | bytes 196616 | tf_op jit(solution)/shard_map/ppermute | solution.py:127
  30.2 17.8 %collective-permute-start.15 = (bf16[128,256]{1,0:T(8,128)(2,1)S(1)}, bf16[128,256]{1,0:T(8,128)(2,1)S(1)}, u32[]{:S(2)}, u32[]{:S(2)}) collective-permute-start(bf16[128,256]{1,0:T(8,128)(2,1)S(1)} %get-tuple-element.59), channel_id=1, source_target_pairs={{0,8},{2,10},{4,12},{6,14},{8,0},{10,2},{12,4},{14,6},{1,9},{3,11}... | collective-permute-start | bytes 196616 | tf_op jit(solution)/shard_map/ppermute | solution.py:127
  33.0 15.2 %collective-permute-start.16 = (bf16[128,256]{1,0:T(8,128)(2,1)S(1)}, bf16[128,256]{1,0:T(8,128)(2,1)S(1)}, u32[]{:S(2)}, u32[]{:S(2)}) collective-permute-start(bf16[128,256]{1,0:T(8,128)(2,1)S(1)} %get-tuple-element.60), channel_id=1, source_target_pairs={{0,12},{2,14},{4,8},{6,10},{8,4},{10,6},{12,0},{14,2},{1,13},{3,15... | collective-permute-start | bytes 196616 | tf_op jit(solution)/shard_map/ppermute | solution.py:127
  38.7 12.3 %collective-permute-start.10 = (bf16[128,256]{1,0:T(8,128)(2,1)S(1)}, bf16[128,256]{1,0:T(8,128)(2,1)S(1)}, u32[]{:S(2)}, u32[]{:S(2)}) collective-permute-start(bf16[128,256]{1,0:T(8,128)(2,1)S(1)} %get-tuple-element.52), channel_id=1, source_target_pairs={{0,4},{2,6},{4,0},{6,2},{8,12},{10,14},{12,8},{14,10},{1,5},{3,7},... | collective-permute-start | bytes 196616 | tf_op jit(solution)/shard_map/ppermute | solution.py:127
  43.8 9.8 %collective-permute-start.11 = (bf16[128,256]{1,0:T(8,128)(2,1)S(1)}, bf16[128,256]{1,0:T(8,128)(2,1)S(1)}, u32[]{:S(2)}, u32[]{:S(2)}) collective-permute-start(bf16[128,256]{1,0:T(8,128)(2,1)S(1)} %get-tuple-element.53), channel_id=1, source_target_pairs={{0,8},{2,10},{4,12},{6,14},{8,0},{10,2},{12,4},{14,6},{1,9},{3,11}... | collective-permute-start | bytes 196616 | tf_op jit(solution)/shard_map/ppermute | solution.py:127
  46.6 7.0 %collective-permute-start.12 = (bf16[128,256]{1,0:T(8,128)(2,1)S(1)}, bf16[128,256]{1,0:T(8,128)(2,1)S(1)}, u32[]{:S(2)}, u32[]{:S(2)}) collective-permute-start(bf16[128,256]{1,0:T(8,128)(2,1)S(1)} %get-tuple-element.54), channel_id=1, source_target_pairs={{0,12},{2,14},{4,8},{6,10},{8,4},{10,6},{12,0},{14,2},{1,13},{3,15... | collective-permute-start | bytes 196616 | tf_op jit(solution)/shard_map/ppermute | solution.py:127
  48.0 10.3 %collective-permute-start.6 = (bf16[128,256]{1,0:T(8,128)(2,1)S(1)}, bf16[128,256]{1,0:T(8,128)(2,1)S(1)}, u32[]{:S(2)}, u32[]{:S(2)}) collective-permute-start(bf16[128,256]{1,0:T(8,128)(2,1)S(1)} %get-tuple-element.46), channel_id=1, source_target_pairs={{0,4},{2,6},{4,0},{6,2},{8,12},{10,14},{12,8},{14,10},{1,5},{3,7},... | collective-permute-start | bytes 196616 | tf_op jit(solution)/shard_map/ppermute | solution.py:127
  48.3 11.2 %collective-permute-start.7 = (bf16[128,256]{1,0:T(8,128)(2,1)}, bf16[128,256]{1,0:T(8,128)(2,1)S(1)}, u32[]{:S(2)}, u32[]{:S(2)}) collective-permute-start(bf16[128,256]{1,0:T(8,128)(2,1)} %get-tuple-element.47), channel_id=1, source_target_pairs={{0,8},{2,10},{4,12},{6,14},{8,0},{10,2},{12,4},{14,6},{1,9},{3,11}... | collective-permute-start | bytes 196616 | tf_op jit(solution)/shard_map/ppermute | solution.py:127
  51.0 8.4 %collective-permute-start.8 = (bf16[128,256]{1,0:T(8,128)(2,1)}, bf16[128,256]{1,0:T(8,128)(2,1)S(1)}, u32[]{:S(2)}, u32[]{:S(2)}) collective-permute-start(bf16[128,256]{1,0:T(8,128)(2,1)} %get-tuple-element.48), channel_id=1, source_target_pairs={{0,12},{2,14},{4,8},{6,10},{8,4},{10,6},{12,0},{14,2},{1,13},{3,15... | collective-permute-start | bytes 196616 | tf_op jit(solution)/shard_map/ppermute | solution.py:127
  53.6 6.3 %collective-permute-start.2 = (bf16[128,256]{1,0:T(8,128)(2,1)}, bf16[128,256]{1,0:T(8,128)(2,1)S(1)}, u32[]{:S(2)}, u32[]{:S(2)}) collective-permute-start(bf16[128,256]{1,0:T(8,128)(2,1)} %get-tuple-element.40), channel_id=1, source_target_pairs={{0,4},{2,6},{4,0},{6,2},{8,12},{10,14},{12,8},{14,10},{1,5},{3,7},... | collective-permute-start | bytes 196616 | tf_op jit(solution)/shard_map/ppermute | solution.py:127
  53.6 9.0 %collective-permute-start.3 = (bf16[128,256]{1,0:T(8,128)(2,1)}, bf16[128,256]{1,0:T(8,128)(2,1)S(1)}, u32[]{:S(2)}, u32[]{:S(2)}) collective-permute-start(bf16[128,256]{1,0:T(8,128)(2,1)} %get-tuple-element.41), channel_id=1, source_target_pairs={{0,8},{2,10},{4,12},{6,14},{8,0},{10,2},{12,4},{14,6},{1,9},{3,11}... | collective-permute-start | bytes 196616 | tf_op jit(solution)/shard_map/ppermute | solution.py:127
  58.3 6.3 %collective-permute-start.4 = (bf16[128,256]{1,0:T(8,128)(2,1)}, bf16[128,256]{1,0:T(8,128)(2,1)S(1)}, u32[]{:S(2)}, u32[]{:S(2)}) collective-permute-start(bf16[128,256]{1,0:T(8,128)(2,1)} %get-tuple-element.42), channel_id=1, source_target_pairs={{0,12},{2,14},{4,8},{6,10},{8,4},{10,6},{12,0},{14,2},{1,13},{3,15... | collective-permute-start | bytes 196616 | tf_op jit(solution)/shard_map/ppermute | solution.py:127
  65.3 1.4 collective-permute-start.17
  66.8 5.6 %collective-permute-start.18 = (f32[136,128]{0,1:T(8,128)S(1)}, f32[136,128]{0,1:T(8,128)S(1)}, u32[]{:S(2)}, u32[]{:S(2)}) collective-permute-start(f32[136,128]{0,1:T(8,128)S(1)} %fusion.3), channel_id=1, source_target_pairs={{0,2},{2,0},{4,6},{6,4},{8,10},{10,8},{12,14},{14,12},{1,3},{3,1},... | collective-permute-start | bytes 208904 | tf_op jit(solution)/shard_map/ppermute | solution.py:144
  72.4 5.0 %collective-permute-start.19 = (f32[136,128]{0,1:T(8,128)S(1)}, f32[136,128]{0,1:T(8,128)S(1)}, u32[]{:S(2)}, u32[]{:S(2)}) collective-permute-start(f32[136,128]{0,1:T(8,128)S(1)} %add.54), channel_id=1, source_target_pairs={{0,4},{2,6},{4,0},{6,2},{8,12},{10,14},{12,8},{14,10},{1,5},{3,7},... | collective-permute-start | bytes 208904 | tf_op jit(solution)/shard_map/ppermute | solution.py:144
  77.4 7.1 %collective-permute-start.20 = (f32[136,128]{0,1:T(8,128)S(1)}, f32[136,128]{0,1:T(8,128)S(1)}, u32[]{:S(2)}, u32[]{:S(2)}) collective-permute-start(f32[136,128]{0,1:T(8,128)S(1)} %add.55), channel_id=1, source_target_pairs={{0,8},{2,10},{4,12},{6,14},{8,0},{10,2},{12,4},{14,6},{1,9},{3,11}... | collective-permute-start | bytes 208904 | tf_op jit(solution)/shard_map/ppermute | solution.py:144
  84.5 1.4 collective-permute-start.21

commit v2 on v1

--- a/solution.py
+++ b/solution.py
@@ -1,4 +1,5 @@
 import functools
+import math
 import jax
 import jax.numpy as jnp
 from jax import lax
@@ -7,6 +8,7 @@
 from jax.sharding import PartitionSpec as P
 
 CHUNKS = 4
+PANEL = 16
 F32 = jnp.float32
 BF16 = jnp.bfloat16
 MIB = 1 << 20
@@ -72,31 +74,144 @@
     )(idx, got, kept)
 
 
-def gram_kernel(n, *refs):
-    own_ref, got, (gram_in, x_ref, gram_ref) = refs[0], refs[1:n], refs[n:]
+def gram_kernel(n, last, *refs):
+    if last:
+        pix_ref, refs = refs[0], refs[1:]
+    own_ref, got, (gram_in, x_ref, *out) = refs[0], refs[1:n], refs[n:]
     x = own_ref[...]
     for g in got:
         x = x + g[...].astype(F32)
     x_ref[...] = x
-    gram_ref[...] = gram_in[...] + lax.dot_general(
+    gram = gram_in[...] + lax.dot_general(
         x, x, (((0,), (0,)), ((), ())), precision=lax.Precision.HIGHEST, preferred_element_type=F32
     )
-
-
-def gram_chunk(own, got, gram):
+    if not last:
+        out[0][...] = gram
+        return
+    half = gram.shape[0] // 2
+    mine, other = out
+    row = lax.broadcasted_iota(jnp.int32, (half, half), 0)
+    col = lax.broadcasted_iota(jnp.int32, (half, half), 1)
+    corner = gram[half:, half:]
+    diag = jnp.sum(jnp.where(row == col, corner, 0.0), 0, keepdims=True)
+    above = gram[:half, half:]
+    both = jnp.where(row >= col, gram[:half, :half], corner)
+    first = pix_ref[0] == 0
+    mine[:half] = jnp.where(first, above, both)
+    other[:half] = jnp.where(first, both, above)
+    mine[half:] = jnp.broadcast_to(diag, (8, half))
+    other[half:] = jnp.broadcast_to(diag, (8, half))
+
+
+def gram_chunk(own, got, gram, pix=None):
     piece, cols = own.shape
     n = 1 + len(got)
+    half = cols // 2
     vmem = pl.BlockSpec(memory_space=pltpu.VMEM)
-    return pl.pallas_call(
-        functools.partial(gram_kernel, n),
-        in_specs=[vmem] * (n + 1),
-        out_specs=[vmem] * 2,
-        out_shape=[jax.ShapeDtypeStruct((piece, cols), F32), jax.ShapeDtypeStruct((cols, cols), F32)],
+    last = pix is not None
+    shapes = [(half + 8, half)] * 2 if last else [(cols, cols)]
+    return pl.pallas_call(
+        functools.partial(gram_kernel, n, last),
+        in_specs=[pl.BlockSpec(memory_space=pltpu.SMEM)] * last + [vmem] * (n + 1),
+        out_specs=[vmem] * (1 + len(shapes)),
+        out_shape=[jax.ShapeDtypeStruct(s, F32) for s in [(piece, cols)] + shapes],
         compiler_params=params(),
         cost_estimate=pl.CostEstimate(
             flops=12 * piece * cols * cols, bytes_accessed=n * piece * cols * 4, transcendentals=0
         ),
-    )(own, *got, gram)
+    )(*[pix] * last, own, *got, gram)
+
+
+def transposed_dot(a, b):
+    return lax.dot_general(
+        a, b, (((0,), (0,)), ((), ())), precision=lax.Precision.HIGHEST, preferred_element_type=F32
+    )
+
+
+def wide(column, width):
+    return column if width == 128 else jnp.concatenate([column] * (width // 128), 1)
+
+
+def invert_factor(gram, inverse):
+    n = gram.shape[0]
+    row = lax.broadcasted_iota(jnp.int32, (PANEL, 128), 0)
+    for k in range(0, n, PANEL):
+        end = k + PANEL
+        start, reach = k // 128 * 128, -(-end // 128) * 128
+        right, left = gram[k:end, start:n], inverse[k:end, :reach]
+        width = n - start
+        columns = [jnp.broadcast_to(right[:, k - start + j:k - start + j + 1], (PANEL, 128)) for j in range(PANEL)]
+        pivots = jnp.ones((PANEL, 128), F32)
+        for j in range(0, PANEL, 2):
+            c0, c1 = columns[j], columns[j + 1]
+            a, b, c = c0[j:j + 1], c1[j:j + 1], c1[j + 1:j + 2]
+            det = a * c - b * b
+            inv_a, inv_det = 1.0 / a, 1.0 / det
+            pivots = jnp.where(row == j, a, jnp.where(row == j + 1, det * inv_a, pivots))
+            below = row > j + 1
+            g0 = jnp.where(below, (c0 * c - c1 * b) * inv_det, jnp.where(row == j + 1, b * inv_a, 0.0))
+            g1 = jnp.where(below, (c1 * a - c0 * b) * inv_det, 0.0)
+            for m in range(j + 2, PANEL):
+                columns[m] = columns[m] - g0 * columns[m][j:j + 1] - g1 * columns[m][j + 1:j + 2]
+            right = right - wide(g0, width) * right[j:j + 1] - wide(g1, width) * right[j + 1:j + 2]
+            left = left - wide(g0, reach) * left[j:j + 1] - wide(g1, reach) * left[j + 1:j + 2]
+        scale = lax.rsqrt(pivots)
+        right, left = right * wide(scale, width), left * wide(scale, reach)
+        inverse[k:end, :reach] = left
+        if end < n:
+            base = end // 128 * 128
+            rest = right[:, base - start:]
+            gram[end:n, base:n] = gram[end:n, base:n] - transposed_dot(rest, rest)[end - base:]
+            inverse[end:n, :reach] = inverse[end:n, :reach] - transposed_dot(rest, left)[end - base:]
+
+
+def basis_kernel(pixels, pix_ref, mine_ref, other_ref, *refs):
+    pieces, (basis_ref, gram, inverse) = refs[:-3], refs[-3:]
+    n = gram.shape[0]
+    half = n // 2
+    first = pix_ref[0] == 0
+    mine, other = mine_ref[...], other_ref[...]
+    above = jnp.where(first, mine[:half], other[:half])
+    both = jnp.where(first, other, mine)
+    row = lax.broadcasted_iota(jnp.int32, (half, half), 0)
+    col = lax.broadcasted_iota(jnp.int32, (half, half), 1)
+    eye = row == col
+    both, corner = both[:half], both[half:half + 1]
+    turned = both.T
+    blocks = [jnp.where(row >= col, both, turned), jnp.where(eye, corner, jnp.where(row > col, turned, both))]
+    across = [lax.rsqrt(jnp.sum(jnp.where(eye, blk, 0.0), 0, keepdims=True)) for blk in blocks]
+    down = [lax.rsqrt(jnp.sum(jnp.where(eye, blk, 0.0), 1, keepdims=True)) for blk in blocks]
+    gram[:half, :half] = blocks[0] * across[0] * down[0]
+    gram[:half, half:] = above * across[1] * down[0]
+    gram[half:, half:] = blocks[1] * across[1] * down[1]
+    zero = jnp.zeros((half, half), F32)
+    root = math.sqrt(pixels)
+    inverse[:half, :half] = jnp.where(eye, jnp.broadcast_to(across[0] * root, (half, half)), 0.0)
+    inverse[half:, half:] = jnp.where(eye, jnp.broadcast_to(across[1] * root, (half, half)), 0.0)
+    inverse[:half, half:] = zero
+    inverse[half:, :half] = zero
+    invert_factor(gram, inverse)
+    rows = 0
+    for x in pieces:
+        basis_ref[rows:rows + x.shape[0]] = lax.dot_general(
+            x[...], inverse[...], (((1,), (1,)), ((), ())),
+            precision=lax.Precision.HIGHEST, preferred_element_type=F32,
+        )
+        rows += x.shape[0]
+
+
+def basis_of(pix, mine, other, image, pixels):
+    cols = image[0].shape[1]
+    rows = sum(x.shape[0] for x in image)
+    vmem = pl.BlockSpec(memory_space=pltpu.VMEM)
+    return pl.pallas_call(
+        functools.partial(basis_kernel, pixels),
+        in_specs=[pl.BlockSpec(memory_space=pltpu.SMEM)] + [vmem] * (2 + len(image)),
+        out_specs=vmem,
+        out_shape=jax.ShapeDtypeStruct((rows, cols), F32),
+        scratch_shapes=[pltpu.VMEM((cols, cols), F32)] * 2,
+        compiler_params=params(),
+    )(pix, mine, other, *image)
 
 
 def xor_pairs(n, d):
@@ -108,9 +223,8 @@
     cols = probes.shape[1]
     outer = n_bins // 2
     rows = rows_dev // n_bins
-    half = cols // 2
     me = lax.axis_index("bins")
-    pix = lax.axis_index("pix")
+    pix = lax.axis_index("pix").astype(jnp.int32).reshape(1)
     idx = jnp.stack([me % 2, me // 2]).astype(jnp.int32)
 
     terms = lax.dot_general(spectra, probes, (((0,), (0,)), ((), ())), preferred_element_type=F32)
@@ -125,36 +239,19 @@
         got = lax.ppermute(away[c], "bins", xor_pairs(n_bins, 1))
         own, *sends = add_chunk(idx, got, kept[c])
         arrived = [lax.ppermute(s, "bins", xor_pairs(n_bins, 2 * (d + 1))) for d, s in enumerate(sends)]
-        x, gram = gram_chunk(own, arrived, gram)
+        if c < CHUNKS - 1:
+            x, gram = gram_chunk(own, arrived, gram)
+        else:
+            x, mine, other = gram_chunk(own, arrived, gram, pix)
         image.append(x)
-    image_rows = jnp.concatenate(image, 0)
-
-    corner = gram[half:, half:]
-    lower = lax.broadcasted_iota(jnp.int32, (half, half), 0) >= lax.broadcasted_iota(jnp.int32, (half, half), 1)
-    diag = jnp.sum(jnp.where(jnp.eye(half, dtype=bool), corner, 0.0), 0)
-    packed = [
-        jnp.concatenate([gram[half:, :half], jnp.zeros((8, half), F32)], 0),
-        jnp.concatenate([jnp.where(lower, gram[:half, :half], corner), jnp.broadcast_to(diag, (8, half))], 0),
-    ]
-    mine = jnp.where(pix == 0, packed[0], packed[1])
-    other = jnp.where(pix == 0, packed[1], packed[0])
+
     mine = mine + lax.ppermute(other, "pix", xor_pairs(2, 1))
     d = 1
     while d < n_bins:
         mine = mine + lax.ppermute(mine, "bins", xor_pairs(n_bins, d))
         d *= 2
     other = lax.ppermute(mine, "pix", xor_pairs(2, 1))
-    below = jnp.where(pix == 0, mine, other)[:half]
-    diags = jnp.where(pix == 0, other, mine)
-    strict = jnp.where(lower, 0.0, diags[:half])
-    first = jnp.where(lower, diags[:half], diags[:half].T)
-    corner = strict + strict.T + jnp.where(jnp.eye(half, dtype=bool), diags[half], 0.0)
-    gram_matrix = jnp.concatenate(
-        [jnp.concatenate([first, below.T], 1), jnp.concatenate([below, corner], 1)], 0
-    ) / F32(rows_dev * 2)
-
-    factor = jnp.linalg.cholesky(gram_matrix)
-    basis = jax.scipy.linalg.solve_triangular(factor, image_rows.T, lower=True).T
+    basis = basis_of(pix, mine, other, image, 2 * rows_dev)
     return basis.reshape(1, rows, cols)
 
 

time: 156 us -> 95 us (0.61)
  other arithmetic: 58.6 us -> 1.44 us
  Pallas kernels: 10.2 us -> 22.3 us
  local copies, waits for them, and re-layouts: 14 us -> 4.99 us
  matrix products: 9.31 us -> 5.73 us
  waiting for transfers between devices: 28.5 us -> 26.4 us
    another operation x10 -> x0, other arithmetic: 56 us -> none  [the longest x7 34.9 us: on_device(): factor = jnp.linalg.cholesky(gram_matrix)]
    pallas_call x4 -> x5, Pallas kernels: 1.67 us -> 14.4 us  [the longest x1 12.7 us: basis_of(): pl.pallas_call(functools.partial(basis_kernel, pixels), in_specs=[pl.Bloc...]
    another operation x13 -> x0, local copies, waits for them, and re-layouts: 7.21 us -> none
    another operation x5 -> x0, matrix products: 3.58 us -> none  [the longest x2 2.15 us: on_device(): factor = jnp.linalg.cholesky(gram_matrix)]
    ppermute x3, waiting for transfers between devices: 13.5 us -> 10.8 us  [on_device(): mine = mine + lax.ppermute(mine, 'bins', xor_pairs(n_bins, d))]
  transfers between devices with their start and end apart: 22 -> 22, of which waited for: 12 -> 12; matrix products, arithmetic and copies ran while one was open for 1% -> 0% of each run, Pallas kernels for 5% -> 7%
where the time goes in v2:
time: 95 us; the launch traced here: 94.8 us
  starting transfers between devices  33.7 us (35%)
  waiting for transfers between devices  26.4 us (28%)
  Pallas kernels  22.3 us (23%)
  matrix products  5.73 us (6%)
  local copies, waits for them, and re-layouts  4.99 us (5%)
  other arithmetic  1.44 us (2%)
    ppermute x12, starting transfers between devices, on_device(): lax.ppermute(s, 'bins', xor_pairs(n_bins, 2 * (d + 1)))  24.6 us
    pallas_call x1, Pallas kernels, basis_of(): pl.pallas_call(functools.partial(basis_kernel, pixels), in_specs=[pl.Bloc...  12.7 us
    ppermute x3, waiting for transfers between devices, on_device(): mine = mine + lax.ppermute(mine, 'bins', xor_pairs(n_bins, d))  10.8 us
    ppermute x4, waiting for transfers between devices, on_device(): got = lax.ppermute(away[c], 'bins', xor_pairs(n_bins, 1))  6.12 us
    dot_general x1, matrix products, on_device(): lax.dot_general(spectra, probes, (((0,), (0,)), ((), ())), preferred_elem...  5.73 us
    ppermute x4, starting transfers between devices, on_device(): got = lax.ppermute(away[c], 'bins', xor_pairs(n_bins, 1))  5.06 us
    unnamed x4, local copies, waits for them, and re-layouts  4.97 us
    pallas_call x2, Pallas kernels, image_half(): pl.pallas_call(image_kernel, grid_spec=pltpu.PrefetchScalarGridSpec(num_s...  4.94 us
  transfers between devices with their start and end apart: 22, of which 12 were waited for; matrix products, arithmetic and copies ran while one was open for 0% of the time, Pallas kernels for 7%

profile of v2, /device:TPU:0, one launch (start us, length us, event | category | flops | bytes accessed | tf_op | source)
XLA Modules:
  0.0 94.8 jit_solution(6521594029468537514)
XLA Ops:
  0.0 1.6 %copy-done = bf16[4096,256]{1,0:T(8,128)(2,1)S(1)} copy-done((bf16[4096,256]{1,0:T(8,128)(2,1)S(1)}, bf16[4096,256]{1,0:T(8,128)(2,1)}, u32[]{:S(2)}) %copy-start) | copy-done | bytes 2097176
  1.6 5.7 %fusion = f32[1024,256]{1,0:T(8,128)S(1)} fusion(bf16[4096,1024]{1,0:T(8,128)(2,1)} %param.2, bf16[4096,256]{1,0:T(8,128)(2,1)S(1)} %copy-done), kind=kOutput, calls=%fused_computation.2 | convolution fusion | flops 2147483648 | bytes 11534336 | tf_op jit(solution)/shard_map/dot_general | solution.py:230
  7.9 2.3 %collective-permute-done = f32[1024,256]{1,0:T(8,128)} collective-permute-done((f32[1024,256]{1,0:T(8,128)S(1)}, f32[1024,256]{1,0:T(8,128)}, u32[]{:S(2)}, u32[]{:S(2)}) %collective-permute-start) | collective-permute-done | bytes 1048608 | tf_op jit(solution)/shard_map/ppermute | solution.py:231
  10.3 1.3 %add_convert_fusion.loadings_ref = bf16[1024,256]{1,0:T(8,128)(2,1)S(1)} fusion(f32[1024,256]{1,0:T(8,128)S(1)} %fusion, f32[1024,256]{1,0:T(8,128)} %collective-permute-done), kind=kLoop, calls=%fused_computation | loop fusion | flops 524288 | bytes 2621440 | tf_op jit(solution)/shard_map/convert_element_type | solution.py:231
  11.6 3.4 %copy-done.1 = bf16[4096,1024]{1,0:T(8,128)(2,1)S(1)} copy-done((bf16[4096,1024]{1,0:T(8,128)(2,1)S(1)}, bf16[4096,1024]{1,0:T(8,128)(2,1)}, u32[]{:S(2)}) %copy-start.1) | copy-done | bytes 8388632
  15.0 2.6 %shard_map.28 = (bf16[4,128,256]{2,1,0:T(8,128)(2,1)S(1)}, bf16[4,128,256]{2,1,0:T(8,128)(2,1)S(1)}, bf16[4,128,256]{2,1,0:T(8,128)(2,1)S(1)}, bf16[4,128,256]{2,1,0:T(8,128)(2,1)S(1)}) custom-call(s32[2]{0:T(128)S(1)} %pad_add_fusion.idx_ref, bf16[4,2,512,1024]{3,2,1,0:T(8,128)(2,1)S(1)} %bitcast.7, bf16[1024,256]{1,0:T(8,128)(2,1)S(1)} %add_convert_fusion.loadings_ref), custom_call_target="tpu_custom_call" | custom-call | flops 1073741824 | bytes 6291456 | tf_op jit(solution)/shard_map/pallas_call | solution.py:34
  17.6 3.0 %collective-permute-start.13 = (bf16[4,128,256]{2,1,0:T(8,128)(2,1)S(1)}, bf16[4,128,256]{2,1,0:T(8,128)(2,1)S(1)}, u32[]{:S(2)}, u32[]{:S(2)}) collective-permute-start(bf16[4,128,256]{2,1,0:T(8,128)(2,1)S(1)} %get-tuple-element.56), channel_id=1, source_target_pairs={{0,2},{2,0},{4,6},{6,4},{8,10},{10,8},{12,14},{14,12},{1,3},{3,1},... | collective-permute-start | bytes 786440 | tf_op jit(solution)/shard_map/ppermute | solution.py:239
  20.6 1.9 %collective-permute-start.5 = (bf16[4,128,256]{2,1,0:T(8,128)(2,1)S(1)}, bf16[4,128,256]{2,1,0:T(8,128)(2,1)S(1)}, u32[]{:S(2)}, u32[]{:S(2)}) collective-permute-start(bf16[4,128,256]{2,1,0:T(8,128)(2,1)S(1)} %get-tuple-element.44), channel_id=1, source_target_pairs={{0,2},{2,0},{4,6},{6,4},{8,10},{10,8},{12,14},{14,12},{1,3},{3,1},... | collective-permute-start | bytes 786440 | tf_op jit(solution)/shard_map/ppermute | solution.py:239
  22.6 2.4 %shard_map.29 = (f32[4,128,256]{2,1,0:T(8,128)S(1)}, f32[4,128,256]{2,1,0:T(8,128)S(1)}, f32[4,128,256]{2,1,0:T(8,128)S(1)}, f32[4,128,256]{2,1,0:T(8,128)S(1)}) custom-call(s32[2]{0:T(128)S(1)} %pad_add_fusion.idx_ref, bf16[4,2,512,1024]{3,2,1,0:T(8,128)(2,1)S(1)} %bitcast.8, bf16[1024,256]{1,0:T(8,128)(2,1)S(1)} %add_convert_fusion.loadings_ref), custom_call_target="tpu_custom_call" | custom-call | flops 1073741824 | bytes 6291456 | tf_op jit(solution)/shard_map/pallas_call | solution.py:34
  25.0 2.6 %collective-permute-done.13.got_ref = bf16[4,128,256]{2,1,0:T(8,128)(2,1)S(1)} collective-permute-done((bf16[4,128,256]{2,1,0:T(8,128)(2,1)S(1)}, bf16[4,128,256]{2,1,0:T(8,128)(2,1)S(1)}, u32[]{:S(2)}, u32[]{:S(2)}) %collective-permute-start.13) | collective-permute-done | bytes 262176 | tf_op jit(solution)/shard_map/ppermute | solution.py:239
  28.2 2.2 %collective-permute-start.14 = (bf16[128,256]{1,0:T(8,128)(2,1)S(1)}, bf16[128,256]{1,0:T(8,128)(2,1)S(1)}, u32[]{:S(2)}, u32[]{:S(2)}) collective-permute-start(bf16[128,256]{1,0:T(8,128)(2,1)S(1)} %get-tuple-element.59), channel_id=1, source_target_pairs={{0,4},{2,6},{4,0},{6,2},{8,12},{10,14},{12,8},{14,10},{1,5},{3,7},... | collective-permute-start | bytes 196616 | tf_op jit(solution)/shard_map/ppermute | solution.py:241
  30.4 2.6 %collective-permute-start.15 = (bf16[128,256]{1,0:T(8,128)(2,1)S(1)}, bf16[128,256]{1,0:T(8,128)(2,1)S(1)}, u32[]{:S(2)}, u32[]{:S(2)}) collective-permute-start(bf16[128,256]{1,0:T(8,128)(2,1)S(1)} %get-tuple-element.60), channel_id=1, source_target_pairs={{0,8},{2,10},{4,12},{6,14},{8,0},{10,2},{12,4},{14,6},{1,9},{3,11}... | collective-permute-start | bytes 196616 | tf_op jit(solution)/shard_map/ppermute | solution.py:241
  33.2 4.2 %collective-permute-start.16 = (bf16[128,256]{1,0:T(8,128)(2,1)S(1)}, bf16[128,256]{1,0:T(8,128)(2,1)S(1)}, u32[]{:S(2)}, u32[]{:S(2)}) collective-permute-start(bf16[128,256]{1,0:T(8,128)(2,1)S(1)} %get-tuple-element.61), channel_id=1, source_target_pairs={{0,12},{2,14},{4,8},{6,10},{8,4},{10,6},{12,0},{14,2},{1,13},{3,15... | collective-permute-start | bytes 196616 | tf_op jit(solution)/shard_map/ppermute | solution.py:241
  38.0 0.9 collective-permute-done.5.got_ref
  38.8 2.1 %collective-permute-start.10 = (bf16[128,256]{1,0:T(8,128)(2,1)S(1)}, bf16[128,256]{1,0:T(8,128)(2,1)S(1)}, u32[]{:S(2)}, u32[]{:S(2)}) collective-permute-start(bf16[128,256]{1,0:T(8,128)(2,1)S(1)} %get-tuple-element.53), channel_id=1, source_target_pairs={{0,4},{2,6},{4,0},{6,2},{8,12},{10,14},{12,8},{14,10},{1,5},{3,7},... | collective-permute-start | bytes 196616 | tf_op jit(solution)/shard_map/ppermute | solution.py:241
  41.6 2.4 %collective-permute-done.1.got_ref = bf16[4,128,256]{2,1,0:T(8,128)(2,1)S(1)} collective-permute-done((bf16[4,128,256]{2,1,0:T(8,128)(2,1)S(1)}, bf16[4,128,256]{2,1,0:T(8,128)(2,1)S(1)}, u32[]{:S(2)}, u32[]{:S(2)}) %collective-permute-start.1) | collective-permute-done | bytes 262176 | tf_op jit(solution)/shard_map/ppermute | solution.py:239
  44.0 2.8 %collective-permute-start.11 = (bf16[128,256]{1,0:T(8,128)(2,1)S(1)}, bf16[128,256]{1,0:T(8,128)(2,1)S(1)}, u32[]{:S(2)}, u32[]{:S(2)}) collective-permute-start(bf16[128,256]{1,0:T(8,128)(2,1)S(1)} %get-tuple-element.54), channel_id=1, source_target_pairs={{0,8},{2,10},{4,12},{6,14},{8,0},{10,2},{12,4},{14,6},{1,9},{3,11}... | collective-permute-start | bytes 196616 | tf_op jit(solution)/shard_map/ppermute | solution.py:241
  46.8 1.3 %collective-permute-start.12 = (bf16[128,256]{1,0:T(8,128)(2,1)S(1)}, bf16[128,256]{1,0:T(8,128)(2,1)S(1)}, u32[]{:S(2)}, u32[]{:S(2)}) collective-permute-start(bf16[128,256]{1,0:T(8,128)(2,1)S(1)} %get-tuple-element.55), channel_id=1, source_target_pairs={{0,12},{2,14},{4,8},{6,10},{8,4},{10,6},{12,0},{14,2},{1,13},{3,15... | collective-permute-start | bytes 196616 | tf_op jit(solution)/shard_map/ppermute | solution.py:241
  48.4 2.7 %collective-permute-start.7 = (bf16[128,256]{1,0:T(8,128)(2,1)S(1)}, bf16[128,256]{1,0:T(8,128)(2,1)S(1)}, u32[]{:S(2)}, u32[]{:S(2)}) collective-permute-start(bf16[128,256]{1,0:T(8,128)(2,1)S(1)} %get-tuple-element.48), channel_id=1, source_target_pairs={{0,8},{2,10},{4,12},{6,14},{8,0},{10,2},{12,4},{14,6},{1,9},{3,11}... | collective-permute-start | bytes 196616 | tf_op jit(solution)/shard_map/ppermute | solution.py:241
  51.2 1.3 %collective-permute-start.8 = (bf16[128,256]{1,0:T(8,128)(2,1)S(1)}, bf16[128,256]{1,0:T(8,128)(2,1)S(1)}, u32[]{:S(2)}, u32[]{:S(2)}) collective-permute-start(bf16[128,256]{1,0:T(8,128)(2,1)S(1)} %get-tuple-element.49), channel_id=1, source_target_pairs={{0,12},{2,14},{4,8},{6,10},{8,4},{10,6},{12,0},{14,2},{1,13},{3,15... | collective-permute-start | bytes 196616 | tf_op jit(solution)/shard_map/ppermute | solution.py:241
  52.5 1.2 %shard_map.30 = (f32[128,256]{1,0:T(8,128)S(1)}, bf16[128,256]{1,0:T(8,128)(2,1)}, bf16[128,256]{1,0:T(8,128)(2,1)}, bf16[128,256]{1,0:T(8,128)(2,1)}) custom-call(s32[2]{0:T(128)S(1)} %pad_add_fusion.idx_ref, bf16[4,128,256]{2,1,0:T(8,128)(2,1)S(1)} %collective-permute-done.1.got_ref, f32[4,128,256]{2,1,0:T(8,128)S(1)} %get-tuple-element.39.kept_ref), custom_call_target="tpu_custom_call" | custom-call | flops 131072 | bytes 1048576 | tf_op jit(solution)/shard_map/pallas_call | solution.py:64
  53.8 4.7 %collective-permute-start.3 = (bf16[128,256]{1,0:T(8,128)(2,1)}, bf16[128,256]{1,0:T(8,128)(2,1)S(1)}, u32[]{:S(2)}, u32[]{:S(2)}) collective-permute-start(bf16[128,256]{1,0:T(8,128)(2,1)} %get-tuple-element.42), channel_id=1, source_target_pairs={{0,8},{2,10},{4,12},{6,14},{8,0},{10,2},{12,4},{14,6},{1,9},{3,11}... | collective-permute-start | bytes 196616 | tf_op jit(solution)/shard_map/ppermute | solution.py:241
  60.1 2.7 %collective-permute-done.3.refs_3_ = bf16[128,256]{1,0:T(8,128)(2,1)S(1)} collective-permute-done((bf16[128,256]{1,0:T(8,128)(2,1)}, bf16[128,256]{1,0:T(8,128)(2,1)S(1)}, u32[]{:S(2)}, u32[]{:S(2)}) %collective-permute-start.3) | collective-permute-done | bytes 65568 | tf_op jit(solution)/shard_map/ppermute | solution.py:241
  62.7 2.0 %collective-permute-done.4.refs_4_ = bf16[128,256]{1,0:T(8,128)(2,1)S(1)} collective-permute-done((bf16[128,256]{1,0:T(8,128)(2,1)}, bf16[128,256]{1,0:T(8,128)(2,1)S(1)}, u32[]{:S(2)}, u32[]{:S(2)}) %collective-permute-start.4) | collective-permute-done | bytes 65568 | tf_op jit(solution)/shard_map/ppermute | solution.py:241
  65.2 1.2 %collective-permute-done.17 = f32[136,128]{1,0:T(8,128)S(1)} collective-permute-done((f32[136,128]{1,0:T(8,128)S(1)}, f32[136,128]{1,0:T(8,128)S(1)}, u32[]{:S(2)}, u32[]{:S(2)}) %collective-permute-start.17) | collective-permute-done | bytes 69664 | tf_op jit(solution)/shard_map/ppermute | solution.py:248
  66.5 1.6 %collective-permute-start.18 = (f32[136,128]{1,0:T(8,128)S(1)}, f32[136,128]{1,0:T(8,128)S(1)}, u32[]{:S(2)}, u32[]{:S(2)}) collective-permute-start(f32[136,128]{1,0:T(8,128)S(1)} %add.22), channel_id=1, source_target_pairs={{0,2},{2,0},{4,6},{6,4},{8,10},{10,8},{12,14},{14,12},{1,3},{3,1},... | collective-permute-start | bytes 208904 | tf_op jit(solution)/shard_map/ppermute | solution.py:251
  68.1 2.8 %collective-permute-done.18 = f32[136,128]{1,0:T(8,128)S(1)} collective-permute-done((f32[136,128]{1,0:T(8,128)S(1)}, f32[136,128]{1,0:T(8,128)S(1)}, u32[]{:S(2)}, u32[]{:S(2)}) %collective-permute-start.18) | collective-permute-done | bytes 69664 | tf_op jit(solution)/shard_map/ppermute | solution.py:251
  70.9 4.3 %collective-permute-done.19 = f32[136,128]{1,0:T(8,128)S(1)} collective-permute-done((f32[136,128]{1,0:T(8,128)S(1)}, f32[136,128]{1,0:T(8,128)S(1)}, u32[]{:S(2)}, u32[]{:S(2)}) %collective-permute-start.19) | collective-permute-done | bytes 69664 | tf_op jit(solution)/shard_map/ppermute | solution.py:251
  75.3 1.8 %collective-permute-start.20 = (f32[136,128]{1,0:T(8,128)S(1)}, f32[136,128]{1,0:T(8,128)S(1)}, u32[]{:S(2)}, u32[]{:S(2)}) collective-permute-start(f32[136,128]{1,0:T(8,128)S(1)} %add.24), channel_id=1, source_target_pairs={{0,8},{2,10},{4,12},{6,14},{8,0},{10,2},{12,4},{14,6},{1,9},{3,11}... | collective-permute-start | bytes 208904 | tf_op jit(solution)/shard_map/ppermute | solution.py:251
  77.0 3.7 %collective-permute-done.20 = f32[136,128]{1,0:T(8,128)S(1)} collective-permute-done((f32[136,128]{1,0:T(8,128)S(1)}, f32[136,128]{1,0:T(8,128)S(1)}, u32[]{:S(2)}, u32[]{:S(2)}) %collective-permute-start.20) | collective-permute-done | bytes 69664 | tf_op jit(solution)/shard_map/ppermute | solution.py:251
  80.8 1.2 %collective-permute-done.21.other_ref = f32[136,128]{1,0:T(8,128)S(1)} collective-permute-done((f32[136,128]{1,0:T(8,128)S(1)}, f32[136,128]{1,0:T(8,128)S(1)}, u32[]{:S(2)}, u32[]{:S(2)}) %collective-permute-start.21) | collective-permute-done | bytes 69664 | tf_op jit(solution)/shard_map/ppermute | solution.py:253
  82.1 12.7 %shard_map.38 = f32[512,256]{1,0:T(8,128)} custom-call(s32[1]{0:T(128)} %bitcast.refs_0_.pix_ref, f32[136,128]{1,0:T(8,128)S(1)} %add.25.mine_ref, f32[136,128]{1,0:T(8,128)S(1)} %collective-permute-done.21.other_ref, f32[128,256]{1,0:T(8,128)S(1)} %get-tuple-element.67.refs_0_, f32[128,256]{1,0:T(8,128)S(1)} %get-tuple-element.68.refs_1_, ...), custom_call_target="tpu_custom_call" | custom-call | tf_op jit(solution)/shard_map/pallas_call | solution.py:207
  (35 shorter events, 5.3 us)
Async XLA Ops:
  0.0 1.6 %copy-start = (bf16[4096,256]{1,0:T(8,128)(2,1)S(1)}, bf16[4096,256]{1,0:T(8,128)(2,1)}, u32[]{:S(2)}) copy-start(bf16[4096,256]{1,0:T(8,128)(2,1)} %param.3) | copy-start | bytes 6291460
  7.3 2.9 %collective-permute-start = (f32[1024,256]{1,0:T(8,128)S(1)}, f32[1024,256]{1,0:T(8,128)}, u32[]{:S(2)}, u32[]{:S(2)}) collective-permute-start(f32[1024,256]{1,0:T(8,128)S(1)} %fusion), channel_id=1, source_target_pairs={{0,1},{1,0},{2,3},{3,2},{4,5},{5,4},{6,7},{7,6},{8,9},{9,8},{10,11... | collective-permute-start | bytes 3145736 | tf_op jit(solution)/shard_map/ppermute | solution.py:231
  11.6 3.4 %copy-start.1 = (bf16[4096,1024]{1,0:T(8,128)(2,1)S(1)}, bf16[4096,1024]{1,0:T(8,128)(2,1)}, u32[]{:S(2)}) copy-start(bf16[4096,1024]{1,0:T(8,128)(2,1)} %param.2) | copy-start | bytes 25165828
  17.6 10.0 %collective-permute-start.13 = (bf16[4,128,256]{2,1,0:T(8,128)(2,1)S(1)}, bf16[4,128,256]{2,1,0:T(8,128)(2,1)S(1)}, u32[]{:S(2)}, u32[]{:S(2)}) collective-permute-start(bf16[4,128,256]{2,1,0:T(8,128)(2,1)S(1)} %get-tuple-element.56), channel_id=1, source_target_pairs={{0,2},{2,0},{4,6},{6,4},{8,10},{10,8},{12,14},{14,12},{1,3},{3,1},... | collective-permute-start | bytes 786440 | tf_op jit(solution)/shard_map/ppermute | solution.py:239
  20.5 12.7 %collective-permute-start.9 = (bf16[4,128,256]{2,1,0:T(8,128)(2,1)S(1)}, bf16[4,128,256]{2,1,0:T(8,128)(2,1)S(1)}, u32[]{:S(2)}, u32[]{:S(2)}) collective-permute-start(bf16[4,128,256]{2,1,0:T(8,128)(2,1)S(1)} %get-tuple-element.50), channel_id=1, source_target_pairs={{0,2},{2,0},{4,6},{6,4},{8,10},{10,8},{12,14},{14,12},{1,3},{3,1},... | collective-permute-start | bytes 786440 | tf_op jit(solution)/shard_map/ppermute | solution.py:239
  20.6 18.2 %collective-permute-start.5 = (bf16[4,128,256]{2,1,0:T(8,128)(2,1)S(1)}, bf16[4,128,256]{2,1,0:T(8,128)(2,1)S(1)}, u32[]{:S(2)}, u32[]{:S(2)}) collective-permute-start(bf16[4,128,256]{2,1,0:T(8,128)(2,1)S(1)} %get-tuple-element.44), channel_id=1, source_target_pairs={{0,2},{2,0},{4,6},{6,4},{8,10},{10,8},{12,14},{14,12},{1,3},{3,1},... | collective-permute-start | bytes 786440 | tf_op jit(solution)/shard_map/ppermute | solution.py:239
  22.5 21.4 %collective-permute-start.1 = (bf16[4,128,256]{2,1,0:T(8,128)(2,1)S(1)}, bf16[4,128,256]{2,1,0:T(8,128)(2,1)S(1)}, u32[]{:S(2)}, u32[]{:S(2)}) collective-permute-start(bf16[4,128,256]{2,1,0:T(8,128)(2,1)S(1)} %get-tuple-element.38), channel_id=1, source_target_pairs={{0,2},{2,0},{4,6},{6,4},{8,10},{10,8},{12,14},{14,12},{1,3},{3,1},... | collective-permute-start | bytes 786440 | tf_op jit(solution)/shard_map/ppermute | solution.py:239
  28.2 18.6 %collective-permute-start.14 = (bf16[128,256]{1,0:T(8,128)(2,1)S(1)}, bf16[128,256]{1,0:T(8,128)(2,1)S(1)}, u32[]{:S(2)}, u32[]{:S(2)}) collective-permute-start(bf16[128,256]{1,0:T(8,128)(2,1)S(1)} %get-tuple-element.59), channel_id=1, source_target_pairs={{0,4},{2,6},{4,0},{6,2},{8,12},{10,14},{12,8},{14,10},{1,5},{3,7},... | collective-permute-start | bytes 196616 | tf_op jit(solution)/shard_map/ppermute | solution.py:241
  30.4 17.8 %collective-permute-start.15 = (bf16[128,256]{1,0:T(8,128)(2,1)S(1)}, bf16[128,256]{1,0:T(8,128)(2,1)S(1)}, u32[]{:S(2)}, u32[]{:S(2)}) collective-permute-start(bf16[128,256]{1,0:T(8,128)(2,1)S(1)} %get-tuple-element.60), channel_id=1, source_target_pairs={{0,8},{2,10},{4,12},{6,14},{8,0},{10,2},{12,4},{14,6},{1,9},{3,11}... | collective-permute-start | bytes 196616 | tf_op jit(solution)/shard_map/ppermute | solution.py:241
  33.2 15.2 %collective-permute-start.16 = (bf16[128,256]{1,0:T(8,128)(2,1)S(1)}, bf16[128,256]{1,0:T(8,128)(2,1)S(1)}, u32[]{:S(2)}, u32[]{:S(2)}) collective-permute-start(bf16[128,256]{1,0:T(8,128)(2,1)S(1)} %get-tuple-element.61), channel_id=1, source_target_pairs={{0,12},{2,14},{4,8},{6,10},{8,4},{10,6},{12,0},{14,2},{1,13},{3,15... | collective-permute-start | bytes 196616 | tf_op jit(solution)/shard_map/ppermute | solution.py:241
  38.8 12.3 %collective-permute-start.10 = (bf16[128,256]{1,0:T(8,128)(2,1)S(1)}, bf16[128,256]{1,0:T(8,128)(2,1)S(1)}, u32[]{:S(2)}, u32[]{:S(2)}) collective-permute-start(bf16[128,256]{1,0:T(8,128)(2,1)S(1)} %get-tuple-element.53), channel_id=1, source_target_pairs={{0,4},{2,6},{4,0},{6,2},{8,12},{10,14},{12,8},{14,10},{1,5},{3,7},... | collective-permute-start | bytes 196616 | tf_op jit(solution)/shard_map/ppermute | solution.py:241
  44.0 9.8 %collective-permute-start.11 = (bf16[128,256]{1,0:T(8,128)(2,1)S(1)}, bf16[128,256]{1,0:T(8,128)(2,1)S(1)}, u32[]{:S(2)}, u32[]{:S(2)}) collective-permute-start(bf16[128,256]{1,0:T(8,128)(2,1)S(1)} %get-tuple-element.54), channel_id=1, source_target_pairs={{0,8},{2,10},{4,12},{6,14},{8,0},{10,2},{12,4},{14,6},{1,9},{3,11}... | collective-permute-start | bytes 196616 | tf_op jit(solution)/shard_map/ppermute | solution.py:241
  46.8 7.0 %collective-permute-start.12 = (bf16[128,256]{1,0:T(8,128)(2,1)S(1)}, bf16[128,256]{1,0:T(8,128)(2,1)S(1)}, u32[]{:S(2)}, u32[]{:S(2)}) collective-permute-start(bf16[128,256]{1,0:T(8,128)(2,1)S(1)} %get-tuple-element.55), channel_id=1, source_target_pairs={{0,12},{2,14},{4,8},{6,10},{8,4},{10,6},{12,0},{14,2},{1,13},{3,15... | collective-permute-start | bytes 196616 | tf_op jit(solution)/shard_map/ppermute | solution.py:241
  48.1 10.3 %collective-permute-start.6 = (bf16[128,256]{1,0:T(8,128)(2,1)S(1)}, bf16[128,256]{1,0:T(8,128)(2,1)S(1)}, u32[]{:S(2)}, u32[]{:S(2)}) collective-permute-start(bf16[128,256]{1,0:T(8,128)(2,1)S(1)} %get-tuple-element.47), channel_id=1, source_target_pairs={{0,4},{2,6},{4,0},{6,2},{8,12},{10,14},{12,8},{14,10},{1,5},{3,7},... | collective-permute-start | bytes 196616 | tf_op jit(solution)/shard_map/ppermute | solution.py:241
  48.4 11.2 %collective-permute-start.7 = (bf16[128,256]{1,0:T(8,128)(2,1)S(1)}, bf16[128,256]{1,0:T(8,128)(2,1)S(1)}, u32[]{:S(2)}, u32[]{:S(2)}) collective-permute-start(bf16[128,256]{1,0:T(8,128)(2,1)S(1)} %get-tuple-element.48), channel_id=1, source_target_pairs={{0,8},{2,10},{4,12},{6,14},{8,0},{10,2},{12,4},{14,6},{1,9},{3,11}... | collective-permute-start | bytes 196616 | tf_op jit(solution)/shard_map/ppermute | solution.py:241
  51.2 8.4 %collective-permute-start.8 = (bf16[128,256]{1,0:T(8,128)(2,1)S(1)}, bf16[128,256]{1,0:T(8,128)(2,1)S(1)}, u32[]{:S(2)}, u32[]{:S(2)}) collective-permute-start(bf16[128,256]{1,0:T(8,128)(2,1)S(1)} %get-tuple-element.49), channel_id=1, source_target_pairs={{0,12},{2,14},{4,8},{6,10},{8,4},{10,6},{12,0},{14,2},{1,13},{3,15... | collective-permute-start | bytes 196616 | tf_op jit(solution)/shard_map/ppermute | solution.py:241
  53.8 6.3 %collective-permute-start.2 = (bf16[128,256]{1,0:T(8,128)(2,1)}, bf16[128,256]{1,0:T(8,128)(2,1)S(1)}, u32[]{:S(2)}, u32[]{:S(2)}) collective-permute-start(bf16[128,256]{1,0:T(8,128)(2,1)} %get-tuple-element.41), channel_id=1, source_target_pairs={{0,4},{2,6},{4,0},{6,2},{8,12},{10,14},{12,8},{14,10},{1,5},{3,7},... | collective-permute-start | bytes 196616 | tf_op jit(solution)/shard_map/ppermute | solution.py:241
  53.8 9.0 %collective-permute-start.3 = (bf16[128,256]{1,0:T(8,128)(2,1)}, bf16[128,256]{1,0:T(8,128)(2,1)S(1)}, u32[]{:S(2)}, u32[]{:S(2)}) collective-permute-start(bf16[128,256]{1,0:T(8,128)(2,1)} %get-tuple-element.42), channel_id=1, source_target_pairs={{0,8},{2,10},{4,12},{6,14},{8,0},{10,2},{12,4},{14,6},{1,9},{3,11}... | collective-permute-start | bytes 196616 | tf_op jit(solution)/shard_map/ppermute | solution.py:241
  58.4 6.3 %collective-permute-start.4 = (bf16[128,256]{1,0:T(8,128)(2,1)}, bf16[128,256]{1,0:T(8,128)(2,1)S(1)}, u32[]{:S(2)}, u32[]{:S(2)}) collective-permute-start(bf16[128,256]{1,0:T(8,128)(2,1)} %get-tuple-element.43), channel_id=1, source_target_pairs={{0,12},{2,14},{4,8},{6,10},{8,4},{10,6},{12,0},{14,2},{1,13},{3,15... | collective-permute-start | bytes 196616 | tf_op jit(solution)/shard_map/ppermute | solution.py:241
  65.1 1.3 %collective-permute-start.17 = (f32[136,128]{1,0:T(8,128)S(1)}, f32[136,128]{1,0:T(8,128)S(1)}, u32[]{:S(2)}, u32[]{:S(2)}) collective-permute-start(f32[136,128]{1,0:T(8,128)S(1)} %get-tuple-element.66), channel_id=1, source_target_pairs={{0,1},{1,0},{2,3},{3,2},{4,5},{5,4},{6,7},{7,6},{8,9},{9,8},{10,11... | collective-permute-start | bytes 208904 | tf_op jit(solution)/shard_map/ppermute | solution.py:248
  66.5 4.4 %collective-permute-start.18 = (f32[136,128]{1,0:T(8,128)S(1)}, f32[136,128]{1,0:T(8,128)S(1)}, u32[]{:S(2)}, u32[]{:S(2)}) collective-permute-start(f32[136,128]{1,0:T(8,128)S(1)} %add.22), channel_id=1, source_target_pairs={{0,2},{2,0},{4,6},{6,4},{8,10},{10,8},{12,14},{14,12},{1,3},{3,1},... | collective-permute-start | bytes 208904 | tf_op jit(solution)/shard_map/ppermute | solution.py:251
  70.9 4.4 %collective-permute-start.19 = (f32[136,128]{1,0:T(8,128)S(1)}, f32[136,128]{1,0:T(8,128)S(1)}, u32[]{:S(2)}, u32[]{:S(2)}) collective-permute-start(f32[136,128]{1,0:T(8,128)S(1)} %add.23), channel_id=1, source_target_pairs={{0,4},{2,6},{4,0},{6,2},{8,12},{10,14},{12,8},{14,10},{1,5},{3,7},... | collective-permute-start | bytes 208904 | tf_op jit(solution)/shard_map/ppermute | solution.py:251
  75.3 5.5 %collective-permute-start.20 = (f32[136,128]{1,0:T(8,128)S(1)}, f32[136,128]{1,0:T(8,128)S(1)}, u32[]{:S(2)}, u32[]{:S(2)}) collective-permute-start(f32[136,128]{1,0:T(8,128)S(1)} %add.24), channel_id=1, source_target_pairs={{0,8},{2,10},{4,12},{6,14},{8,0},{10,2},{12,4},{14,6},{1,9},{3,11}... | collective-permute-start | bytes 208904 | tf_op jit(solution)/shard_map/ppermute | solution.py:251
  80.7 1.3 %collective-permute-start.21 = (f32[136,128]{1,0:T(8,128)S(1)}, f32[136,128]{1,0:T(8,128)S(1)}, u32[]{:S(2)}, u32[]{:S(2)}) collective-permute-start(f32[136,128]{1,0:T(8,128)S(1)} %add.25.mine_ref), channel_id=1, source_target_pairs={{0,1},{1,0},{2,3},{3,2},{4,5},{5,4},{6,7},{7,6},{8,9},{9,8},{10,11... | collective-permute-start | bytes 208904 | tf_op jit(solution)/shard_map/ppermute | solution.py:253

commit v3 on v2

--- a/solution.py
+++ b/solution.py
@@ -7,50 +7,160 @@
 from jax.experimental.pallas import tpu as pltpu
 from jax.sharding import PartitionSpec as P
 
-CHUNKS = 4
+SHARES = (1, 1, 1)
+PIECES = 8
 PANEL = 16
 F32 = jnp.float32
 BF16 = jnp.bfloat16
 MIB = 1 << 20
+VMEM = pl.BlockSpec(memory_space=pltpu.VMEM)
+SMEM = pl.BlockSpec(memory_space=pltpu.SMEM)
+HBM = pl.BlockSpec(memory_space=pltpu.HBM)
 
 
 def params(mib=32):
     return pltpu.CompilerParams(vmem_limit_bytes=mib * MIB)
 
 
-def image_kernel(idx_ref, spectra_ref, loadings_ref, *out_refs):
-    rows = out_refs[0].shape[1]
-    for c, out in enumerate(out_refs):
-        out[0] = jnp.dot(
-            spectra_ref[0, 0, c * rows:(c + 1) * rows, :], loadings_ref[...], preferred_element_type=F32
-        ).astype(out.dtype)
-
-
-def image_half(idx, spectra, loadings, own, dtype):
-    outer, _, rows, bins = spectra.shape
-    cols = loadings.shape[1]
-    piece = rows // CHUNKS
-    side = (lambda i, idx: (i, idx[0], 0, 0)) if own else (lambda i, idx: (i, 1 - idx[0], 0, 0))
-    return pl.pallas_call(
-        image_kernel,
-        grid_spec=pltpu.PrefetchScalarGridSpec(
-            num_scalar_prefetch=1,
-            grid=(outer,),
-            in_specs=[
-                pl.BlockSpec((1, 1, rows, bins), side),
-                pl.BlockSpec((bins, cols), lambda i, idx: (0, 0)),
-            ],
-            out_specs=[pl.BlockSpec((1, piece, cols), lambda i, idx: (i, 0, 0))] * CHUNKS,
-        ),
-        out_shape=[jax.ShapeDtypeStruct((outer, piece, cols), dtype)] * CHUNKS,
+def loadings_kernel(spectra_hbm, probes_hbm, terms_ref, spectra_ref, probes_ref, sems):
+    rows = spectra_ref.shape[0] // PIECES
+
+    def copies(i):
+        part = pl.ds(i * rows, rows)
+        return (
+            pltpu.make_async_copy(probes_hbm.at[part], probes_ref.at[part], sems.at[0, i]),
+            pltpu.make_async_copy(spectra_hbm.at[part], spectra_ref.at[part], sems.at[1, i]),
+        )
+
+    for i in range(PIECES):
+        for copy in copies(i):
+            copy.start()
+    for i in range(PIECES):
+        for copy in copies(i):
+            copy.wait()
+        part = pl.ds(i * rows, rows)
+        term = lax.dot_general(
+            probes_ref[part], spectra_ref[part], (((0,), (0,)), ((), ())), preferred_element_type=F32
+        )
+        if i == 0:
+            terms_ref[...] = term
+        else:
+            terms_ref[...] += term
+
+
+def loadings_terms(spectra, probes):
+    rows, bins = spectra.shape
+    cols = probes.shape[1]
+    return pl.pallas_call(
+        loadings_kernel,
+        in_specs=[HBM, HBM],
+        out_specs=VMEM,
+        out_shape=jax.ShapeDtypeStruct((cols, bins), F32),
+        scratch_shapes=[
+            pltpu.VMEM((rows, bins), BF16),
+            pltpu.VMEM((rows, cols), BF16),
+            pltpu.SemaphoreType.DMA((2, PIECES)),
+        ],
+        compiler_params=params(51),
+        cost_estimate=pl.CostEstimate(
+            flops=2 * rows * bins * cols, bytes_accessed=rows * (bins + cols) * 2, transcendentals=0
+        ),
+    )(spectra, probes)
+
+
+def block_copies(spectra_hbm, blocks_ref, sems, side):
+    outer, rows, _ = blocks_ref.shape
+    starts = [pl.multiple_of((i * 2 + side) * rows, 16) for i in range(outer)]
+    return [
+        pltpu.make_async_copy(spectra_hbm.at[pl.ds(start, rows)], blocks_ref.at[i], sems.at[i])
+        for i, start in enumerate(starts)
+    ]
+
+
+def fetch_kernel(idx_ref, spectra_hbm, after_ref, blocks_ref, sems):
+    copies = block_copies(spectra_hbm, blocks_ref, sems, 1 - idx_ref[0])
+    for copy in copies:
+        copy.start()
+    for copy in copies:
+        copy.wait()
+
+
+def fetch_blocks(idx, spectra, rows, after):
+    outer, bins = spectra.shape[0] // (2 * rows), spectra.shape[1]
+    return pl.pallas_call(
+        fetch_kernel,
+        in_specs=[SMEM, HBM, pl.BlockSpec(memory_space=pl.ANY)],
+        out_specs=VMEM,
+        out_shape=jax.ShapeDtypeStruct((outer, rows, bins), BF16),
+        scratch_shapes=[pltpu.SemaphoreType.DMA((outer,))],
+        compiler_params=params(48),
+        cost_estimate=pl.CostEstimate(flops=0, bytes_accessed=outer * rows * bins * 4, transcendentals=0),
+    )(idx, spectra, after)
+
+
+def away_kernel(blocks_ref, mine_ref, got_ref, loadings_ref, *out_refs):
+    loadings_ref[...] = (mine_ref[...] + got_ref[...]).T.astype(BF16)
+    first = 0
+    for out_ref in out_refs:
+        size = out_ref.shape[1]
+        for i in range(out_ref.shape[0]):
+            out_ref[i] = jnp.dot(
+                blocks_ref[i, first:first + size], loadings_ref[...], preferred_element_type=F32
+            ).astype(out_ref.dtype)
+        first += size
+
+
+def image_away(blocks, mine, got, sizes):
+    outer, rows, bins = blocks.shape
+    cols = mine.shape[0]
+    shapes = [jax.ShapeDtypeStruct((bins, cols), BF16)]
+    shapes += [jax.ShapeDtypeStruct((outer, size, cols), BF16) for size in sizes]
+    return pl.pallas_call(
+        away_kernel,
+        in_specs=[VMEM] * 3,
+        out_specs=[VMEM] * len(shapes),
+        out_shape=shapes,
         compiler_params=params(),
         cost_estimate=pl.CostEstimate(
+            flops=2 * outer * rows * bins * cols, bytes_accessed=outer * rows * cols * 4, transcendentals=0
+        ),
+    )(blocks, mine, got)
+
+
+def kept_kernel(idx_ref, spectra_hbm, loadings_ref, *refs):
+    *out_refs, blocks_ref, sems = refs
+    copies = block_copies(spectra_hbm, blocks_ref, sems, idx_ref[0])
+    for copy in copies:
+        copy.start()
+    for i, copy in enumerate(copies):
+        copy.wait()
+        first = 0
+        for out_ref in out_refs:
+            size = out_ref.shape[1]
+            out_ref[i] = jnp.dot(
+                blocks_ref[i, first:first + size], loadings_ref[...], preferred_element_type=F32
+            )
+            first += size
+
+
+def image_kept(idx, spectra, loadings, sizes):
+    rows = sum(sizes)
+    outer, (bins, cols) = spectra.shape[0] // (2 * rows), loadings.shape
+    return pl.pallas_call(
+        kept_kernel,
+        in_specs=[SMEM, HBM, VMEM],
+        out_specs=[VMEM] * len(sizes),
+        out_shape=[jax.ShapeDtypeStruct((outer, size, cols), F32) for size in sizes],
+        scratch_shapes=[pltpu.VMEM((outer, rows, bins), BF16), pltpu.SemaphoreType.DMA((outer,))],
+        compiler_params=params(48),
+        cost_estimate=pl.CostEstimate(
             flops=2 * outer * rows * bins * cols, bytes_accessed=outer * rows * (bins * 2 + cols * 4), transcendentals=0
         ),
     )(idx, spectra, loadings)
 
 
-def add_kernel(idx_ref, got_ref, kept_ref, own_ref, *send_refs):
+def add_kernel(n_after, idx_ref, got_ref, kept_ref, *refs):
+    own_ref, *send_refs = refs[n_after:]
     me = idx_ref[1]
     own_ref[...] = got_ref[me].astype(F32) + kept_ref[me]
     for d, send in enumerate(send_refs):
@@ -58,20 +168,19 @@
         send[...] = (got_ref[other].astype(F32) + kept_ref[other]).astype(send.dtype)
 
 
-def add_chunk(idx, got, kept):
+def add_chunk(idx, got, kept, after):
     outer, piece, cols = got.shape
-    vmem = pl.BlockSpec(memory_space=pltpu.VMEM)
-    return pl.pallas_call(
-        add_kernel,
-        in_specs=[pl.BlockSpec(memory_space=pltpu.SMEM), vmem, vmem],
-        out_specs=[vmem] * outer,
+    return pl.pallas_call(
+        functools.partial(add_kernel, len(after)),
+        in_specs=[SMEM, VMEM, VMEM] + [pl.BlockSpec(memory_space=pl.ANY)] * len(after),
+        out_specs=[VMEM] * outer,
         out_shape=[jax.ShapeDtypeStruct((piece, cols), F32)]
         + [jax.ShapeDtypeStruct((piece, cols), BF16)] * (outer - 1),
         compiler_params=params(),
         cost_estimate=pl.CostEstimate(
             flops=outer * piece * cols, bytes_accessed=outer * piece * cols * 8, transcendentals=0
         ),
-    )(idx, got, kept)
+    )(idx, got, kept, *after)
 
 
 def gram_kernel(n, last, *refs):
@@ -107,13 +216,12 @@
     piece, cols = own.shape
     n = 1 + len(got)
     half = cols // 2
-    vmem = pl.BlockSpec(memory_space=pltpu.VMEM)
     last = pix is not None
     shapes = [(half + 8, half)] * 2 if last else [(cols, cols)]
     return pl.pallas_call(
         functools.partial(gram_kernel, n, last),
-        in_specs=[pl.BlockSpec(memory_space=pltpu.SMEM)] * last + [vmem] * (n + 1),
-        out_specs=[vmem] * (1 + len(shapes)),
+        in_specs=[SMEM] * last + [VMEM] * (n + 1),
+        out_specs=[VMEM] * (1 + len(shapes)),
         out_shape=[jax.ShapeDtypeStruct(s, F32) for s in [(piece, cols)] + shapes],
         compiler_params=params(),
         cost_estimate=pl.CostEstimate(
@@ -203,17 +311,21 @@
 def basis_of(pix, mine, other, image, pixels):
     cols = image[0].shape[1]
     rows = sum(x.shape[0] for x in image)
-    vmem = pl.BlockSpec(memory_space=pltpu.VMEM)
     return pl.pallas_call(
         functools.partial(basis_kernel, pixels),
-        in_specs=[pl.BlockSpec(memory_space=pltpu.SMEM)] + [vmem] * (2 + len(image)),
-        out_specs=vmem,
+        in_specs=[SMEM] + [VMEM] * (2 + len(image)),
+        out_specs=VMEM,
         out_shape=jax.ShapeDtypeStruct((rows, cols), F32),
         scratch_shapes=[pltpu.VMEM((cols, cols), F32)] * 2,
         compiler_params=params(),
     )(pix, mine, other, *image)
 
 
+def split(rows):
+    ends = [-(-rows // 16 * sum(SHARES[:k]) // sum(SHARES)) * 16 for k in range(len(SHARES) + 1)]
+    return [last - first for first, last in zip(ends, ends[1:]) if last > first]
+
+
 def xor_pairs(n, d):
     return [(i, i ^ d) for i in range(n)]
 
@@ -221,25 +333,24 @@
 def on_device(n_bins, spectra, probes):
     rows_dev, bins = spectra.shape
     cols = probes.shape[1]
-    outer = n_bins // 2
     rows = rows_dev // n_bins
     me = lax.axis_index("bins")
     pix = lax.axis_index("pix").astype(jnp.int32).reshape(1)
     idx = jnp.stack([me % 2, me // 2]).astype(jnp.int32)
 
-    terms = lax.dot_general(spectra, probes, (((0,), (0,)), ((), ())), preferred_element_type=F32)
-    loadings = (terms + lax.ppermute(terms, "pix", xor_pairs(2, 1))).astype(BF16)
-
-    blocks = spectra.reshape(outer, 2, rows, bins)
-    away = image_half(idx, blocks, loadings, False, BF16)
-    kept = image_half(idx, blocks, loadings, True, F32)
+    sizes = split(rows)
+    terms = loadings_terms(spectra, probes)
+    got = lax.ppermute(terms, "pix", xor_pairs(2, 1))
+    blocks = fetch_blocks(idx, spectra, rows, terms)
+    loadings, *away = image_away(blocks, terms, got, sizes)
+    away = [lax.ppermute(out, "bins", xor_pairs(n_bins, 1)) for out in away]
+    kept = image_kept(idx, spectra, loadings, sizes)
     gram = jnp.zeros((cols, cols), F32)
     image = []
-    for c in range(CHUNKS):
-        got = lax.ppermute(away[c], "bins", xor_pairs(n_bins, 1))
-        own, *sends = add_chunk(idx, got, kept[c])
+    for c in range(len(sizes)):
+        own, *sends = add_chunk(idx, away[c], kept[c], image[c - 2:c - 1] if c > 1 else [])
         arrived = [lax.ppermute(s, "bins", xor_pairs(n_bins, 2 * (d + 1))) for d, s in enumerate(sends)]
-        if c < CHUNKS - 1:
+        if c < len(sizes) - 1:
             x, gram = gram_chunk(own, arrived, gram)
         else:
             x, mine, other = gram_chunk(own, arrived, gram, pix)

time: 95 us -> 77.8 us (0.82)
  starting transfers between devices: 33.7 us -> 26.4 us
  Pallas kernels: 22.3 us -> 28.5 us
  matrix products: 5.73 us -> 0 us
  local copies, waits for them, and re-layouts: 4.99 us -> 0.02 us
  waiting for transfers between devices: 26.4 us -> 22.5 us
  other arithmetic: 1.44 us -> 0.11 us
    ppermute x12 -> x9, starting transfers between devices: 24.6 us -> 15.2 us  [on_device(): lax.ppermute(s, 'bins', xor_pairs(n_bins, 2 * (d + 1)))]
    pallas_call x11, Pallas kernels: 22.3 us -> 28.5 us  [the longest x1 12.7 us: basis_of(): pl.pallas_call(functools.partial(basis_kernel, pixels), in_specs=[SMEM] +...]
    dot_general x1 -> x0, matrix products: 5.73 us -> none  [on_device(): lax.dot_general(spectra, probes, (((0,), (0,)), ((), ())), preferred_elem...]
    unnamed x4 -> x0, local copies, waits for them, and re-layouts: 4.97 us -> none
    ppermute x5 -> x4, waiting for transfers between devices: 8.46 us -> 5.72 us  [the longest x3 5.72 us: on_device(): away = [lax.ppermute(out, 'bins', xor_pairs(n_bins, 1)) for out in away]]
    ppermute x3, waiting for transfers between devices: 10.8 us -> 8.11 us  [on_device(): mine = mine + lax.ppermute(mine, 'bins', xor_pairs(n_bins, d))]
    ppermute x3, starting transfers between devices: 3.42 us -> 5.92 us  [on_device(): mine = mine + lax.ppermute(mine, 'bins', xor_pairs(n_bins, d))]
    ppermute x12 -> x9, waiting for transfers between devices: 4.66 us -> 6.19 us  [on_device(): lax.ppermute(s, 'bins', xor_pairs(n_bins, 2 * (d + 1)))]
  transfers between devices with their start and end apart: 22 -> 18, of which waited for: 12 -> 9; matrix products, arithmetic and copies ran while one was open for 0% -> 0% of each run, Pallas kernels for 7% -> 12%
where the time goes in v3:
time: 77.8 us; the launch traced here: 77.7 us
  Pallas kernels  28.5 us (37%)
  starting transfers between devices  26.4 us (34%)
  waiting for transfers between devices  22.5 us (29%)
    ppermute x9, starting transfers between devices, on_device(): lax.ppermute(s, 'bins', xor_pairs(n_bins, 2 * (d + 1)))  15.2 us
    pallas_call x1, Pallas kernels, basis_of(): pl.pallas_call(functools.partial(basis_kernel, pixels), in_specs=[SMEM] +...  12.7 us
    ppermute x3, waiting for transfers between devices, on_device(): mine = mine + lax.ppermute(mine, 'bins', xor_pairs(n_bins, d))  8.11 us
    ppermute x9, waiting for transfers between devices, on_device(): lax.ppermute(s, 'bins', xor_pairs(n_bins, 2 * (d + 1)))  6.19 us
    ppermute x3, starting transfers between devices, on_device(): mine = mine + lax.ppermute(mine, 'bins', xor_pairs(n_bins, d))  5.92 us
    ppermute x3, waiting for transfers between devices, on_device(): away = [lax.ppermute(out, 'bins', xor_pairs(n_bins, 1)) for out in away]  5.72 us
    ppermute x3, starting transfers between devices, on_device(): away = [lax.ppermute(out, 'bins', xor_pairs(n_bins, 1)) for out in away]  4.64 us
    pallas_call x1, Pallas kernels, loadings_terms(): pl.pallas_call(loadings_kernel, in_specs=[HBM, HBM], out_specs=VMEM, out_...  4.61 us
  transfers between devices with their start and end apart: 18, of which 9 were waited for; matrix products, arithmetic and copies ran while one was open for 0% of the time, Pallas kernels for 12%

profile of v3, /device:TPU:0, one launch (start us, length us, event | category | flops | bytes accessed | tf_op | source)
XLA Modules:
  0.0 77.7 jit_solution(16977604145860478570)
XLA Ops:
  0.0 4.6 %shard_map.28.after_ref.mine_ref = f32[256,1024]{1,0:T(8,128)S(1)} custom-call(bf16[4096,1024]{1,0:T(8,128)(2,1)} %spectra_hbm.5, bf16[4096,256]{1,0:T(8,128)(2,1)} %probes_hbm.1), custom_call_target="tpu_custom_call" | custom-call | flops 2147483648 | bytes 10485760 | tf_op jit(solution)/shard_map/pallas_call | solution.py:54
  4.6 0.5 collective-permute-start
  5.2 2.8 %shard_map.29.blocks_ref = bf16[4,512,1024]{2,1,0:T(8,128)(2,1)S(1)} custom-call(s32[2]{0:T(128)S(1)} %pad_add_fusion.idx_ref, bf16[4096,1024]{1,0:T(8,128)(2,1)} %spectra_hbm.5, f32[256,1024]{1,0:T(8,128)S(1)} %shard_map.28.after_ref.mine_ref), custom_call_target="tpu_custom_call" | custom-call | bytes 8388608 | tf_op jit(solution)/shard_map/pallas_call | solution.py:90
  8.0 1.4 %shard_map.30 = (bf16[1024,256]{1,0:T(8,128)(2,1)S(1)}, bf16[4,176,256]{2,1,0:T(8,128)(2,1)S(1)}, bf16[4,176,256]{2,1,0:T(8,128)(2,1)S(1)}, bf16[4,160,256]{2,1,0:T(8,128)(2,1)S(1)}) custom-call(bf16[4,512,1024]{2,1,0:T(8,128)(2,1)S(1)} %shard_map.29.blocks_ref, f32[256,1024]{1,0:T(8,128)S(1)} %shard_map.28.after_ref.mine_ref, ...), custom_call_target="tpu_custom_call" | custom-call | flops 1073741824 | bytes 2097152 | tf_op jit(solution)/shard_map/pallas_call | solution.py:118
  9.4 2.6 %collective-permute-start.2 = (bf16[4,176,256]{2,1,0:T(8,128)(2,1)S(1)}, bf16[4,176,256]{2,1,0:T(8,128)(2,1)S(1)}, u32[]{:S(2)}, u32[]{:S(2)}) collective-permute-start(bf16[4,176,256]{2,1,0:T(8,128)(2,1)S(1)} %get-tuple-element.34), channel_id=1, source_target_pairs={{0,2},{2,0},{4,6},{6,4},{8,10},{10,8},{12,14},{14,12},{1,3},{3,1},... | collective-permute-start | bytes 1081352 | tf_op jit(solution)/shard_map/ppermute | solution.py:346
  12.1 1.9 %collective-permute-start.1 = (bf16[4,160,256]{2,1,0:T(8,128)(2,1)S(1)}, bf16[4,160,256]{2,1,0:T(8,128)(2,1)S(1)}, u32[]{:S(2)}, u32[]{:S(2)}) collective-permute-start(bf16[4,160,256]{2,1,0:T(8,128)(2,1)S(1)} %get-tuple-element.31), channel_id=1, source_target_pairs={{0,2},{2,0},{4,6},{6,4},{8,10},{10,8},{12,14},{14,12},{1,3},{3,1},... | collective-permute-start | bytes 983048 | tf_op jit(solution)/shard_map/ppermute | solution.py:346
  14.0 4.0 %shard_map.31 = (f32[4,176,256]{2,1,0:T(8,128)S(1)}, f32[4,176,256]{2,1,0:T(8,128)S(1)}, f32[4,160,256]{2,1,0:T(8,128)S(1)}) custom-call(s32[2]{0:T(128)S(1)} %pad_add_fusion.idx_ref, bf16[4096,1024]{1,0:T(8,128)(2,1)} %spectra_hbm.5, bf16[1024,256]{1,0:T(8,128)(2,1)S(1)} %get-tuple-element.32.loadings_ref), custom_call_target="tpu_custom_call" | custom-call | flops 1073741824 | bytes 6291456 | tf_op jit(solution)/shard_map/pallas_call | solution.py:149
  18.0 3.3 %collective-permute-done.2.got_ref = bf16[4,176,256]{2,1,0:T(8,128)(2,1)S(1)} collective-permute-done((bf16[4,176,256]{2,1,0:T(8,128)(2,1)S(1)}, bf16[4,176,256]{2,1,0:T(8,128)(2,1)S(1)}, u32[]{:S(2)}, u32[]{:S(2)}) %collective-permute-start.2) | collective-permute-done | bytes 360480 | tf_op jit(solution)/shard_map/ppermute | solution.py:346
  21.2 0.6 shard_map.32
  21.9 2.1 %collective-permute-start.3 = (bf16[176,256]{1,0:T(8,128)(2,1)S(1)}, bf16[176,256]{1,0:T(8,128)(2,1)S(1)}, u32[]{:S(2)}, u32[]{:S(2)}) collective-permute-start(bf16[176,256]{1,0:T(8,128)(2,1)S(1)} %get-tuple-element.37), channel_id=1, source_target_pairs={{0,4},{2,6},{4,0},{6,2},{8,12},{10,14},{12,8},{14,10},{1,5},{3,7},... | collective-permute-start | bytes 270344 | tf_op jit(solution)/shard_map/ppermute | solution.py:352
  23.9 2.6 %collective-permute-start.4 = (bf16[176,256]{1,0:T(8,128)(2,1)S(1)}, bf16[176,256]{1,0:T(8,128)(2,1)S(1)}, u32[]{:S(2)}, u32[]{:S(2)}) collective-permute-start(bf16[176,256]{1,0:T(8,128)(2,1)S(1)} %get-tuple-element.38), channel_id=1, source_target_pairs={{0,8},{2,10},{4,12},{6,14},{8,0},{10,2},{12,4},{14,6},{1,9},{3,11}... | collective-permute-start | bytes 270344 | tf_op jit(solution)/shard_map/ppermute | solution.py:352
  26.5 2.5 %collective-permute-done.9.got_ref = bf16[4,176,256]{2,1,0:T(8,128)(2,1)S(1)} collective-permute-done((bf16[4,176,256]{2,1,0:T(8,128)(2,1)S(1)}, bf16[4,176,256]{2,1,0:T(8,128)(2,1)S(1)}, u32[]{:S(2)}, u32[]{:S(2)}) %collective-permute-start.9) | collective-permute-done | bytes 360480 | tf_op jit(solution)/shard_map/ppermute | solution.py:346
  29.0 0.6 shard_map.35
  29.6 2.1 %collective-permute-start.10 = (bf16[176,256]{1,0:T(8,128)(2,1)S(1)}, bf16[176,256]{1,0:T(8,128)(2,1)S(1)}, u32[]{:S(2)}, u32[]{:S(2)}) collective-permute-start(bf16[176,256]{1,0:T(8,128)(2,1)S(1)} %get-tuple-element.48), channel_id=1, source_target_pairs={{0,4},{2,6},{4,0},{6,2},{8,12},{10,14},{12,8},{14,10},{1,5},{3,7},... | collective-permute-start | bytes 270344 | tf_op jit(solution)/shard_map/ppermute | solution.py:352
  31.7 2.6 %collective-permute-start.11 = (bf16[176,256]{1,0:T(8,128)(2,1)S(1)}, bf16[176,256]{1,0:T(8,128)(2,1)S(1)}, u32[]{:S(2)}, u32[]{:S(2)}) collective-permute-start(bf16[176,256]{1,0:T(8,128)(2,1)S(1)} %get-tuple-element.49), channel_id=1, source_target_pairs={{0,8},{2,10},{4,12},{6,14},{8,0},{10,2},{12,4},{14,6},{1,9},{3,11}... | collective-permute-start | bytes 270344 | tf_op jit(solution)/shard_map/ppermute | solution.py:352
  34.2 1.4 %collective-permute-start.12 = (bf16[176,256]{1,0:T(8,128)(2,1)S(1)}, bf16[176,256]{1,0:T(8,128)(2,1)S(1)}, u32[]{:S(2)}, u32[]{:S(2)}) collective-permute-start(bf16[176,256]{1,0:T(8,128)(2,1)S(1)} %get-tuple-element.50), channel_id=1, source_target_pairs={{0,12},{2,14},{4,8},{6,10},{8,4},{10,6},{12,0},{14,2},{1,13},{3,15... | collective-permute-start | bytes 270344 | tf_op jit(solution)/shard_map/ppermute | solution.py:352
  35.7 0.4 shard_map.33
  36.1 0.6 shard_map.34
  36.8 1.5 %collective-permute-start.6 = (bf16[160,256]{1,0:T(8,128)(2,1)S(1)}, bf16[160,256]{1,0:T(8,128)(2,1)S(1)}, u32[]{:S(2)}, u32[]{:S(2)}) collective-permute-start(bf16[160,256]{1,0:T(8,128)(2,1)S(1)} %get-tuple-element.42), channel_id=1, source_target_pairs={{0,4},{2,6},{4,0},{6,2},{8,12},{10,14},{12,8},{14,10},{1,5},{3,7},... | collective-permute-start | bytes 245768 | tf_op jit(solution)/shard_map/ppermute | solution.py:352
  38.2 2.6 %collective-permute-start.7 = (bf16[160,256]{1,0:T(8,128)(2,1)S(1)}, bf16[160,256]{1,0:T(8,128)(2,1)S(1)}, u32[]{:S(2)}, u32[]{:S(2)}) collective-permute-start(bf16[160,256]{1,0:T(8,128)(2,1)S(1)} %get-tuple-element.43), channel_id=1, source_target_pairs={{0,8},{2,10},{4,12},{6,14},{8,0},{10,2},{12,4},{14,6},{1,9},{3,11}... | collective-permute-start | bytes 245768 | tf_op jit(solution)/shard_map/ppermute | solution.py:352
  41.7 1.0 %collective-permute-done.6.refs_2_ = bf16[160,256]{1,0:T(8,128)(2,1)S(1)} collective-permute-done((bf16[160,256]{1,0:T(8,128)(2,1)S(1)}, bf16[160,256]{1,0:T(8,128)(2,1)S(1)}, u32[]{:S(2)}, u32[]{:S(2)}) %collective-permute-start.6) | collective-permute-done | bytes 81952 | tf_op jit(solution)/shard_map/ppermute | solution.py:352
  42.6 5.2 %collective-permute-done.7.refs_3_ = bf16[160,256]{1,0:T(8,128)(2,1)S(1)} collective-permute-done((bf16[160,256]{1,0:T(8,128)(2,1)S(1)}, bf16[160,256]{1,0:T(8,128)(2,1)S(1)}, u32[]{:S(2)}, u32[]{:S(2)}) %collective-permute-start.7) | collective-permute-done | bytes 81952 | tf_op jit(solution)/shard_map/ppermute | solution.py:352
  47.8 0.4 shard_map.37
  48.4 1.2 %collective-permute-done.13 = f32[136,128]{1,0:T(8,128)S(1)} collective-permute-done((f32[136,128]{1,0:T(8,128)S(1)}, f32[136,128]{1,0:T(8,128)S(1)}, u32[]{:S(2)}, u32[]{:S(2)}) %collective-permute-start.13) | collective-permute-done | bytes 69664 | tf_op jit(solution)/shard_map/ppermute | solution.py:359
  49.6 1.5 %collective-permute-start.14 = (f32[136,128]{1,0:T(8,128)S(1)}, f32[136,128]{1,0:T(8,128)S(1)}, u32[]{:S(2)}, u32[]{:S(2)}) collective-permute-start(f32[136,128]{1,0:T(8,128)S(1)} %add.18), channel_id=1, source_target_pairs={{0,2},{2,0},{4,6},{6,4},{8,10},{10,8},{12,14},{14,12},{1,3},{3,1},... | collective-permute-start | bytes 208904 | tf_op jit(solution)/shard_map/ppermute | solution.py:362
  51.2 2.8 %collective-permute-done.14 = f32[136,128]{1,0:T(8,128)S(1)} collective-permute-done((f32[136,128]{1,0:T(8,128)S(1)}, f32[136,128]{1,0:T(8,128)S(1)}, u32[]{:S(2)}, u32[]{:S(2)}) %collective-permute-start.14) | collective-permute-done | bytes 69664 | tf_op jit(solution)/shard_map/ppermute | solution.py:362
  54.0 1.7 %collective-permute-start.15 = (f32[136,128]{1,0:T(8,128)S(1)}, f32[136,128]{1,0:T(8,128)S(1)}, u32[]{:S(2)}, u32[]{:S(2)}) collective-permute-start(f32[136,128]{1,0:T(8,128)S(1)} %add.19), channel_id=1, source_target_pairs={{0,4},{2,6},{4,0},{6,2},{8,12},{10,14},{12,8},{14,10},{1,5},{3,7},... | collective-permute-start | bytes 208904 | tf_op jit(solution)/shard_map/ppermute | solution.py:362
  55.7 2.7 %collective-permute-done.15 = f32[136,128]{1,0:T(8,128)S(1)} collective-permute-done((f32[136,128]{1,0:T(8,128)S(1)}, f32[136,128]{1,0:T(8,128)S(1)}, u32[]{:S(2)}, u32[]{:S(2)}) %collective-permute-start.15) | collective-permute-done | bytes 69664 | tf_op jit(solution)/shard_map/ppermute | solution.py:362
  58.4 2.7 %collective-permute-start.16 = (f32[136,128]{1,0:T(8,128)S(1)}, f32[136,128]{1,0:T(8,128)S(1)}, u32[]{:S(2)}, u32[]{:S(2)}) collective-permute-start(f32[136,128]{1,0:T(8,128)S(1)} %add.20), channel_id=1, source_target_pairs={{0,8},{2,10},{4,12},{6,14},{8,0},{10,2},{12,4},{14,6},{1,9},{3,11}... | collective-permute-start | bytes 208904 | tf_op jit(solution)/shard_map/ppermute | solution.py:362
  61.1 2.6 %collective-permute-done.16 = f32[136,128]{1,0:T(8,128)S(1)} collective-permute-done((f32[136,128]{1,0:T(8,128)S(1)}, f32[136,128]{1,0:T(8,128)S(1)}, u32[]{:S(2)}, u32[]{:S(2)}) %collective-permute-start.16) | collective-permute-done | bytes 69664 | tf_op jit(solution)/shard_map/ppermute | solution.py:362
  63.8 1.2 %collective-permute-done.17.other_ref = f32[136,128]{1,0:T(8,128)S(1)} collective-permute-done((f32[136,128]{1,0:T(8,128)S(1)}, f32[136,128]{1,0:T(8,128)S(1)}, u32[]{:S(2)}, u32[]{:S(2)}) %collective-permute-start.17) | collective-permute-done | bytes 69664 | tf_op jit(solution)/shard_map/ppermute | solution.py:364
  65.0 12.7 %shard_map.38 = f32[512,256]{1,0:T(8,128)} custom-call(s32[1]{0:T(128)} %bitcast.refs_0_.pix_ref, f32[136,128]{1,0:T(8,128)S(1)} %add.21.mine_ref, f32[136,128]{1,0:T(8,128)S(1)} %collective-permute-done.17.other_ref, f32[176,256]{1,0:T(8,128)S(1)} %get-tuple-element.40.refs_0_, f32[176,256]{1,0:T(8,128)S(1)} %get-tuple-element.55.refs_1_, ...), custom_call_target="tpu_custom_call" | custom-call | tf_op jit(solution)/shard_map/pallas_call | solution.py:314
  (21 shorter events, 1.2 us)
Async XLA Ops:
  4.6 3.4 %collective-permute-start = (f32[256,1024]{1,0:T(8,128)S(1)}, f32[256,1024]{1,0:T(8,128)S(1)}, u32[]{:S(2)}, u32[]{:S(2)}) collective-permute-start(f32[256,1024]{1,0:T(8,128)S(1)} %shard_map.28.after_ref.mine_ref), channel_id=1, source_target_pairs={{0,1},{1,0},{2,3},{3,2},{4,5},{5,4},{6,7},{7,6},{8,9},{9,8},{10,11... | collective-permute-start | bytes 3145736 | tf_op jit(solution)/shard_map/ppermute | solution.py:343
  9.4 11.9 %collective-permute-start.2 = (bf16[4,176,256]{2,1,0:T(8,128)(2,1)S(1)}, bf16[4,176,256]{2,1,0:T(8,128)(2,1)S(1)}, u32[]{:S(2)}, u32[]{:S(2)}) collective-permute-start(bf16[4,176,256]{2,1,0:T(8,128)(2,1)S(1)} %get-tuple-element.34), channel_id=1, source_target_pairs={{0,2},{2,0},{4,6},{6,4},{8,10},{10,8},{12,14},{14,12},{1,3},{3,1},... | collective-permute-start | bytes 1081352 | tf_op jit(solution)/shard_map/ppermute | solution.py:346
  12.0 17.0 %collective-permute-start.9 = (bf16[4,176,256]{2,1,0:T(8,128)(2,1)S(1)}, bf16[4,176,256]{2,1,0:T(8,128)(2,1)S(1)}, u32[]{:S(2)}, u32[]{:S(2)}) collective-permute-start(bf16[4,176,256]{2,1,0:T(8,128)(2,1)S(1)} %get-tuple-element.45), channel_id=1, source_target_pairs={{0,2},{2,0},{4,6},{6,4},{8,10},{10,8},{12,14},{14,12},{1,3},{3,1},... | collective-permute-start | bytes 1081352 | tf_op jit(solution)/shard_map/ppermute | solution.py:346
  12.1 24.1 %collective-permute-start.1 = (bf16[4,160,256]{2,1,0:T(8,128)(2,1)S(1)}, bf16[4,160,256]{2,1,0:T(8,128)(2,1)S(1)}, u32[]{:S(2)}, u32[]{:S(2)}) collective-permute-start(bf16[4,160,256]{2,1,0:T(8,128)(2,1)S(1)} %get-tuple-element.31), channel_id=1, source_target_pairs={{0,2},{2,0},{4,6},{6,4},{8,10},{10,8},{12,14},{14,12},{1,3},{3,1},... | collective-permute-start | bytes 983048 | tf_op jit(solution)/shard_map/ppermute | solution.py:346
  21.9 9.8 %collective-permute-start.3 = (bf16[176,256]{1,0:T(8,128)(2,1)S(1)}, bf16[176,256]{1,0:T(8,128)(2,1)S(1)}, u32[]{:S(2)}, u32[]{:S(2)}) collective-permute-start(bf16[176,256]{1,0:T(8,128)(2,1)S(1)} %get-tuple-element.37), channel_id=1, source_target_pairs={{0,4},{2,6},{4,0},{6,2},{8,12},{10,14},{12,8},{14,10},{1,5},{3,7},... | collective-permute-start | bytes 270344 | tf_op jit(solution)/shard_map/ppermute | solution.py:352
  23.9 10.3 %collective-permute-start.4 = (bf16[176,256]{1,0:T(8,128)(2,1)S(1)}, bf16[176,256]{1,0:T(8,128)(2,1)S(1)}, u32[]{:S(2)}, u32[]{:S(2)}) collective-permute-start(bf16[176,256]{1,0:T(8,128)(2,1)S(1)} %get-tuple-element.38), channel_id=1, source_target_pairs={{0,8},{2,10},{4,12},{6,14},{8,0},{10,2},{12,4},{14,6},{1,9},{3,11}... | collective-permute-start | bytes 270344 | tf_op jit(solution)/shard_map/ppermute | solution.py:352
  26.5 9.2 %collective-permute-start.5 = (bf16[176,256]{1,0:T(8,128)(2,1)S(1)}, bf16[176,256]{1,0:T(8,128)(2,1)S(1)}, u32[]{:S(2)}, u32[]{:S(2)}) collective-permute-start(bf16[176,256]{1,0:T(8,128)(2,1)S(1)} %get-tuple-element.39), channel_id=1, source_target_pairs={{0,12},{2,14},{4,8},{6,10},{8,4},{10,6},{12,0},{14,2},{1,13},{3,15... | collective-permute-start | bytes 270344 | tf_op jit(solution)/shard_map/ppermute | solution.py:352
  29.6 11.2 %collective-permute-start.10 = (bf16[176,256]{1,0:T(8,128)(2,1)S(1)}, bf16[176,256]{1,0:T(8,128)(2,1)S(1)}, u32[]{:S(2)}, u32[]{:S(2)}) collective-permute-start(bf16[176,256]{1,0:T(8,128)(2,1)S(1)} %get-tuple-element.48), channel_id=1, source_target_pairs={{0,4},{2,6},{4,0},{6,2},{8,12},{10,14},{12,8},{14,10},{1,5},{3,7},... | collective-permute-start | bytes 270344 | tf_op jit(solution)/shard_map/ppermute | solution.py:352
  31.7 9.6 %collective-permute-start.11 = (bf16[176,256]{1,0:T(8,128)(2,1)S(1)}, bf16[176,256]{1,0:T(8,128)(2,1)S(1)}, u32[]{:S(2)}, u32[]{:S(2)}) collective-permute-start(bf16[176,256]{1,0:T(8,128)(2,1)S(1)} %get-tuple-element.49), channel_id=1, source_target_pairs={{0,8},{2,10},{4,12},{6,14},{8,0},{10,2},{12,4},{14,6},{1,9},{3,11}... | collective-permute-start | bytes 270344 | tf_op jit(solution)/shard_map/ppermute | solution.py:352
  34.2 7.0 %collective-permute-start.12 = (bf16[176,256]{1,0:T(8,128)(2,1)S(1)}, bf16[176,256]{1,0:T(8,128)(2,1)S(1)}, u32[]{:S(2)}, u32[]{:S(2)}) collective-permute-start(bf16[176,256]{1,0:T(8,128)(2,1)S(1)} %get-tuple-element.50), channel_id=1, source_target_pairs={{0,12},{2,14},{4,8},{6,10},{8,4},{10,6},{12,0},{14,2},{1,13},{3,15... | collective-permute-start | bytes 270344 | tf_op jit(solution)/shard_map/ppermute | solution.py:352
  36.8 5.9 %collective-permute-start.6 = (bf16[160,256]{1,0:T(8,128)(2,1)S(1)}, bf16[160,256]{1,0:T(8,128)(2,1)S(1)}, u32[]{:S(2)}, u32[]{:S(2)}) collective-permute-start(bf16[160,256]{1,0:T(8,128)(2,1)S(1)} %get-tuple-element.42), channel_id=1, source_target_pairs={{0,4},{2,6},{4,0},{6,2},{8,12},{10,14},{12,8},{14,10},{1,5},{3,7},... | collective-permute-start | bytes 245768 | tf_op jit(solution)/shard_map/ppermute | solution.py:352
  38.2 9.6 %collective-permute-start.7 = (bf16[160,256]{1,0:T(8,128)(2,1)S(1)}, bf16[160,256]{1,0:T(8,128)(2,1)S(1)}, u32[]{:S(2)}, u32[]{:S(2)}) collective-permute-start(bf16[160,256]{1,0:T(8,128)(2,1)S(1)} %get-tuple-element.43), channel_id=1, source_target_pairs={{0,8},{2,10},{4,12},{6,14},{8,0},{10,2},{12,4},{14,6},{1,9},{3,11}... | collective-permute-start | bytes 245768 | tf_op jit(solution)/shard_map/ppermute | solution.py:352
  40.8 7.0 %collective-permute-start.8 = (bf16[160,256]{1,0:T(8,128)(2,1)S(1)}, bf16[160,256]{1,0:T(8,128)(2,1)S(1)}, u32[]{:S(2)}, u32[]{:S(2)}) collective-permute-start(bf16[160,256]{1,0:T(8,128)(2,1)S(1)} %get-tuple-element.44), channel_id=1, source_target_pairs={{0,12},{2,14},{4,8},{6,10},{8,4},{10,6},{12,0},{14,2},{1,13},{3,15... | collective-permute-start | bytes 245768 | tf_op jit(solution)/shard_map/ppermute | solution.py:352
  48.3 1.3 %collective-permute-start.13 = (f32[136,128]{1,0:T(8,128)S(1)}, f32[136,128]{1,0:T(8,128)S(1)}, u32[]{:S(2)}, u32[]{:S(2)}) collective-permute-start(f32[136,128]{1,0:T(8,128)S(1)} %get-tuple-element.54), channel_id=1, source_target_pairs={{0,1},{1,0},{2,3},{3,2},{4,5},{5,4},{6,7},{7,6},{8,9},{9,8},{10,11... | collective-permute-start | bytes 208904 | tf_op jit(solution)/shard_map/ppermute | solution.py:359
  49.6 4.4 %collective-permute-start.14 = (f32[136,128]{1,0:T(8,128)S(1)}, f32[136,128]{1,0:T(8,128)S(1)}, u32[]{:S(2)}, u32[]{:S(2)}) collective-permute-start(f32[136,128]{1,0:T(8,128)S(1)} %add.18), channel_id=1, source_target_pairs={{0,2},{2,0},{4,6},{6,4},{8,10},{10,8},{12,14},{14,12},{1,3},{3,1},... | collective-permute-start | bytes 208904 | tf_op jit(solution)/shard_map/ppermute | solution.py:362
  54.0 4.4 %collective-permute-start.15 = (f32[136,128]{1,0:T(8,128)S(1)}, f32[136,128]{1,0:T(8,128)S(1)}, u32[]{:S(2)}, u32[]{:S(2)}) collective-permute-start(f32[136,128]{1,0:T(8,128)S(1)} %add.19), channel_id=1, source_target_pairs={{0,4},{2,6},{4,0},{6,2},{8,12},{10,14},{12,8},{14,10},{1,5},{3,7},... | collective-permute-start | bytes 208904 | tf_op jit(solution)/shard_map/ppermute | solution.py:362
  58.4 5.3 %collective-permute-start.16 = (f32[136,128]{1,0:T(8,128)S(1)}, f32[136,128]{1,0:T(8,128)S(1)}, u32[]{:S(2)}, u32[]{:S(2)}) collective-permute-start(f32[136,128]{1,0:T(8,128)S(1)} %add.20), channel_id=1, source_target_pairs={{0,8},{2,10},{4,12},{6,14},{8,0},{10,2},{12,4},{14,6},{1,9},{3,11}... | collective-permute-start | bytes 208904 | tf_op jit(solution)/shard_map/ppermute | solution.py:362
  63.7 1.3 %collective-permute-start.17 = (f32[136,128]{1,0:T(8,128)S(1)}, f32[136,128]{1,0:T(8,128)S(1)}, u32[]{:S(2)}, u32[]{:S(2)}) collective-permute-start(f32[136,128]{1,0:T(8,128)S(1)} %add.21.mine_ref), channel_id=1, source_target_pairs={{0,1},{1,0},{2,3},{3,2},{4,5},{5,4},{6,7},{7,6},{8,9},{9,8},{10,11... | collective-permute-start | bytes 208904 | tf_op jit(solution)/shard_map/ppermute | solution.py:364

commit v4 on v3

--- a/solution.py
+++ b/solution.py
@@ -10,6 +10,7 @@
 SHARES = (1, 1, 1)
 PIECES = 8
 PANEL = 16
+WINDOW = 32
 F32 = jnp.float32
 BF16 = jnp.bfloat16
 MIB = 1 << 20
@@ -231,8 +232,16 @@
 
 
 def transposed_dot(a, b):
+    def terms(x):
+        high = x.astype(BF16)
+        rest = x - high.astype(F32)
+        middle = rest.astype(BF16)
+        return high, middle, (rest - middle.astype(F32)).astype(BF16)
+
+    (a0, a1, a2), (b0, b1, b2) = terms(a), terms(b)
     return lax.dot_general(
-        a, b, (((0,), (0,)), ((), ())), precision=lax.Precision.HIGHEST, preferred_element_type=F32
+        jnp.concatenate([a0, a0, a1, a1, a0, a2], 0), jnp.concatenate([b0, b1, b0, b1, b2, b0], 0),
+        (((0,), (0,)), ((), ())), preferred_element_type=F32,
     )
 
 
@@ -240,37 +249,49 @@
     return column if width == 128 else jnp.concatenate([column] * (width // 128), 1)
 
 
+def eliminate_panel(right, left, at):
+    rows, width = right.shape
+    reach = left.shape[1]
+    row = lax.broadcasted_iota(jnp.int32, (rows, 128), 0)
+    own = row[:PANEL]
+    columns = [jnp.broadcast_to(right[:, at + j:at + j + 1], (rows, 128)) for j in range(PANEL)]
+    pivots = jnp.ones((PANEL, 128), F32)
+    for j in range(0, PANEL, 2):
+        c0, c1 = columns[j], columns[j + 1]
+        a, b, c = c0[j:j + 1], c1[j:j + 1], c1[j + 1:j + 2]
+        det = a * c - b * b
+        inv_a, inv_det = 1.0 / a, 1.0 / det
+        pivots = jnp.where(own == j, a, jnp.where(own == j + 1, det * inv_a, pivots))
+        below = row > j + 1
+        g0 = jnp.where(below, (c0 * c - c1 * b) * inv_det, jnp.where(row == j + 1, b * inv_a, 0.0))
+        g1 = jnp.where(below, (c1 * a - c0 * b) * inv_det, 0.0)
+        for m in range(j + 2, PANEL):
+            columns[m] = columns[m] - g0 * columns[m][j:j + 1] - g1 * columns[m][j + 1:j + 2]
+        right = right - wide(g0, width) * right[j:j + 1] - wide(g1, width) * right[j + 1:j + 2]
+        left = left - wide(g0, reach) * left[j:j + 1] - wide(g1, reach) * left[j + 1:j + 2]
+    scale = lax.rsqrt(pivots)
+    done = right[:PANEL] * wide(scale, width), left[:PANEL] * wide(scale, reach)
+    return done, right[PANEL:], left[PANEL:]
+
+
 def invert_factor(gram, inverse):
     n = gram.shape[0]
-    row = lax.broadcasted_iota(jnp.int32, (PANEL, 128), 0)
-    for k in range(0, n, PANEL):
-        end = k + PANEL
+    for k in range(0, n, WINDOW):
+        end = k + WINDOW
         start, reach = k // 128 * 128, -(-end // 128) * 128
         right, left = gram[k:end, start:n], inverse[k:end, :reach]
-        width = n - start
-        columns = [jnp.broadcast_to(right[:, k - start + j:k - start + j + 1], (PANEL, 128)) for j in range(PANEL)]
-        pivots = jnp.ones((PANEL, 128), F32)
-        for j in range(0, PANEL, 2):
-            c0, c1 = columns[j], columns[j + 1]
-            a, b, c = c0[j:j + 1], c1[j:j + 1], c1[j + 1:j + 2]
-            det = a * c - b * b
-            inv_a, inv_det = 1.0 / a, 1.0 / det
-            pivots = jnp.where(row == j, a, jnp.where(row == j + 1, det * inv_a, pivots))
-            below = row > j + 1
-            g0 = jnp.where(below, (c0 * c - c1 * b) * inv_det, jnp.where(row == j + 1, b * inv_a, 0.0))
-            g1 = jnp.where(below, (c1 * a - c0 * b) * inv_det, 0.0)
-            for m in range(j + 2, PANEL):
-                columns[m] = columns[m] - g0 * columns[m][j:j + 1] - g1 * columns[m][j + 1:j + 2]
-            right = right - wide(g0, width) * right[j:j + 1] - wide(g1, width) * right[j + 1:j + 2]
-            left = left - wide(g0, reach) * left[j:j + 1] - wide(g1, reach) * left[j + 1:j + 2]
-        scale = lax.rsqrt(pivots)
-        right, left = right * wide(scale, width), left * wide(scale, reach)
+        done = []
+        for first in range(0, WINDOW, PANEL):
+            panel, right, left = eliminate_panel(right, left, k - start + first)
+            done.append(panel)
+        right, left = (jnp.concatenate(part, 0) for part in zip(*done, strict=True))
         inverse[k:end, :reach] = left
         if end < n:
             base = end // 128 * 128
             rest = right[:, base - start:]
-            gram[end:n, base:n] = gram[end:n, base:n] - transposed_dot(rest, rest)[end - base:]
-            inverse[end:n, :reach] = inverse[end:n, :reach] - transposed_dot(rest, left)[end - base:]
+            change = transposed_dot(rest, jnp.concatenate([rest, left], 1))[end - base:]
+            gram[end:n, base:n] -= change[:, :n - base]
+            inverse[end:n, :reach] -= change[:, n - base:]
 
 
 def basis_kernel(pixels, pix_ref, mine_ref, other_ref, *refs):

time: 77.8 us -> 73.4 us (0.943)
  Pallas kernels: 28.5 us -> 24.1 us
    pallas_call x1, Pallas kernels: 12.7 us -> 8.22 us  [basis_of(): pl.pallas_call(functools.partial(basis_kernel, pixels), in_specs=[SMEM] +...]
  transfers between devices with their start and end apart: 18 -> 18, of which waited for: 9 -> 9; matrix products, arithmetic and copies ran while one was open for 0% -> 0% of each run, Pallas kernels for 12% -> 13%
where the time goes in v4:
time: 73.4 us; the launch traced here: 73.2 us
  starting transfers between devices  26.4 us (36%)
  Pallas kernels  24.1 us (33%)
  waiting for transfers between devices  22.5 us (31%)
    ppermute x9, starting transfers between devices, on_device(): lax.ppermute(s, 'bins', xor_pairs(n_bins, 2 * (d + 1)))  15.2 us
    pallas_call x1, Pallas kernels, basis_of(): pl.pallas_call(functools.partial(basis_kernel, pixels), in_specs=[SMEM] +...  8.22 us
    ppermute x3, waiting for transfers between devices, on_device(): mine = mine + lax.ppermute(mine, 'bins', xor_pairs(n_bins, d))  8.09 us
    ppermute x9, waiting for transfers between devices, on_device(): lax.ppermute(s, 'bins', xor_pairs(n_bins, 2 * (d + 1)))  6.19 us
    ppermute x3, starting transfers between devices, on_device(): mine = mine + lax.ppermute(mine, 'bins', xor_pairs(n_bins, d))  5.93 us
    ppermute x3, waiting for transfers between devices, on_device(): away = [lax.ppermute(out, 'bins', xor_pairs(n_bins, 1)) for out in away]  5.71 us
    ppermute x3, starting transfers between devices, on_device(): away = [lax.ppermute(out, 'bins', xor_pairs(n_bins, 1)) for out in away]  4.65 us
    pallas_call x1, Pallas kernels, loadings_terms(): pl.pallas_call(loadings_kernel, in_specs=[HBM, HBM], out_specs=VMEM, out_...  4.61 us
  transfers between devices with their start and end apart: 18, of which 9 were waited for; matrix products, arithmetic and copies ran while one was open for 0% of the time, Pallas kernels for 13%

profile of v4, /device:TPU:0, one launch (start us, length us, event | category | flops | bytes accessed | tf_op | source)
XLA Modules:
  0.0 73.2 jit_solution(15703420085717359705)
XLA Ops:
  0.0 4.6 %shard_map.28.after_ref.mine_ref = f32[256,1024]{1,0:T(8,128)S(1)} custom-call(bf16[4096,1024]{1,0:T(8,128)(2,1)} %spectra_hbm.5, bf16[4096,256]{1,0:T(8,128)(2,1)} %probes_hbm.1), custom_call_target="tpu_custom_call" | custom-call | flops 2147483648 | bytes 10485760 | tf_op jit(solution)/shard_map/pallas_call | solution.py:55
  4.6 0.5 collective-permute-start
  5.2 2.8 %shard_map.29.blocks_ref = bf16[4,512,1024]{2,1,0:T(8,128)(2,1)S(1)} custom-call(s32[2]{0:T(128)S(1)} %pad_add_fusion.idx_ref, bf16[4096,1024]{1,0:T(8,128)(2,1)} %spectra_hbm.5, f32[256,1024]{1,0:T(8,128)S(1)} %shard_map.28.after_ref.mine_ref), custom_call_target="tpu_custom_call" | custom-call | bytes 8388608 | tf_op jit(solution)/shard_map/pallas_call | solution.py:91
  8.0 1.4 %shard_map.30 = (bf16[1024,256]{1,0:T(8,128)(2,1)S(1)}, bf16[4,176,256]{2,1,0:T(8,128)(2,1)S(1)}, bf16[4,176,256]{2,1,0:T(8,128)(2,1)S(1)}, bf16[4,160,256]{2,1,0:T(8,128)(2,1)S(1)}) custom-call(bf16[4,512,1024]{2,1,0:T(8,128)(2,1)S(1)} %shard_map.29.blocks_ref, f32[256,1024]{1,0:T(8,128)S(1)} %shard_map.28.after_ref.mine_ref, ...), custom_call_target="tpu_custom_call" | custom-call | flops 1073741824 | bytes 2097152 | tf_op jit(solution)/shard_map/pallas_call | solution.py:119
  9.4 2.6 %collective-permute-start.2 = (bf16[4,176,256]{2,1,0:T(8,128)(2,1)S(1)}, bf16[4,176,256]{2,1,0:T(8,128)(2,1)S(1)}, u32[]{:S(2)}, u32[]{:S(2)}) collective-permute-start(bf16[4,176,256]{2,1,0:T(8,128)(2,1)S(1)} %get-tuple-element.34), channel_id=1, source_target_pairs={{0,2},{2,0},{4,6},{6,4},{8,10},{10,8},{12,14},{14,12},{1,3},{3,1},... | collective-permute-start | bytes 1081352 | tf_op jit(solution)/shard_map/ppermute | solution.py:367
  12.1 1.9 %collective-permute-start.1 = (bf16[4,160,256]{2,1,0:T(8,128)(2,1)S(1)}, bf16[4,160,256]{2,1,0:T(8,128)(2,1)S(1)}, u32[]{:S(2)}, u32[]{:S(2)}) collective-permute-start(bf16[4,160,256]{2,1,0:T(8,128)(2,1)S(1)} %get-tuple-element.31), channel_id=1, source_target_pairs={{0,2},{2,0},{4,6},{6,4},{8,10},{10,8},{12,14},{14,12},{1,3},{3,1},... | collective-permute-start | bytes 983048 | tf_op jit(solution)/shard_map/ppermute | solution.py:367
  14.0 4.0 %shard_map.31 = (f32[4,176,256]{2,1,0:T(8,128)S(1)}, f32[4,176,256]{2,1,0:T(8,128)S(1)}, f32[4,160,256]{2,1,0:T(8,128)S(1)}) custom-call(s32[2]{0:T(128)S(1)} %pad_add_fusion.idx_ref, bf16[4096,1024]{1,0:T(8,128)(2,1)} %spectra_hbm.5, bf16[1024,256]{1,0:T(8,128)(2,1)S(1)} %get-tuple-element.32.loadings_ref), custom_call_target="tpu_custom_call" | custom-call | flops 1073741824 | bytes 6291456 | tf_op jit(solution)/shard_map/pallas_call | solution.py:150
  18.0 3.3 %collective-permute-done.2.got_ref = bf16[4,176,256]{2,1,0:T(8,128)(2,1)S(1)} collective-permute-done((bf16[4,176,256]{2,1,0:T(8,128)(2,1)S(1)}, bf16[4,176,256]{2,1,0:T(8,128)(2,1)S(1)}, u32[]{:S(2)}, u32[]{:S(2)}) %collective-permute-start.2) | collective-permute-done | bytes 360480 | tf_op jit(solution)/shard_map/ppermute | solution.py:367
  21.2 0.6 shard_map.32
  21.9 2.1 %collective-permute-start.3 = (bf16[176,256]{1,0:T(8,128)(2,1)S(1)}, bf16[176,256]{1,0:T(8,128)(2,1)S(1)}, u32[]{:S(2)}, u32[]{:S(2)}) collective-permute-start(bf16[176,256]{1,0:T(8,128)(2,1)S(1)} %get-tuple-element.37), channel_id=1, source_target_pairs={{0,4},{2,6},{4,0},{6,2},{8,12},{10,14},{12,8},{14,10},{1,5},{3,7},... | collective-permute-start | bytes 270344 | tf_op jit(solution)/shard_map/ppermute | solution.py:373
  23.9 2.6 %collective-permute-start.4 = (bf16[176,256]{1,0:T(8,128)(2,1)S(1)}, bf16[176,256]{1,0:T(8,128)(2,1)S(1)}, u32[]{:S(2)}, u32[]{:S(2)}) collective-permute-start(bf16[176,256]{1,0:T(8,128)(2,1)S(1)} %get-tuple-element.38), channel_id=1, source_target_pairs={{0,8},{2,10},{4,12},{6,14},{8,0},{10,2},{12,4},{14,6},{1,9},{3,11}... | collective-permute-start | bytes 270344 | tf_op jit(solution)/shard_map/ppermute | solution.py:373
  26.5 2.4 %collective-permute-done.9.got_ref = bf16[4,176,256]{2,1,0:T(8,128)(2,1)S(1)} collective-permute-done((bf16[4,176,256]{2,1,0:T(8,128)(2,1)S(1)}, bf16[4,176,256]{2,1,0:T(8,128)(2,1)S(1)}, u32[]{:S(2)}, u32[]{:S(2)}) %collective-permute-start.9) | collective-permute-done | bytes 360480 | tf_op jit(solution)/shard_map/ppermute | solution.py:367
  29.0 0.6 shard_map.35
  29.6 2.1 %collective-permute-start.10 = (bf16[176,256]{1,0:T(8,128)(2,1)S(1)}, bf16[176,256]{1,0:T(8,128)(2,1)S(1)}, u32[]{:S(2)}, u32[]{:S(2)}) collective-permute-start(bf16[176,256]{1,0:T(8,128)(2,1)S(1)} %get-tuple-element.48), channel_id=1, source_target_pairs={{0,4},{2,6},{4,0},{6,2},{8,12},{10,14},{12,8},{14,10},{1,5},{3,7},... | collective-permute-start | bytes 270344 | tf_op jit(solution)/shard_map/ppermute | solution.py:373
  31.6 2.6 %collective-permute-start.11 = (bf16[176,256]{1,0:T(8,128)(2,1)S(1)}, bf16[176,256]{1,0:T(8,128)(2,1)S(1)}, u32[]{:S(2)}, u32[]{:S(2)}) collective-permute-start(bf16[176,256]{1,0:T(8,128)(2,1)S(1)} %get-tuple-element.49), channel_id=1, source_target_pairs={{0,8},{2,10},{4,12},{6,14},{8,0},{10,2},{12,4},{14,6},{1,9},{3,11}... | collective-permute-start | bytes 270344 | tf_op jit(solution)/shard_map/ppermute | solution.py:373
  34.2 1.4 %collective-permute-start.12 = (bf16[176,256]{1,0:T(8,128)(2,1)S(1)}, bf16[176,256]{1,0:T(8,128)(2,1)S(1)}, u32[]{:S(2)}, u32[]{:S(2)}) collective-permute-start(bf16[176,256]{1,0:T(8,128)(2,1)S(1)} %get-tuple-element.50), channel_id=1, source_target_pairs={{0,12},{2,14},{4,8},{6,10},{8,4},{10,6},{12,0},{14,2},{1,13},{3,15... | collective-permute-start | bytes 270344 | tf_op jit(solution)/shard_map/ppermute | solution.py:373
  35.7 0.4 shard_map.33
  36.1 0.6 shard_map.34
  36.8 1.5 %collective-permute-start.6 = (bf16[160,256]{1,0:T(8,128)(2,1)S(1)}, bf16[160,256]{1,0:T(8,128)(2,1)S(1)}, u32[]{:S(2)}, u32[]{:S(2)}) collective-permute-start(bf16[160,256]{1,0:T(8,128)(2,1)S(1)} %get-tuple-element.42), channel_id=1, source_target_pairs={{0,4},{2,6},{4,0},{6,2},{8,12},{10,14},{12,8},{14,10},{1,5},{3,7},... | collective-permute-start | bytes 245768 | tf_op jit(solution)/shard_map/ppermute | solution.py:373
  38.2 2.6 %collective-permute-start.7 = (bf16[160,256]{1,0:T(8,128)(2,1)S(1)}, bf16[160,256]{1,0:T(8,128)(2,1)S(1)}, u32[]{:S(2)}, u32[]{:S(2)}) collective-permute-start(bf16[160,256]{1,0:T(8,128)(2,1)S(1)} %get-tuple-element.43), channel_id=1, source_target_pairs={{0,8},{2,10},{4,12},{6,14},{8,0},{10,2},{12,4},{14,6},{1,9},{3,11}... | collective-permute-start | bytes 245768 | tf_op jit(solution)/shard_map/ppermute | solution.py:373
  41.7 1.0 %collective-permute-done.6.refs_2_ = bf16[160,256]{1,0:T(8,128)(2,1)S(1)} collective-permute-done((bf16[160,256]{1,0:T(8,128)(2,1)S(1)}, bf16[160,256]{1,0:T(8,128)(2,1)S(1)}, u32[]{:S(2)}, u32[]{:S(2)}) %collective-permute-start.6) | collective-permute-done | bytes 81952 | tf_op jit(solution)/shard_map/ppermute | solution.py:373
  42.6 5.2 %collective-permute-done.7.refs_3_ = bf16[160,256]{1,0:T(8,128)(2,1)S(1)} collective-permute-done((bf16[160,256]{1,0:T(8,128)(2,1)S(1)}, bf16[160,256]{1,0:T(8,128)(2,1)S(1)}, u32[]{:S(2)}, u32[]{:S(2)}) %collective-permute-start.7) | collective-permute-done | bytes 81952 | tf_op jit(solution)/shard_map/ppermute | solution.py:373
  47.8 0.4 shard_map.37
  48.4 1.2 %collective-permute-done.13 = f32[136,128]{1,0:T(8,128)S(1)} collective-permute-done((f32[136,128]{1,0:T(8,128)S(1)}, f32[136,128]{1,0:T(8,128)S(1)}, u32[]{:S(2)}, u32[]{:S(2)}) %collective-permute-start.13) | collective-permute-done | bytes 69664 | tf_op jit(solution)/shard_map/ppermute | solution.py:380
  49.6 1.5 %collective-permute-start.14 = (f32[136,128]{1,0:T(8,128)S(1)}, f32[136,128]{1,0:T(8,128)S(1)}, u32[]{:S(2)}, u32[]{:S(2)}) collective-permute-start(f32[136,128]{1,0:T(8,128)S(1)} %add.18), channel_id=1, source_target_pairs={{0,2},{2,0},{4,6},{6,4},{8,10},{10,8},{12,14},{14,12},{1,3},{3,1},... | collective-permute-start | bytes 208904 | tf_op jit(solution)/shard_map/ppermute | solution.py:383
  51.1 2.8 %collective-permute-done.14 = f32[136,128]{1,0:T(8,128)S(1)} collective-permute-done((f32[136,128]{1,0:T(8,128)S(1)}, f32[136,128]{1,0:T(8,128)S(1)}, u32[]{:S(2)}, u32[]{:S(2)}) %collective-permute-start.14) | collective-permute-done | bytes 69664 | tf_op jit(solution)/shard_map/ppermute | solution.py:383
  54.0 1.7 %collective-permute-start.15 = (f32[136,128]{1,0:T(8,128)S(1)}, f32[136,128]{1,0:T(8,128)S(1)}, u32[]{:S(2)}, u32[]{:S(2)}) collective-permute-start(f32[136,128]{1,0:T(8,128)S(1)} %add.19), channel_id=1, source_target_pairs={{0,4},{2,6},{4,0},{6,2},{8,12},{10,14},{12,8},{14,10},{1,5},{3,7},... | collective-permute-start | bytes 208904 | tf_op jit(solution)/shard_map/ppermute | solution.py:383
  55.7 2.7 %collective-permute-done.15 = f32[136,128]{1,0:T(8,128)S(1)} collective-permute-done((f32[136,128]{1,0:T(8,128)S(1)}, f32[136,128]{1,0:T(8,128)S(1)}, u32[]{:S(2)}, u32[]{:S(2)}) %collective-permute-start.15) | collective-permute-done | bytes 69664 | tf_op jit(solution)/shard_map/ppermute | solution.py:383
  58.4 2.7 %collective-permute-start.16 = (f32[136,128]{1,0:T(8,128)S(1)}, f32[136,128]{1,0:T(8,128)S(1)}, u32[]{:S(2)}, u32[]{:S(2)}) collective-permute-start(f32[136,128]{1,0:T(8,128)S(1)} %add.20), channel_id=1, source_target_pairs={{0,8},{2,10},{4,12},{6,14},{8,0},{10,2},{12,4},{14,6},{1,9},{3,11}... | collective-permute-start | bytes 208904 | tf_op jit(solution)/shard_map/ppermute | solution.py:383
  61.1 2.6 %collective-permute-done.16 = f32[136,128]{1,0:T(8,128)S(1)} collective-permute-done((f32[136,128]{1,0:T(8,128)S(1)}, f32[136,128]{1,0:T(8,128)S(1)}, u32[]{:S(2)}, u32[]{:S(2)}) %collective-permute-start.16) | collective-permute-done | bytes 69664 | tf_op jit(solution)/shard_map/ppermute | solution.py:383
  63.8 1.2 %collective-permute-done.17.other_ref = f32[136,128]{1,0:T(8,128)S(1)} collective-permute-done((f32[136,128]{1,0:T(8,128)S(1)}, f32[136,128]{1,0:T(8,128)S(1)}, u32[]{:S(2)}, u32[]{:S(2)}) %collective-permute-start.17) | collective-permute-done | bytes 69664 | tf_op jit(solution)/shard_map/ppermute | solution.py:385
  65.0 8.2 %shard_map.38 = f32[512,256]{1,0:T(8,128)} custom-call(s32[1]{0:T(128)} %bitcast.refs_0_.pix_ref, f32[136,128]{1,0:T(8,128)S(1)} %add.21.mine_ref, f32[136,128]{1,0:T(8,128)S(1)} %collective-permute-done.17.other_ref, f32[176,256]{1,0:T(8,128)S(1)} %get-tuple-element.40.refs_0_, f32[176,256]{1,0:T(8,128)S(1)} %get-tuple-element.55.refs_1_, ...), custom_call_target="tpu_custom_call" | custom-call | tf_op jit(solution)/shard_map/pallas_call | solution.py:335
  (21 shorter events, 1.2 us)
Async XLA Ops:
  4.6 3.4 %collective-permute-start = (f32[256,1024]{1,0:T(8,128)S(1)}, f32[256,1024]{1,0:T(8,128)S(1)}, u32[]{:S(2)}, u32[]{:S(2)}) collective-permute-start(f32[256,1024]{1,0:T(8,128)S(1)} %shard_map.28.after_ref.mine_ref), channel_id=1, source_target_pairs={{0,1},{1,0},{2,3},{3,2},{4,5},{5,4},{6,7},{7,6},{8,9},{9,8},{10,11... | collective-permute-start | bytes 3145736 | tf_op jit(solution)/shard_map/ppermute | solution.py:364
  9.4 11.9 %collective-permute-start.2 = (bf16[4,176,256]{2,1,0:T(8,128)(2,1)S(1)}, bf16[4,176,256]{2,1,0:T(8,128)(2,1)S(1)}, u32[]{:S(2)}, u32[]{:S(2)}) collective-permute-start(bf16[4,176,256]{2,1,0:T(8,128)(2,1)S(1)} %get-tuple-element.34), channel_id=1, source_target_pairs={{0,2},{2,0},{4,6},{6,4},{8,10},{10,8},{12,14},{14,12},{1,3},{3,1},... | collective-permute-start | bytes 1081352 | tf_op jit(solution)/shard_map/ppermute | solution.py:367
  12.0 17.0 %collective-permute-start.9 = (bf16[4,176,256]{2,1,0:T(8,128)(2,1)S(1)}, bf16[4,176,256]{2,1,0:T(8,128)(2,1)S(1)}, u32[]{:S(2)}, u32[]{:S(2)}) collective-permute-start(bf16[4,176,256]{2,1,0:T(8,128)(2,1)S(1)} %get-tuple-element.45), channel_id=1, source_target_pairs={{0,2},{2,0},{4,6},{6,4},{8,10},{10,8},{12,14},{14,12},{1,3},{3,1},... | collective-permute-start | bytes 1081352 | tf_op jit(solution)/shard_map/ppermute | solution.py:367
  12.1 24.1 %collective-permute-start.1 = (bf16[4,160,256]{2,1,0:T(8,128)(2,1)S(1)}, bf16[4,160,256]{2,1,0:T(8,128)(2,1)S(1)}, u32[]{:S(2)}, u32[]{:S(2)}) collective-permute-start(bf16[4,160,256]{2,1,0:T(8,128)(2,1)S(1)} %get-tuple-element.31), channel_id=1, source_target_pairs={{0,2},{2,0},{4,6},{6,4},{8,10},{10,8},{12,14},{14,12},{1,3},{3,1},... | collective-permute-start | bytes 983048 | tf_op jit(solution)/shard_map/ppermute | solution.py:367
  21.9 9.8 %collective-permute-start.3 = (bf16[176,256]{1,0:T(8,128)(2,1)S(1)}, bf16[176,256]{1,0:T(8,128)(2,1)S(1)}, u32[]{:S(2)}, u32[]{:S(2)}) collective-permute-start(bf16[176,256]{1,0:T(8,128)(2,1)S(1)} %get-tuple-element.37), channel_id=1, source_target_pairs={{0,4},{2,6},{4,0},{6,2},{8,12},{10,14},{12,8},{14,10},{1,5},{3,7},... | collective-permute-start | bytes 270344 | tf_op jit(solution)/shard_map/ppermute | solution.py:373
  23.9 10.3 %collective-permute-start.4 = (bf16[176,256]{1,0:T(8,128)(2,1)S(1)}, bf16[176,256]{1,0:T(8,128)(2,1)S(1)}, u32[]{:S(2)}, u32[]{:S(2)}) collective-permute-start(bf16[176,256]{1,0:T(8,128)(2,1)S(1)} %get-tuple-element.38), channel_id=1, source_target_pairs={{0,8},{2,10},{4,12},{6,14},{8,0},{10,2},{12,4},{14,6},{1,9},{3,11}... | collective-permute-start | bytes 270344 | tf_op jit(solution)/shard_map/ppermute | solution.py:373
  26.5 9.1 %collective-permute-start.5 = (bf16[176,256]{1,0:T(8,128)(2,1)S(1)}, bf16[176,256]{1,0:T(8,128)(2,1)S(1)}, u32[]{:S(2)}, u32[]{:S(2)}) collective-permute-start(bf16[176,256]{1,0:T(8,128)(2,1)S(1)} %get-tuple-element.39), channel_id=1, source_target_pairs={{0,12},{2,14},{4,8},{6,10},{8,4},{10,6},{12,0},{14,2},{1,13},{3,15... | collective-permute-start | bytes 270344 | tf_op jit(solution)/shard_map/ppermute | solution.py:373
  29.6 11.2 %collective-permute-start.10 = (bf16[176,256]{1,0:T(8,128)(2,1)S(1)}, bf16[176,256]{1,0:T(8,128)(2,1)S(1)}, u32[]{:S(2)}, u32[]{:S(2)}) collective-permute-start(bf16[176,256]{1,0:T(8,128)(2,1)S(1)} %get-tuple-element.48), channel_id=1, source_target_pairs={{0,4},{2,6},{4,0},{6,2},{8,12},{10,14},{12,8},{14,10},{1,5},{3,7},... | collective-permute-start | bytes 270344 | tf_op jit(solution)/shard_map/ppermute | solution.py:373
  31.6 9.6 %collective-permute-start.11 = (bf16[176,256]{1,0:T(8,128)(2,1)S(1)}, bf16[176,256]{1,0:T(8,128)(2,1)S(1)}, u32[]{:S(2)}, u32[]{:S(2)}) collective-permute-start(bf16[176,256]{1,0:T(8,128)(2,1)S(1)} %get-tuple-element.49), channel_id=1, source_target_pairs={{0,8},{2,10},{4,12},{6,14},{8,0},{10,2},{12,4},{14,6},{1,9},{3,11}... | collective-permute-start | bytes 270344 | tf_op jit(solution)/shard_map/ppermute | solution.py:373
  34.2 7.0 %collective-permute-start.12 = (bf16[176,256]{1,0:T(8,128)(2,1)S(1)}, bf16[176,256]{1,0:T(8,128)(2,1)S(1)}, u32[]{:S(2)}, u32[]{:S(2)}) collective-permute-start(bf16[176,256]{1,0:T(8,128)(2,1)S(1)} %get-tuple-element.50), channel_id=1, source_target_pairs={{0,12},{2,14},{4,8},{6,10},{8,4},{10,6},{12,0},{14,2},{1,13},{3,15... | collective-permute-start | bytes 270344 | tf_op jit(solution)/shard_map/ppermute | solution.py:373
  36.8 5.9 %collective-permute-start.6 = (bf16[160,256]{1,0:T(8,128)(2,1)S(1)}, bf16[160,256]{1,0:T(8,128)(2,1)S(1)}, u32[]{:S(2)}, u32[]{:S(2)}) collective-permute-start(bf16[160,256]{1,0:T(8,128)(2,1)S(1)} %get-tuple-element.42), channel_id=1, source_target_pairs={{0,4},{2,6},{4,0},{6,2},{8,12},{10,14},{12,8},{14,10},{1,5},{3,7},... | collective-permute-start | bytes 245768 | tf_op jit(solution)/shard_map/ppermute | solution.py:373
  38.2 9.6 %collective-permute-start.7 = (bf16[160,256]{1,0:T(8,128)(2,1)S(1)}, bf16[160,256]{1,0:T(8,128)(2,1)S(1)}, u32[]{:S(2)}, u32[]{:S(2)}) collective-permute-start(bf16[160,256]{1,0:T(8,128)(2,1)S(1)} %get-tuple-element.43), channel_id=1, source_target_pairs={{0,8},{2,10},{4,12},{6,14},{8,0},{10,2},{12,4},{14,6},{1,9},{3,11}... | collective-permute-start | bytes 245768 | tf_op jit(solution)/shard_map/ppermute | solution.py:373
  40.8 7.0 %collective-permute-start.8 = (bf16[160,256]{1,0:T(8,128)(2,1)S(1)}, bf16[160,256]{1,0:T(8,128)(2,1)S(1)}, u32[]{:S(2)}, u32[]{:S(2)}) collective-permute-start(bf16[160,256]{1,0:T(8,128)(2,1)S(1)} %get-tuple-element.44), channel_id=1, source_target_pairs={{0,12},{2,14},{4,8},{6,10},{8,4},{10,6},{12,0},{14,2},{1,13},{3,15... | collective-permute-start | bytes 245768 | tf_op jit(solution)/shard_map/ppermute | solution.py:373
  48.3 1.3 %collective-permute-start.13 = (f32[136,128]{1,0:T(8,128)S(1)}, f32[136,128]{1,0:T(8,128)S(1)}, u32[]{:S(2)}, u32[]{:S(2)}) collective-permute-start(f32[136,128]{1,0:T(8,128)S(1)} %get-tuple-element.54), channel_id=1, source_target_pairs={{0,1},{1,0},{2,3},{3,2},{4,5},{5,4},{6,7},{7,6},{8,9},{9,8},{10,11... | collective-permute-start | bytes 208904 | tf_op jit(solution)/shard_map/ppermute | solution.py:380
  49.6 4.4 %collective-permute-start.14 = (f32[136,128]{1,0:T(8,128)S(1)}, f32[136,128]{1,0:T(8,128)S(1)}, u32[]{:S(2)}, u32[]{:S(2)}) collective-permute-start(f32[136,128]{1,0:T(8,128)S(1)} %add.18), channel_id=1, source_target_pairs={{0,2},{2,0},{4,6},{6,4},{8,10},{10,8},{12,14},{14,12},{1,3},{3,1},... | collective-permute-start | bytes 208904 | tf_op jit(solution)/shard_map/ppermute | solution.py:383
  54.0 4.4 %collective-permute-start.15 = (f32[136,128]{1,0:T(8,128)S(1)}, f32[136,128]{1,0:T(8,128)S(1)}, u32[]{:S(2)}, u32[]{:S(2)}) collective-permute-start(f32[136,128]{1,0:T(8,128)S(1)} %add.19), channel_id=1, source_target_pairs={{0,4},{2,6},{4,0},{6,2},{8,12},{10,14},{12,8},{14,10},{1,5},{3,7},... | collective-permute-start | bytes 208904 | tf_op jit(solution)/shard_map/ppermute | solution.py:383
  58.4 5.3 %collective-permute-start.16 = (f32[136,128]{1,0:T(8,128)S(1)}, f32[136,128]{1,0:T(8,128)S(1)}, u32[]{:S(2)}, u32[]{:S(2)}) collective-permute-start(f32[136,128]{1,0:T(8,128)S(1)} %add.20), channel_id=1, source_target_pairs={{0,8},{2,10},{4,12},{6,14},{8,0},{10,2},{12,4},{14,6},{1,9},{3,11}... | collective-permute-start | bytes 208904 | tf_op jit(solution)/shard_map/ppermute | solution.py:383
  63.7 1.3 %collective-permute-start.17 = (f32[136,128]{1,0:T(8,128)S(1)}, f32[136,128]{1,0:T(8,128)S(1)}, u32[]{:S(2)}, u32[]{:S(2)}) collective-permute-start(f32[136,128]{1,0:T(8,128)S(1)} %add.21.mine_ref), channel_id=1, source_target_pairs={{0,1},{1,0},{2,3},{3,2},{4,5},{5,4},{6,7},{7,6},{8,9},{9,8},{10,11... | collective-permute-start | bytes 208904 | tf_op jit(solution)/shard_map/ppermute | solution.py:385

commit v5 on v4

--- a/solution.py
+++ b/solution.py
@@ -7,7 +7,7 @@
 from jax.experimental.pallas import tpu as pltpu
 from jax.sharding import PartitionSpec as P
 
-SHARES = (1, 1, 1)
+SHARES = (13, 13, 6)
 PIECES = 8
 PANEL = 16
 WINDOW = 32
@@ -69,95 +69,131 @@
     )(spectra, probes)
 
 
-def block_copies(spectra_hbm, blocks_ref, sems, side):
-    outer, rows, _ = blocks_ref.shape
-    starts = [pl.multiple_of((i * 2 + side) * rows, 16) for i in range(outer)]
+def block_copies(spectra_hbm, target_ref, sems, sources, size):
     return [
-        pltpu.make_async_copy(spectra_hbm.at[pl.ds(start, rows)], blocks_ref.at[i], sems.at[i])
-        for i, start in enumerate(starts)
+        pltpu.make_async_copy(
+            spectra_hbm.at[pl.ds(pl.multiple_of(start, 16), size)], target_ref.at[pl.ds(i * size, size)], sems.at[i]
+        )
+        for i, start in enumerate(sources)
     ]
 
 
-def fetch_kernel(idx_ref, spectra_hbm, after_ref, blocks_ref, sems):
-    copies = block_copies(spectra_hbm, blocks_ref, sems, 1 - idx_ref[0])
+def fetch_kernel(sizes, idx_ref, spectra_hbm, after_ref, *refs):
+    *targets, sems = refs
+    rows, outer = sum(sizes), spectra_hbm.shape[0] // (2 * sum(sizes))
+    side, me = idx_ref[0], idx_ref[1]
+    copies, first = [], 0
+    for c, size in enumerate(sizes):
+        if c < len(sizes) - 1:
+            sources = [(i * 2 + 1 - side) * rows + first for i in range(outer)]
+        else:
+            sources = [
+                (lax.bitwise_xor(me, d) * 2 + y) * rows + first for d in range(outer) for y in (side, 1 - side)
+            ]
+        copies += block_copies(spectra_hbm, targets[c], sems.at[c], sources, size)
+        first += size
     for copy in copies:
         copy.start()
     for copy in copies:
         copy.wait()
 
 
-def fetch_blocks(idx, spectra, rows, after):
-    outer, bins = spectra.shape[0] // (2 * rows), spectra.shape[1]
-    return pl.pallas_call(
-        fetch_kernel,
+def fetch_blocks(idx, spectra, sizes, after):
+    outer, bins = spectra.shape[0] // (2 * sum(sizes)), spectra.shape[1]
+    heights = [outer * size for size in sizes[:-1]] + [2 * outer * sizes[-1]]
+    return pl.pallas_call(
+        functools.partial(fetch_kernel, sizes),
         in_specs=[SMEM, HBM, pl.BlockSpec(memory_space=pl.ANY)],
-        out_specs=VMEM,
-        out_shape=jax.ShapeDtypeStruct((outer, rows, bins), BF16),
-        scratch_shapes=[pltpu.SemaphoreType.DMA((outer,))],
-        compiler_params=params(48),
-        cost_estimate=pl.CostEstimate(flops=0, bytes_accessed=outer * rows * bins * 4, transcendentals=0),
+        out_specs=[VMEM] * len(sizes),
+        out_shape=[jax.ShapeDtypeStruct((height, bins), BF16) for height in heights],
+        scratch_shapes=[pltpu.SemaphoreType.DMA((len(sizes), 2 * outer))],
+        compiler_params=params(46),
+        cost_estimate=pl.CostEstimate(flops=0, bytes_accessed=sum(heights) * bins * 4, transcendentals=0),
     )(idx, spectra, after)
 
 
-def away_kernel(blocks_ref, mine_ref, got_ref, loadings_ref, *out_refs):
+def away_kernel(n, *refs):
+    blocks, (mine_ref, got_ref, loadings_ref, *outs) = refs[:n], refs[n:]
     loadings_ref[...] = (mine_ref[...] + got_ref[...]).T.astype(BF16)
-    first = 0
-    for out_ref in out_refs:
-        size = out_ref.shape[1]
-        for i in range(out_ref.shape[0]):
-            out_ref[i] = jnp.dot(
-                blocks_ref[i, first:first + size], loadings_ref[...], preferred_element_type=F32
-            ).astype(out_ref.dtype)
-        first += size
-
-
-def image_away(blocks, mine, got, sizes):
-    outer, rows, bins = blocks.shape
-    cols = mine.shape[0]
+    products = [jnp.dot(x[...], loadings_ref[...], preferred_element_type=F32) for x in blocks]
+    for product, out_ref in zip(products[:-1], outs):
+        out_ref[...] = product.astype(BF16)
+    size = outs[-1].shape[0]
+    for d, out_ref in enumerate(outs[n - 1:]):
+        out_ref[...] = products[-1][d * size:(d + 1) * size].astype(out_ref.dtype)
+
+
+def image_away(blocks, mine, got, outer):
+    cols, bins = mine.shape
+    size = blocks[-1].shape[0] // outer
     shapes = [jax.ShapeDtypeStruct((bins, cols), BF16)]
-    shapes += [jax.ShapeDtypeStruct((outer, size, cols), BF16) for size in sizes]
-    return pl.pallas_call(
-        away_kernel,
-        in_specs=[VMEM] * 3,
+    shapes += [jax.ShapeDtypeStruct((x.shape[0], cols), BF16) for x in blocks[:-1]]
+    shapes += [jax.ShapeDtypeStruct((size, cols), BF16 if d else F32) for d in range(outer)]
+    height = sum(x.shape[0] for x in blocks)
+    return pl.pallas_call(
+        functools.partial(away_kernel, len(blocks)),
+        in_specs=[VMEM] * (len(blocks) + 2),
         out_specs=[VMEM] * len(shapes),
         out_shape=shapes,
         compiler_params=params(),
         cost_estimate=pl.CostEstimate(
-            flops=2 * outer * rows * bins * cols, bytes_accessed=outer * rows * cols * 4, transcendentals=0
+            flops=2 * height * bins * cols, bytes_accessed=height * cols * 4, transcendentals=0
         ),
-    )(blocks, mine, got)
-
-
-def kept_kernel(idx_ref, spectra_hbm, loadings_ref, *refs):
-    *out_refs, blocks_ref, sems = refs
-    copies = block_copies(spectra_hbm, blocks_ref, sems, idx_ref[0])
+    )(*blocks, mine, got)
+
+
+def kept_kernel(rows, sizes, idx_ref, spectra_hbm, loadings_ref, *refs):
+    outs, (blocks_ref, sems) = refs[:-2], refs[-2:]
+    outer, size = blocks_ref.shape[0] // sum(sizes), sum(sizes)
+    copies = block_copies(
+        spectra_hbm, blocks_ref, sems, [(i * 2 + idx_ref[0]) * rows for i in range(outer)], size
+    )
     for copy in copies:
         copy.start()
     for i, copy in enumerate(copies):
         copy.wait()
+        product = jnp.dot(blocks_ref[i * size:(i + 1) * size], loadings_ref[...], preferred_element_type=F32)
         first = 0
-        for out_ref in out_refs:
-            size = out_ref.shape[1]
-            out_ref[i] = jnp.dot(
-                blocks_ref[i, first:first + size], loadings_ref[...], preferred_element_type=F32
-            )
-            first += size
-
-
-def image_kept(idx, spectra, loadings, sizes):
-    rows = sum(sizes)
+        for out_ref in outs:
+            out_ref[i] = product[first:first + out_ref.shape[1]]
+            first += out_ref.shape[1]
+
+
+def image_kept(idx, spectra, loadings, rows, sizes):
     outer, (bins, cols) = spectra.shape[0] // (2 * rows), loadings.shape
     return pl.pallas_call(
-        kept_kernel,
+        functools.partial(kept_kernel, rows, sizes),
         in_specs=[SMEM, HBM, VMEM],
         out_specs=[VMEM] * len(sizes),
         out_shape=[jax.ShapeDtypeStruct((outer, size, cols), F32) for size in sizes],
-        scratch_shapes=[pltpu.VMEM((outer, rows, bins), BF16), pltpu.SemaphoreType.DMA((outer,))],
+        scratch_shapes=[pltpu.VMEM((outer * sum(sizes), bins), BF16), pltpu.SemaphoreType.DMA((outer,))],
         compiler_params=params(48),
         cost_estimate=pl.CostEstimate(
             flops=2 * outer * rows * bins * cols, bytes_accessed=outer * rows * (bins * 2 + cols * 4), transcendentals=0
         ),
     )(idx, spectra, loadings)
+
+
+def sides_kernel(mine_ref, *refs):
+    *got_refs, own_ref, send_ref = refs
+    total = mine_ref[...]
+    for got in got_refs:
+        total = total + got[...].astype(F32)
+    size = own_ref.shape[0]
+    own_ref[...] = total[:size]
+    send_ref[...] = total[size:].astype(BF16)
+
+
+def sides_chunk(mine, got):
+    size, cols = mine.shape[0] // 2, mine.shape[1]
+    return pl.pallas_call(
+        sides_kernel,
+        in_specs=[VMEM] * (1 + len(got)),
+        out_specs=[VMEM] * 2,
+        out_shape=[jax.ShapeDtypeStruct((size, cols), F32), jax.ShapeDtypeStruct((size, cols), BF16)],
+        compiler_params=params(),
+        cost_estimate=pl.CostEstimate(flops=8 * size * cols, bytes_accessed=16 * size * cols, transcendentals=0),
+    )(mine, *got)
 
 
 def add_kernel(n_after, idx_ref, got_ref, kept_ref, *refs):
@@ -362,26 +398,44 @@
     sizes = split(rows)
     terms = loadings_terms(spectra, probes)
     got = lax.ppermute(terms, "pix", xor_pairs(2, 1))
-    blocks = fetch_blocks(idx, spectra, rows, terms)
-    loadings, *away = image_away(blocks, terms, got, sizes)
-    away = [lax.ppermute(out, "bins", xor_pairs(n_bins, 1)) for out in away]
-    kept = image_kept(idx, spectra, loadings, sizes)
+    outer = n_bins // 2
+    blocks = fetch_blocks(idx, spectra, sizes, terms)
+    loadings, *parts = image_away(blocks, terms, got, outer)
+    n = len(sizes) - 1
+    away = [
+        lax.ppermute(out.reshape(outer, -1, cols), "bins", xor_pairs(n_bins, 1)) for out in parts[:n]
+    ]
+
+    def along_z(sends):
+        return [
+            lax.ppermute(sends[d - 1], "bins", xor_pairs(n_bins, 2 * d)) for d in range(outer - 1, 0, -1)
+        ]
+
+    sides = along_z(parts[n + 1:])
+    kept = image_kept(idx, spectra, loadings, rows, sizes[:-1])
     gram = jnp.zeros((cols, cols), F32)
+    own, send = sides_chunk(parts[n], sides)
+    crossed = lax.ppermute(send, "bins", xor_pairs(n_bins, 1))
+    last, gram = gram_chunk(own, [crossed], gram)
     image = []
-    for c in range(len(sizes)):
-        own, *sends = add_chunk(idx, away[c], kept[c], image[c - 2:c - 1] if c > 1 else [])
-        arrived = [lax.ppermute(s, "bins", xor_pairs(n_bins, 2 * (d + 1))) for d, s in enumerate(sends)]
-        if c < len(sizes) - 1:
-            x, gram = gram_chunk(own, arrived, gram)
+    for c in range(n):
+        first, *sends = add_chunk(idx, away[c], kept[c], [own] if c == 0 else [])
+        arrived = along_z(sends)
+        if c < n - 1:
+            x, gram = gram_chunk(first, arrived, gram)
         else:
-            x, mine, other = gram_chunk(own, arrived, gram, pix)
+            x, mine, other = gram_chunk(first, arrived, gram, pix)
         image.append(x)
+    image.append(last)
 
     mine = mine + lax.ppermute(other, "pix", xor_pairs(2, 1))
     d = 1
     while d < n_bins:
-        mine = mine + lax.ppermute(mine, "bins", xor_pairs(n_bins, d))
-        d *= 2
+        if d == 1 and n_bins > 2:
+            both, near, far = (lax.ppermute(mine, "bins", xor_pairs(n_bins, k)) for k in (3, 1, 2))
+            mine, d = (mine + near) + (far + both), 4
+        else:
+            mine, d = mine + lax.ppermute(mine, "bins", xor_pairs(n_bins, d)), 2 * d
     other = lax.ppermute(mine, "pix", xor_pairs(2, 1))
     basis = basis_of(pix, mine, other, image, 2 * rows_dev)
     return basis.reshape(1, rows, cols)

time: 73.4 us -> 70.6 us (0.962)
  starting transfers between devices: 26.4 us -> 24.7 us
  waiting for transfers between devices: 22.5 us -> 21.2 us
    ppermute x15 -> x16, starting transfers between devices: 25.7 us -> 24.1 us  [the longest x9 13.8 us: along_z(): lax.ppermute(sends[d - 1], 'bins', xor_pairs(n_bins, 2 * d))]
    ppermute x15 -> x16, waiting for transfers between devices: 20 us -> 18.7 us  [the longest x9 11.6 us: along_z(): lax.ppermute(sends[d - 1], 'bins', xor_pairs(n_bins, 2 * d))]
    pallas_call x3 -> x4, Pallas kernels: 8.08 us -> 8.89 us  [the longest x1 4.1 us: image_kept(): pl.pallas_call(functools.partial(kept_kernel, rows, sizes), in_specs=[SME...]
    pallas_call x3 -> x2, Pallas kernels: 1.84 us -> 1.27 us  [add_chunk(): pl.pallas_call(functools.partial(add_kernel, len(after)), in_specs=[SMEM,...]
  transfers between devices with their start and end apart: 18 -> 19, of which waited for: 9 -> 10; matrix products, arithmetic and copies ran while one was open for 0% -> 0% of each run, Pallas kernels for 13% -> 13%
where the time goes in v5:
time: 70.6 us; the launch traced here: 70.4 us
  starting transfers between devices  24.7 us (35%)
  Pallas kernels  24.3 us (34%)
  waiting for transfers between devices  21.2 us (30%)
    ppermute x9, starting transfers between devices, along_z(): lax.ppermute(sends[d - 1], 'bins', xor_pairs(n_bins, 2 * d))  13.8 us
    ppermute x9, waiting for transfers between devices, along_z(): lax.ppermute(sends[d - 1], 'bins', xor_pairs(n_bins, 2 * d))  11.6 us
    pallas_call x1, Pallas kernels, basis_of(): pl.pallas_call(functools.partial(basis_kernel, pixels), in_specs=[SMEM] +...  8.21 us
    pallas_call x1, Pallas kernels, loadings_terms(): pl.pallas_call(loadings_kernel, in_specs=[HBM, HBM], out_specs=VMEM, out_...  4.61 us
    pallas_call x1, Pallas kernels, image_kept(): pl.pallas_call(functools.partial(kept_kernel, rows, sizes), in_specs=[SME...  4.1 us
    ppermute x3, waiting for transfers between devices, on_device(): lax.ppermute(mine, 'bins', xor_pairs(n_bins, k))  3.64 us
    ppermute x3, starting transfers between devices, on_device(): lax.ppermute(mine, 'bins', xor_pairs(n_bins, k))  3.55 us
    pallas_call x1, Pallas kernels, fetch_blocks(): pl.pallas_call(functools.partial(fetch_kernel, sizes), in_specs=[SMEM, HB...  3.13 us
  transfers between devices with their start and end apart: 19, of which 10 were waited for; matrix products, arithmetic and copies ran while one was open for 0% of the time, Pallas kernels for 13%

profile of v5, /device:TPU:0, one launch (start us, length us, event | category | flops | bytes accessed | tf_op | source)
XLA Modules:
  0.0 70.4 jit_solution(2698579709538494079)
XLA Ops:
  0.0 4.6 %shard_map.28.after_ref.refs_3_ = f32[256,1024]{1,0:T(8,128)S(1)} custom-call(bf16[4096,1024]{1,0:T(8,128)(2,1)} %spectra_hbm.5, bf16[4096,256]{1,0:T(8,128)(2,1)} %probes_hbm.1), custom_call_target="tpu_custom_call" | custom-call | flops 2147483648 | bytes 10485760 | tf_op jit(solution)/shard_map/pallas_call | solution.py:55
  4.6 0.5 collective-permute-start
  5.2 3.1 %shard_map.29 = (bf16[832,1024]{1,0:T(8,128)(2,1)S(1)}, bf16[832,1024]{1,0:T(8,128)(2,1)S(1)}, bf16[768,1024]{1,0:T(8,128)(2,1)S(1)}) custom-call(s32[2]{0:T(128)S(1)} %pad_add_fusion.idx_ref, bf16[4096,1024]{1,0:T(8,128)(2,1)} %spectra_hbm.5, f32[256,1024]{1,0:T(8,128)S(1)} %shard_map.28.after_ref.refs_3_), custom_call_target="tpu_custom_call" | custom-call | bytes 9961472 | tf_op jit(solution)/shard_map/pallas_call | solution.py:104
  8.4 1.6 %shard_map.30 = (bf16[1024,256]{1,0:T(8,128)(2,1)S(1)}, bf16[832,256]{1,0:T(8,128)(2,1)S(1)}, bf16[832,256]{1,0:T(8,128)(2,1)S(1)}, f32[192,256]{1,0:T(8,128)S(1...) custom-call(bf16[832,1024]{1,0:T(8,128)(2,1)S(1)} %get-tuple-element.34.refs_0_, ...), custom_call_target="tpu_custom_call" | custom-call | flops 1275068416 | bytes 2490368 | tf_op jit(solution)/shard_map/pallas_call | solution.py:133
  10.0 2.6 %collective-permute-start.5 = (bf16[4,208,256]{2,1,0:T(8,128)(2,1)S(1)}, bf16[4,208,256]{2,1,0:T(8,128)(2,1)S(1)}, u32[]{:S(2)}, u32[]{:S(2)}) collective-permute-start(bf16[4,208,256]{2,1,0:T(8,128)(2,1)S(1)} %bitcast.7), channel_id=1, source_target_pairs={{0,2},{2,0},{4,6},{6,4},{8,10},{10,8},{12,14},{14,12},{1,3},{3,1},... | collective-permute-start | bytes 1277960 | tf_op jit(solution)/shard_map/ppermute | solution.py:406
  12.7 4.0 %collective-permute-start.6 = (bf16[192,256]{1,0:T(8,128)(2,1)S(1)}, bf16[192,256]{1,0:T(8,128)(2,1)S(1)}, u32[]{:S(2)}, u32[]{:S(2)}) collective-permute-start(bf16[192,256]{1,0:T(8,128)(2,1)S(1)} %get-tuple-element.47), channel_id=1, source_target_pairs={{0,12},{2,14},{4,8},{6,10},{8,4},{10,6},{12,0},{14,2},{1,13},{3,15... | collective-permute-start | bytes 294920 | tf_op jit(solution)/shard_map/ppermute | solution.py:411
  16.7 0.6 collective-permute-start.8
  17.3 4.1 %shard_map.31 = (f32[4,208,256]{2,1,0:T(8,128)S(1)}, f32[4,208,256]{2,1,0:T(8,128)S(1)}) custom-call(s32[2]{0:T(128)S(1)} %pad_add_fusion.idx_ref, bf16[4096,1024]{1,0:T(8,128)(2,1)} %spectra_hbm.5, bf16[1024,256]{1,0:T(8,128)(2,1)S(1)} %get-tuple-element.38.loadings_ref), custom_call_target="tpu_custom_call" | custom-call | flops 1073741824 | bytes 6291456 | tf_op jit(solution)/shard_map/pallas_call | solution.py:164
  21.4 3.7 %collective-permute-done.7.refs_1_ = bf16[192,256]{1,0:T(8,128)(2,1)S(1)} collective-permute-done((bf16[192,256]{1,0:T(8,128)(2,1)S(1)}, bf16[192,256]{1,0:T(8,128)(2,1)S(1)}, u32[]{:S(2)}, u32[]{:S(2)}) %collective-permute-start.7) | collective-permute-done | bytes 98336 | tf_op jit(solution)/shard_map/ppermute | solution.py:411
  25.1 0.6 shard_map.34
  25.7 1.2 %collective-permute-start.10 = (bf16[208,256]{1,0:T(8,128)(2,1)S(1)}, bf16[208,256]{1,0:T(8,128)(2,1)S(1)}, u32[]{:S(2)}, u32[]{:S(2)}) collective-permute-start(bf16[208,256]{1,0:T(8,128)(2,1)S(1)} %get-tuple-element.53), channel_id=1, source_target_pairs={{0,8},{2,10},{4,12},{6,14},{8,0},{10,2},{12,4},{14,6},{1,9},{3,11}... | collective-permute-start | bytes 319496 | tf_op jit(solution)/shard_map/ppermute | solution.py:411
  27.0 1.5 %collective-permute-start.12 = (bf16[96,256]{1,0:T(8,128)(2,1)S(1)}, bf16[96,256]{1,0:T(8,128)(2,1)S(1)}, u32[]{:S(2)}, u32[]{:S(2)}) collective-permute-start(bf16[96,256]{1,0:T(8,128)(2,1)S(1)} %get-tuple-element.55), channel_id=1, source_target_pairs={{0,2},{2,0},{4,6},{6,4},{8,10},{10,8},{12,14},{14,12},{1,3},{3,1},... | collective-permute-start | bytes 147464 | tf_op jit(solution)/shard_map/ppermute | solution.py:418
  28.5 1.9 %collective-permute-start.11 = (bf16[208,256]{1,0:T(8,128)(2,1)S(1)}, bf16[208,256]{1,0:T(8,128)(2,1)S(1)}, u32[]{:S(2)}, u32[]{:S(2)}) collective-permute-start(bf16[208,256]{1,0:T(8,128)(2,1)S(1)} %get-tuple-element.54), channel_id=1, source_target_pairs={{0,4},{2,6},{4,0},{6,2},{8,12},{10,14},{12,8},{14,10},{1,5},{3,7},... | collective-permute-start | bytes 319496 | tf_op jit(solution)/shard_map/ppermute | solution.py:411
  30.4 1.4 %collective-permute-start.9 = (bf16[208,256]{1,0:T(8,128)(2,1)S(1)}, bf16[208,256]{1,0:T(8,128)(2,1)S(1)}, u32[]{:S(2)}, u32[]{:S(2)}) collective-permute-start(bf16[208,256]{1,0:T(8,128)(2,1)S(1)} %get-tuple-element.52), channel_id=1, source_target_pairs={{0,12},{2,14},{4,8},{6,10},{8,4},{10,6},{12,0},{14,2},{1,13},{3,15... | collective-permute-start | bytes 319496 | tf_op jit(solution)/shard_map/ppermute | solution.py:411
  31.7 0.7 collective-permute-done.1.got_ref
  32.4 0.6 shard_map.32
  33.0 4.1 %collective-permute-start.2 = (bf16[208,256]{1,0:T(8,128)(2,1)S(1)}, bf16[208,256]{1,0:T(8,128)(2,1)S(1)}, u32[]{:S(2)}, u32[]{:S(2)}) collective-permute-start(bf16[208,256]{1,0:T(8,128)(2,1)S(1)} %get-tuple-element.41), channel_id=1, source_target_pairs={{0,12},{2,14},{4,8},{6,10},{8,4},{10,6},{12,0},{14,2},{1,13},{3,15... | collective-permute-start | bytes 319496 | tf_op jit(solution)/shard_map/ppermute | solution.py:411
  37.1 0.6 collective-permute-start.4
  38.2 0.4 shard_map.36
  38.7 2.4 %collective-permute-done.2.refs_2_ = bf16[208,256]{1,0:T(8,128)(2,1)S(1)} collective-permute-done((bf16[208,256]{1,0:T(8,128)(2,1)S(1)}, bf16[208,256]{1,0:T(8,128)(2,1)S(1)}, u32[]{:S(2)}, u32[]{:S(2)}) %collective-permute-start.2) | collective-permute-done | bytes 106528 | tf_op jit(solution)/shard_map/ppermute | solution.py:411
  41.0 5.6 %collective-permute-done.3.refs_3_ = bf16[208,256]{1,0:T(8,128)(2,1)S(1)} collective-permute-done((bf16[208,256]{1,0:T(8,128)(2,1)S(1)}, bf16[208,256]{1,0:T(8,128)(2,1)S(1)}, u32[]{:S(2)}, u32[]{:S(2)}) %collective-permute-start.3) | collective-permute-done | bytes 106528 | tf_op jit(solution)/shard_map/ppermute | solution.py:411
  46.6 0.4 shard_map.37
  47.1 1.2 %collective-permute-done.13 = f32[136,128]{1,0:T(8,128)S(1)} collective-permute-done((f32[136,128]{1,0:T(8,128)S(1)}, f32[136,128]{1,0:T(8,128)S(1)}, u32[]{:S(2)}, u32[]{:S(2)}) %collective-permute-start.13) | collective-permute-done | bytes 69664 | tf_op jit(solution)/shard_map/ppermute | solution.py:431
  48.4 1.6 %collective-permute-start.14 = (f32[136,128]{1,0:T(8,128)S(1)}, f32[136,128]{1,0:T(8,128)S(1)}, u32[]{:S(2)}, u32[]{:S(2)}) collective-permute-start(f32[136,128]{1,0:T(8,128)S(1)} %add.21), channel_id=1, source_target_pairs={{0,2},{2,0},{4,6},{6,4},{8,10},{10,8},{12,14},{14,12},{1,3},{3,1},... | collective-permute-start | bytes 208904 | tf_op jit(solution)/shard_map/ppermute | solution.py:435
  50.0 2.0 %collective-permute-start.16 = (f32[136,128]{1,0:T(8,128)S(1)}, f32[136,128]{1,0:T(8,128)S(1)}, u32[]{:S(2)}, u32[]{:S(2)}) collective-permute-start(f32[136,128]{1,0:T(8,128)S(1)} %add.21), channel_id=1, source_target_pairs={{0,6},{2,4},{4,2},{6,0},{8,14},{10,12},{12,10},{14,8},{1,7},{3,5},... | collective-permute-start | bytes 208904 | tf_op jit(solution)/shard_map/ppermute | solution.py:435
  52.0 0.8 %collective-permute-done.14 = f32[136,128]{1,0:T(8,128)S(1)} collective-permute-done((f32[136,128]{1,0:T(8,128)S(1)}, f32[136,128]{1,0:T(8,128)S(1)}, u32[]{:S(2)}, u32[]{:S(2)}) %collective-permute-start.14) | collective-permute-done | bytes 69664 | tf_op jit(solution)/shard_map/ppermute | solution.py:435
  52.8 1.9 %collective-permute-done.15 = f32[136,128]{1,0:T(8,128)S(1)} collective-permute-done((f32[136,128]{1,0:T(8,128)S(1)}, f32[136,128]{1,0:T(8,128)S(1)}, u32[]{:S(2)}, u32[]{:S(2)}) %collective-permute-start.15) | collective-permute-done | bytes 69664 | tf_op jit(solution)/shard_map/ppermute | solution.py:435
  54.7 0.9 %collective-permute-done.16 = f32[136,128]{1,0:T(8,128)S(1)} collective-permute-done((f32[136,128]{1,0:T(8,128)S(1)}, f32[136,128]{1,0:T(8,128)S(1)}, u32[]{:S(2)}, u32[]{:S(2)}) %collective-permute-start.16) | collective-permute-done | bytes 69664 | tf_op jit(solution)/shard_map/ppermute | solution.py:435
  55.6 2.5 %collective-permute-start.17 = (f32[136,128]{1,0:T(8,128)S(1)}, f32[136,128]{1,0:T(8,128)S(1)}, u32[]{:S(2)}, u32[]{:S(2)}) collective-permute-start(f32[136,128]{1,0:T(8,128)S(1)} %add_add_fusion), channel_id=1, source_target_pairs={{0,8},{2,10},{4,12},{6,14},{8,0},{10,2},{12,4},{14,6},{1,9},{3,11}... | collective-permute-start | bytes 208904 | tf_op jit(solution)/shard_map/ppermute | solution.py:438
  58.1 2.8 %collective-permute-done.17 = f32[136,128]{1,0:T(8,128)S(1)} collective-permute-done((f32[136,128]{1,0:T(8,128)S(1)}, f32[136,128]{1,0:T(8,128)S(1)}, u32[]{:S(2)}, u32[]{:S(2)}) %collective-permute-start.17) | collective-permute-done | bytes 69664 | tf_op jit(solution)/shard_map/ppermute | solution.py:438
  61.0 1.2 %collective-permute-done.18.other_ref = f32[136,128]{1,0:T(8,128)S(1)} collective-permute-done((f32[136,128]{1,0:T(8,128)S(1)}, f32[136,128]{1,0:T(8,128)S(1)}, u32[]{:S(2)}, u32[]{:S(2)}) %collective-permute-start.18) | collective-permute-done | bytes 69664 | tf_op jit(solution)/shard_map/ppermute | solution.py:439
  62.2 8.2 %shard_map.38 = f32[512,256]{1,0:T(8,128)} custom-call(s32[1]{0:T(128)} %bitcast.refs_0_.pix_ref, f32[136,128]{1,0:T(8,128)S(1)} %add.25.mine_ref, f32[136,128]{1,0:T(8,128)S(1)} %collective-permute-done.18.other_ref, f32[208,256]{1,0:T(8,128)S(1)} %get-tuple-element.60.refs_0_, f32[208,256]{1,0:T(8,128)S(1)} %get-tuple-element.61.refs_1_, ...), custom_call_target="tpu_custom_call" | custom-call | tf_op jit(solution)/shard_map/pallas_call | solution.py:371
  (22 shorter events, 0.8 us)
Async XLA Ops:
  4.6 3.7 %collective-permute-start = (f32[256,1024]{1,0:T(8,128)S(1)}, f32[256,1024]{1,0:T(8,128)S(1)}, u32[]{:S(2)}, u32[]{:S(2)}) collective-permute-start(f32[256,1024]{1,0:T(8,128)S(1)} %shard_map.28.after_ref.refs_3_), channel_id=1, source_target_pairs={{0,1},{1,0},{2,3},{3,2},{4,5},{5,4},{6,7},{7,6},{8,9},{9,8},{10,11... | collective-permute-start | bytes 3145736 | tf_op jit(solution)/shard_map/ppermute | solution.py:400
  10.0 15.1 %collective-permute-start.5 = (bf16[4,208,256]{2,1,0:T(8,128)(2,1)S(1)}, bf16[4,208,256]{2,1,0:T(8,128)(2,1)S(1)}, u32[]{:S(2)}, u32[]{:S(2)}) collective-permute-start(bf16[4,208,256]{2,1,0:T(8,128)(2,1)S(1)} %bitcast.7), channel_id=1, source_target_pairs={{0,2},{2,0},{4,6},{6,4},{8,10},{10,8},{12,14},{14,12},{1,3},{3,1},... | collective-permute-start | bytes 1277960 | tf_op jit(solution)/shard_map/ppermute | solution.py:406
  12.6 19.8 %collective-permute-start.1 = (bf16[4,208,256]{2,1,0:T(8,128)(2,1)S(1)}, bf16[4,208,256]{2,1,0:T(8,128)(2,1)S(1)}, u32[]{:S(2)}, u32[]{:S(2)}) collective-permute-start(bf16[4,208,256]{2,1,0:T(8,128)(2,1)S(1)} %bitcast.6), channel_id=1, source_target_pairs={{0,2},{2,0},{4,6},{6,4},{8,10},{10,8},{12,14},{14,12},{1,3},{3,1},... | collective-permute-start | bytes 1277960 | tf_op jit(solution)/shard_map/ppermute | solution.py:406
  12.7 8.7 %collective-permute-start.6 = (bf16[192,256]{1,0:T(8,128)(2,1)S(1)}, bf16[192,256]{1,0:T(8,128)(2,1)S(1)}, u32[]{:S(2)}, u32[]{:S(2)}) collective-permute-start(bf16[192,256]{1,0:T(8,128)(2,1)S(1)} %get-tuple-element.47), channel_id=1, source_target_pairs={{0,12},{2,14},{4,8},{6,10},{8,4},{10,6},{12,0},{14,2},{1,13},{3,15... | collective-permute-start | bytes 294920 | tf_op jit(solution)/shard_map/ppermute | solution.py:411
  16.7 8.3 %collective-permute-start.7 = (bf16[192,256]{1,0:T(8,128)(2,1)S(1)}, bf16[192,256]{1,0:T(8,128)(2,1)S(1)}, u32[]{:S(2)}, u32[]{:S(2)}) collective-permute-start(bf16[192,256]{1,0:T(8,128)(2,1)S(1)} %get-tuple-element.48), channel_id=1, source_target_pairs={{0,8},{2,10},{4,12},{6,14},{8,0},{10,2},{12,4},{14,6},{1,9},{3,11}... | collective-permute-start | bytes 294920 | tf_op jit(solution)/shard_map/ppermute | solution.py:411
  16.7 8.3 %collective-permute-start.8 = (bf16[192,256]{1,0:T(8,128)(2,1)S(1)}, bf16[192,256]{1,0:T(8,128)(2,1)S(1)}, u32[]{:S(2)}, u32[]{:S(2)}) collective-permute-start(bf16[192,256]{1,0:T(8,128)(2,1)S(1)} %get-tuple-element.49), channel_id=1, source_target_pairs={{0,4},{2,6},{4,0},{6,2},{8,12},{10,14},{12,8},{14,10},{1,5},{3,7},... | collective-permute-start | bytes 294920 | tf_op jit(solution)/shard_map/ppermute | solution.py:411
  25.7 11.4 %collective-permute-start.10 = (bf16[208,256]{1,0:T(8,128)(2,1)S(1)}, bf16[208,256]{1,0:T(8,128)(2,1)S(1)}, u32[]{:S(2)}, u32[]{:S(2)}) collective-permute-start(bf16[208,256]{1,0:T(8,128)(2,1)S(1)} %get-tuple-element.53), channel_id=1, source_target_pairs={{0,8},{2,10},{4,12},{6,14},{8,0},{10,2},{12,4},{14,6},{1,9},{3,11}... | collective-permute-start | bytes 319496 | tf_op jit(solution)/shard_map/ppermute | solution.py:411
  27.0 10.1 %collective-permute-start.12 = (bf16[96,256]{1,0:T(8,128)(2,1)S(1)}, bf16[96,256]{1,0:T(8,128)(2,1)S(1)}, u32[]{:S(2)}, u32[]{:S(2)}) collective-permute-start(bf16[96,256]{1,0:T(8,128)(2,1)S(1)} %get-tuple-element.55), channel_id=1, source_target_pairs={{0,2},{2,0},{4,6},{6,4},{8,10},{10,8},{12,14},{14,12},{1,3},{3,1},... | collective-permute-start | bytes 147464 | tf_op jit(solution)/shard_map/ppermute | solution.py:418
  28.5 9.7 %collective-permute-start.11 = (bf16[208,256]{1,0:T(8,128)(2,1)S(1)}, bf16[208,256]{1,0:T(8,128)(2,1)S(1)}, u32[]{:S(2)}, u32[]{:S(2)}) collective-permute-start(bf16[208,256]{1,0:T(8,128)(2,1)S(1)} %get-tuple-element.54), channel_id=1, source_target_pairs={{0,4},{2,6},{4,0},{6,2},{8,12},{10,14},{12,8},{14,10},{1,5},{3,7},... | collective-permute-start | bytes 319496 | tf_op jit(solution)/shard_map/ppermute | solution.py:411
  30.4 7.9 %collective-permute-start.9 = (bf16[208,256]{1,0:T(8,128)(2,1)S(1)}, bf16[208,256]{1,0:T(8,128)(2,1)S(1)}, u32[]{:S(2)}, u32[]{:S(2)}) collective-permute-start(bf16[208,256]{1,0:T(8,128)(2,1)S(1)} %get-tuple-element.52), channel_id=1, source_target_pairs={{0,12},{2,14},{4,8},{6,10},{8,4},{10,6},{12,0},{14,2},{1,13},{3,15... | collective-permute-start | bytes 319496 | tf_op jit(solution)/shard_map/ppermute | solution.py:411
  33.0 8.0 %collective-permute-start.2 = (bf16[208,256]{1,0:T(8,128)(2,1)S(1)}, bf16[208,256]{1,0:T(8,128)(2,1)S(1)}, u32[]{:S(2)}, u32[]{:S(2)}) collective-permute-start(bf16[208,256]{1,0:T(8,128)(2,1)S(1)} %get-tuple-element.41), channel_id=1, source_target_pairs={{0,12},{2,14},{4,8},{6,10},{8,4},{10,6},{12,0},{14,2},{1,13},{3,15... | collective-permute-start | bytes 319496 | tf_op jit(solution)/shard_map/ppermute | solution.py:411
  37.1 9.5 %collective-permute-start.3 = (bf16[208,256]{1,0:T(8,128)(2,1)S(1)}, bf16[208,256]{1,0:T(8,128)(2,1)S(1)}, u32[]{:S(2)}, u32[]{:S(2)}) collective-permute-start(bf16[208,256]{1,0:T(8,128)(2,1)S(1)} %get-tuple-element.42), channel_id=1, source_target_pairs={{0,8},{2,10},{4,12},{6,14},{8,0},{10,2},{12,4},{14,6},{1,9},{3,11}... | collective-permute-start | bytes 319496 | tf_op jit(solution)/shard_map/ppermute | solution.py:411
  37.1 9.5 %collective-permute-start.4 = (bf16[208,256]{1,0:T(8,128)(2,1)S(1)}, bf16[208,256]{1,0:T(8,128)(2,1)S(1)}, u32[]{:S(2)}, u32[]{:S(2)}) collective-permute-start(bf16[208,256]{1,0:T(8,128)(2,1)S(1)} %get-tuple-element.43), channel_id=1, source_target_pairs={{0,4},{2,6},{4,0},{6,2},{8,12},{10,14},{12,8},{14,10},{1,5},{3,7},... | collective-permute-start | bytes 319496 | tf_op jit(solution)/shard_map/ppermute | solution.py:411
  47.1 1.3 %collective-permute-start.13 = (f32[136,128]{1,0:T(8,128)S(1)}, f32[136,128]{1,0:T(8,128)S(1)}, u32[]{:S(2)}, u32[]{:S(2)}) collective-permute-start(f32[136,128]{1,0:T(8,128)S(1)} %get-tuple-element.59), channel_id=1, source_target_pairs={{0,1},{1,0},{2,3},{3,2},{4,5},{5,4},{6,7},{7,6},{8,9},{9,8},{10,11... | collective-permute-start | bytes 208904 | tf_op jit(solution)/shard_map/ppermute | solution.py:431
  48.4 4.4 %collective-permute-start.14 = (f32[136,128]{1,0:T(8,128)S(1)}, f32[136,128]{1,0:T(8,128)S(1)}, u32[]{:S(2)}, u32[]{:S(2)}) collective-permute-start(f32[136,128]{1,0:T(8,128)S(1)} %add.21), channel_id=1, source_target_pairs={{0,2},{2,0},{4,6},{6,4},{8,10},{10,8},{12,14},{14,12},{1,3},{3,1},... | collective-permute-start | bytes 208904 | tf_op jit(solution)/shard_map/ppermute | solution.py:435
  50.0 4.7 %collective-permute-start.15 = (f32[136,128]{1,0:T(8,128)S(1)}, f32[136,128]{1,0:T(8,128)S(1)}, u32[]{:S(2)}, u32[]{:S(2)}) collective-permute-start(f32[136,128]{1,0:T(8,128)S(1)} %add.21), channel_id=1, source_target_pairs={{0,4},{2,6},{4,0},{6,2},{8,12},{10,14},{12,8},{14,10},{1,5},{3,7},... | collective-permute-start | bytes 208904 | tf_op jit(solution)/shard_map/ppermute | solution.py:435
  50.0 5.6 %collective-permute-start.16 = (f32[136,128]{1,0:T(8,128)S(1)}, f32[136,128]{1,0:T(8,128)S(1)}, u32[]{:S(2)}, u32[]{:S(2)}) collective-permute-start(f32[136,128]{1,0:T(8,128)S(1)} %add.21), channel_id=1, source_target_pairs={{0,6},{2,4},{4,2},{6,0},{8,14},{10,12},{12,10},{14,8},{1,7},{3,5},... | collective-permute-start | bytes 208904 | tf_op jit(solution)/shard_map/ppermute | solution.py:435
  55.6 5.3 %collective-permute-start.17 = (f32[136,128]{1,0:T(8,128)S(1)}, f32[136,128]{1,0:T(8,128)S(1)}, u32[]{:S(2)}, u32[]{:S(2)}) collective-permute-start(f32[136,128]{1,0:T(8,128)S(1)} %add_add_fusion), channel_id=1, source_target_pairs={{0,8},{2,10},{4,12},{6,14},{8,0},{10,2},{12,4},{14,6},{1,9},{3,11}... | collective-permute-start | bytes 208904 | tf_op jit(solution)/shard_map/ppermute | solution.py:438
  60.9 1.3 %collective-permute-start.18 = (f32[136,128]{1,0:T(8,128)S(1)}, f32[136,128]{1,0:T(8,128)S(1)}, u32[]{:S(2)}, u32[]{:S(2)}) collective-permute-start(f32[136,128]{1,0:T(8,128)S(1)} %add.25.mine_ref), channel_id=1, source_target_pairs={{0,1},{1,0},{2,3},{3,2},{4,5},{5,4},{6,7},{7,6},{8,9},{9,8},{10,11... | collective-permute-start | bytes 208904 | tf_op jit(solution)/shard_map/ppermute | solution.py:439

commit v6 on v5

--- a/solution.py
+++ b/solution.py
@@ -7,7 +7,7 @@
 from jax.experimental.pallas import tpu as pltpu
 from jax.sharding import PartitionSpec as P
 
-SHARES = (13, 13, 6)
+SHARES = (13, 12, 7)
 PIECES = 8
 PANEL = 16
 WINDOW = 32
@@ -196,8 +196,7 @@
     )(mine, *got)
 
 
-def add_kernel(n_after, idx_ref, got_ref, kept_ref, *refs):
-    own_ref, *send_refs = refs[n_after:]
+def add_kernel(idx_ref, got_ref, kept_ref, own_ref, *send_refs):
     me = idx_ref[1]
     own_ref[...] = got_ref[me].astype(F32) + kept_ref[me]
     for d, send in enumerate(send_refs):
@@ -205,11 +204,11 @@
         send[...] = (got_ref[other].astype(F32) + kept_ref[other]).astype(send.dtype)
 
 
-def add_chunk(idx, got, kept, after):
+def add_chunk(idx, got, kept):
     outer, piece, cols = got.shape
     return pl.pallas_call(
-        functools.partial(add_kernel, len(after)),
-        in_specs=[SMEM, VMEM, VMEM] + [pl.BlockSpec(memory_space=pl.ANY)] * len(after),
+        add_kernel,
+        in_specs=[SMEM, VMEM, VMEM],
         out_specs=[VMEM] * outer,
         out_shape=[jax.ShapeDtypeStruct((piece, cols), F32)]
         + [jax.ShapeDtypeStruct((piece, cols), BF16)] * (outer - 1),
@@ -217,7 +216,7 @@
         cost_estimate=pl.CostEstimate(
             flops=outer * piece * cols, bytes_accessed=outer * piece * cols * 8, transcendentals=0
         ),
-    )(idx, got, kept, *after)
+    )(idx, got, kept)
 
 
 def gram_kernel(n, last, *refs):
@@ -419,7 +418,7 @@
     last, gram = gram_chunk(own, [crossed], gram)
     image = []
     for c in range(n):
-        first, *sends = add_chunk(idx, away[c], kept[c], [own] if c == 0 else [])
+        first, *sends = add_chunk(idx, away[c], kept[c])
         arrived = along_z(sends)
         if c < n - 1:
             x, gram = gram_chunk(first, arrived, gram)

time: 70.6 us -> 68.8 us (0.975)
  waiting for transfers between devices: 21.2 us -> 18.3 us
  starting transfers between devices: 24.7 us -> 25.9 us
    ppermute x9, waiting for transfers between devices: 11.6 us -> 6.84 us  [along_z(): lax.ppermute(sends[d - 1], 'bins', xor_pairs(n_bins, 2 * d))]
    ppermute x2, waiting for transfers between devices: 0.67 us -> 3.05 us  [on_device(): lax.ppermute(out.reshape(outer, -1, cols), 'bins', xor_pairs(n_bins, 1))]
  transfers between devices with their start and end apart: 19 -> 19, of which waited for: 10 -> 10; matrix products, arithmetic and copies ran while one was open for 0% -> 0% of each run, Pallas kernels for 13% -> 14%
where the time goes in v6:
time: 68.8 us; the launch traced here: 68.7 us
  starting transfers between devices  25.9 us (38%)
  Pallas kernels  24.2 us (35%)
  waiting for transfers between devices  18.3 us (27%)
    ppermute x9, starting transfers between devices, along_z(): lax.ppermute(sends[d - 1], 'bins', xor_pairs(n_bins, 2 * d))  14.4 us
    pallas_call x1, Pallas kernels, basis_of(): pl.pallas_call(functools.partial(basis_kernel, pixels), in_specs=[SMEM] +...  8.21 us
    ppermute x9, waiting for transfers between devices, along_z(): lax.ppermute(sends[d - 1], 'bins', xor_pairs(n_bins, 2 * d))  6.84 us
    pallas_call x1, Pallas kernels, loadings_terms(): pl.pallas_call(loadings_kernel, in_specs=[HBM, HBM], out_specs=VMEM, out_...  4.61 us
    pallas_call x1, Pallas kernels, image_kept(): pl.pallas_call(functools.partial(kept_kernel, rows, sizes), in_specs=[SME...  4.03 us
    ppermute x3, waiting for transfers between devices, on_device(): lax.ppermute(mine, 'bins', xor_pairs(n_bins, k))  3.65 us
    ppermute x3, starting transfers between devices, on_device(): lax.ppermute(mine, 'bins', xor_pairs(n_bins, k))  3.55 us
    pallas_call x1, Pallas kernels, fetch_blocks(): pl.pallas_call(functools.partial(fetch_kernel, sizes), in_specs=[SMEM, HB...  3.17 us
  transfers between devices with their start and end apart: 19, of which 10 were waited for; matrix products, arithmetic and copies ran while one was open for 0% of the time, Pallas kernels for 14%

profile of v6, /device:TPU:0, one launch (start us, length us, event | category | flops | bytes accessed | tf_op | source)
XLA Modules:
  0.0 68.7 jit_solution(11959914457025037815)
XLA Ops:
  0.0 4.6 %shard_map.28.after_ref.refs_3_ = f32[256,1024]{1,0:T(8,128)S(1)} custom-call(bf16[4096,1024]{1,0:T(8,128)(2,1)} %spectra_hbm.5, bf16[4096,256]{1,0:T(8,128)(2,1)} %probes_hbm.1), custom_call_target="tpu_custom_call" | custom-call | flops 2147483648 | bytes 10485760 | tf_op jit(solution)/shard_map/pallas_call | solution.py:55
  4.6 0.5 collective-permute-start
  5.2 3.2 %shard_map.29 = (bf16[832,1024]{1,0:T(8,128)(2,1)S(1)}, bf16[768,1024]{1,0:T(8,128)(2,1)S(1)}, bf16[896,1024]{1,0:T(8,128)(2,1)S(1)}) custom-call(s32[2]{0:T(128)S(1)} %pad_add_fusion.idx_ref, bf16[4096,1024]{1,0:T(8,128)(2,1)} %spectra_hbm.5, f32[256,1024]{1,0:T(8,128)S(1)} %shard_map.28.after_ref.refs_3_), custom_call_target="tpu_custom_call" | custom-call | bytes 10223616 | tf_op jit(solution)/shard_map/pallas_call | solution.py:104
  8.4 1.6 %shard_map.30 = (bf16[1024,256]{1,0:T(8,128)(2,1)S(1)}, bf16[832,256]{1,0:T(8,128)(2,1)S(1)}, bf16[768,256]{1,0:T(8,128)(2,1)S(1)}, f32[224,256]{1,0:T(8,128)S(1...) custom-call(bf16[832,1024]{1,0:T(8,128)(2,1)S(1)} %get-tuple-element.34.refs_0_, ...), custom_call_target="tpu_custom_call" | custom-call | flops 1308622848 | bytes 2555904 | tf_op jit(solution)/shard_map/pallas_call | solution.py:133
  10.0 2.6 %collective-permute-start.5 = (bf16[4,208,256]{2,1,0:T(8,128)(2,1)S(1)}, bf16[4,208,256]{2,1,0:T(8,128)(2,1)S(1)}, u32[]{:S(2)}, u32[]{:S(2)}) collective-permute-start(bf16[4,208,256]{2,1,0:T(8,128)(2,1)S(1)} %bitcast.6), channel_id=1, source_target_pairs={{0,2},{2,0},{4,6},{6,4},{8,10},{10,8},{12,14},{14,12},{1,3},{3,1},... | collective-permute-start | bytes 1277960 | tf_op jit(solution)/shard_map/ppermute | solution.py:405
  12.7 3.0 %collective-permute-start.10 = (bf16[224,256]{1,0:T(8,128)(2,1)S(1)}, bf16[224,256]{1,0:T(8,128)(2,1)S(1)}, u32[]{:S(2)}, u32[]{:S(2)}) collective-permute-start(bf16[224,256]{1,0:T(8,128)(2,1)S(1)} %get-tuple-element.52), channel_id=1, source_target_pairs={{0,8},{2,10},{4,12},{6,14},{8,0},{10,2},{12,4},{14,6},{1,9},{3,11}... | collective-permute-start | bytes 344072 | tf_op jit(solution)/shard_map/ppermute | solution.py:410
  15.7 1.6 %collective-permute-start.11 = (bf16[224,256]{1,0:T(8,128)(2,1)S(1)}, bf16[224,256]{1,0:T(8,128)(2,1)S(1)}, u32[]{:S(2)}, u32[]{:S(2)}) collective-permute-start(bf16[224,256]{1,0:T(8,128)(2,1)S(1)} %get-tuple-element.53), channel_id=1, source_target_pairs={{0,4},{2,6},{4,0},{6,2},{8,12},{10,14},{12,8},{14,10},{1,5},{3,7},... | collective-permute-start | bytes 344072 | tf_op jit(solution)/shard_map/ppermute | solution.py:410
  17.3 4.0 %shard_map.31 = (f32[4,208,256]{2,1,0:T(8,128)S(1)}, f32[4,192,256]{2,1,0:T(8,128)S(1)}) custom-call(s32[2]{0:T(128)S(1)} %pad_add_fusion.idx_ref, bf16[4096,1024]{1,0:T(8,128)(2,1)} %spectra_hbm.5, bf16[1024,256]{1,0:T(8,128)(2,1)S(1)} %get-tuple-element.38.loadings_ref), custom_call_target="tpu_custom_call" | custom-call | flops 1073741824 | bytes 6291456 | tf_op jit(solution)/shard_map/pallas_call | solution.py:164
  21.4 2.0 %collective-permute-done.5.got_ref = bf16[4,208,256]{2,1,0:T(8,128)(2,1)S(1)} collective-permute-done((bf16[4,208,256]{2,1,0:T(8,128)(2,1)S(1)}, bf16[4,208,256]{2,1,0:T(8,128)(2,1)S(1)}, u32[]{:S(2)}, u32[]{:S(2)}) %collective-permute-start.5) | collective-permute-done | bytes 426016 | tf_op jit(solution)/shard_map/ppermute | solution.py:405
  23.3 0.6 shard_map.33
  23.9 4.1 %collective-permute-start.6 = (bf16[208,256]{1,0:T(8,128)(2,1)S(1)}, bf16[208,256]{1,0:T(8,128)(2,1)S(1)}, u32[]{:S(2)}, u32[]{:S(2)}) collective-permute-start(bf16[208,256]{1,0:T(8,128)(2,1)S(1)} %get-tuple-element.47), channel_id=1, source_target_pairs={{0,12},{2,14},{4,8},{6,10},{8,4},{10,6},{12,0},{14,2},{1,13},{3,15... | collective-permute-start | bytes 319496 | tf_op jit(solution)/shard_map/ppermute | solution.py:410
  28.1 1.6 %collective-permute-start.12 = (bf16[112,256]{1,0:T(8,128)(2,1)S(1)}, bf16[112,256]{1,0:T(8,128)(2,1)S(1)}, u32[]{:S(2)}, u32[]{:S(2)}) collective-permute-start(bf16[112,256]{1,0:T(8,128)(2,1)S(1)} %get-tuple-element.55), channel_id=1, source_target_pairs={{0,2},{2,0},{4,6},{6,4},{8,10},{10,8},{12,14},{14,12},{1,3},{3,1},... | collective-permute-start | bytes 172040 | tf_op jit(solution)/shard_map/ppermute | solution.py:417
  29.7 0.9 %collective-permute-start.7 = (bf16[208,256]{1,0:T(8,128)(2,1)S(1)}, bf16[208,256]{1,0:T(8,128)(2,1)S(1)}, u32[]{:S(2)}, u32[]{:S(2)}) collective-permute-start(bf16[208,256]{1,0:T(8,128)(2,1)S(1)} %get-tuple-element.48), channel_id=1, source_target_pairs={{0,8},{2,10},{4,12},{6,14},{8,0},{10,2},{12,4},{14,6},{1,9},{3,11}... | collective-permute-start | bytes 319496 | tf_op jit(solution)/shard_map/ppermute | solution.py:410
  30.6 1.1 %collective-permute-done.1.got_ref = bf16[4,192,256]{2,1,0:T(8,128)(2,1)S(1)} collective-permute-done((bf16[4,192,256]{2,1,0:T(8,128)(2,1)S(1)}, bf16[4,192,256]{2,1,0:T(8,128)(2,1)S(1)}, u32[]{:S(2)}, u32[]{:S(2)}) %collective-permute-start.1) | collective-permute-done | bytes 393248 | tf_op jit(solution)/shard_map/ppermute | solution.py:405
  31.7 0.6 shard_map.32
  32.4 4.1 %collective-permute-start.2 = (bf16[192,256]{1,0:T(8,128)(2,1)S(1)}, bf16[192,256]{1,0:T(8,128)(2,1)S(1)}, u32[]{:S(2)}, u32[]{:S(2)}) collective-permute-start(bf16[192,256]{1,0:T(8,128)(2,1)S(1)} %get-tuple-element.41), channel_id=1, source_target_pairs={{0,12},{2,14},{4,8},{6,10},{8,4},{10,6},{12,0},{14,2},{1,13},{3,15... | collective-permute-start | bytes 294920 | tf_op jit(solution)/shard_map/ppermute | solution.py:410
  36.5 0.7 collective-permute-start.4
  37.2 0.4 shard_map.35
  37.6 3.1 %collective-permute-done.7.refs_2_ = bf16[208,256]{1,0:T(8,128)(2,1)S(1)} collective-permute-done((bf16[208,256]{1,0:T(8,128)(2,1)S(1)}, bf16[208,256]{1,0:T(8,128)(2,1)S(1)}, u32[]{:S(2)}, u32[]{:S(2)}) %collective-permute-start.7) | collective-permute-done | bytes 106528 | tf_op jit(solution)/shard_map/ppermute | solution.py:410
  40.7 0.4 shard_map.36
  41.2 3.7 %collective-permute-done.3.refs_3_ = bf16[192,256]{1,0:T(8,128)(2,1)S(1)} collective-permute-done((bf16[192,256]{1,0:T(8,128)(2,1)S(1)}, bf16[192,256]{1,0:T(8,128)(2,1)S(1)}, u32[]{:S(2)}, u32[]{:S(2)}) %collective-permute-start.3) | collective-permute-done | bytes 98336 | tf_op jit(solution)/shard_map/ppermute | solution.py:410
  44.9 0.5 shard_map.37
  45.4 1.2 %collective-permute-done.13 = f32[136,128]{1,0:T(8,128)S(1)} collective-permute-done((f32[136,128]{1,0:T(8,128)S(1)}, f32[136,128]{1,0:T(8,128)S(1)}, u32[]{:S(2)}, u32[]{:S(2)}) %collective-permute-start.13) | collective-permute-done | bytes 69664 | tf_op jit(solution)/shard_map/ppermute | solution.py:430
  46.7 1.6 %collective-permute-start.14 = (f32[136,128]{1,0:T(8,128)S(1)}, f32[136,128]{1,0:T(8,128)S(1)}, u32[]{:S(2)}, u32[]{:S(2)}) collective-permute-start(f32[136,128]{1,0:T(8,128)S(1)} %add.21), channel_id=1, source_target_pairs={{0,2},{2,0},{4,6},{6,4},{8,10},{10,8},{12,14},{14,12},{1,3},{3,1},... | collective-permute-start | bytes 208904 | tf_op jit(solution)/shard_map/ppermute | solution.py:434
  48.3 2.0 %collective-permute-start.16 = (f32[136,128]{1,0:T(8,128)S(1)}, f32[136,128]{1,0:T(8,128)S(1)}, u32[]{:S(2)}, u32[]{:S(2)}) collective-permute-start(f32[136,128]{1,0:T(8,128)S(1)} %add.21), channel_id=1, source_target_pairs={{0,6},{2,4},{4,2},{6,0},{8,14},{10,12},{12,10},{14,8},{1,7},{3,5},... | collective-permute-start | bytes 208904 | tf_op jit(solution)/shard_map/ppermute | solution.py:434
  50.2 0.8 %collective-permute-done.14 = f32[136,128]{1,0:T(8,128)S(1)} collective-permute-done((f32[136,128]{1,0:T(8,128)S(1)}, f32[136,128]{1,0:T(8,128)S(1)}, u32[]{:S(2)}, u32[]{:S(2)}) %collective-permute-start.14) | collective-permute-done | bytes 69664 | tf_op jit(solution)/shard_map/ppermute | solution.py:434
  51.0 1.9 %collective-permute-done.15 = f32[136,128]{1,0:T(8,128)S(1)} collective-permute-done((f32[136,128]{1,0:T(8,128)S(1)}, f32[136,128]{1,0:T(8,128)S(1)}, u32[]{:S(2)}, u32[]{:S(2)}) %collective-permute-start.15) | collective-permute-done | bytes 69664 | tf_op jit(solution)/shard_map/ppermute | solution.py:434
  53.0 0.9 %collective-permute-done.16 = f32[136,128]{1,0:T(8,128)S(1)} collective-permute-done((f32[136,128]{1,0:T(8,128)S(1)}, f32[136,128]{1,0:T(8,128)S(1)}, u32[]{:S(2)}, u32[]{:S(2)}) %collective-permute-start.16) | collective-permute-done | bytes 69664 | tf_op jit(solution)/shard_map/ppermute | solution.py:434
  53.9 3.0 %collective-permute-start.17 = (f32[136,128]{1,0:T(8,128)S(1)}, f32[136,128]{1,0:T(8,128)S(1)}, u32[]{:S(2)}, u32[]{:S(2)}) collective-permute-start(f32[136,128]{1,0:T(8,128)S(1)} %add_add_fusion), channel_id=1, source_target_pairs={{0,8},{2,10},{4,12},{6,14},{8,0},{10,2},{12,4},{14,6},{1,9},{3,11}... | collective-permute-start | bytes 208904 | tf_op jit(solution)/shard_map/ppermute | solution.py:437
  56.9 2.3 %collective-permute-done.17 = f32[136,128]{1,0:T(8,128)S(1)} collective-permute-done((f32[136,128]{1,0:T(8,128)S(1)}, f32[136,128]{1,0:T(8,128)S(1)}, u32[]{:S(2)}, u32[]{:S(2)}) %collective-permute-start.17) | collective-permute-done | bytes 69664 | tf_op jit(solution)/shard_map/ppermute | solution.py:437
  59.2 1.2 %collective-permute-done.18.other_ref = f32[136,128]{1,0:T(8,128)S(1)} collective-permute-done((f32[136,128]{1,0:T(8,128)S(1)}, f32[136,128]{1,0:T(8,128)S(1)}, u32[]{:S(2)}, u32[]{:S(2)}) %collective-permute-start.18) | collective-permute-done | bytes 69664 | tf_op jit(solution)/shard_map/ppermute | solution.py:438
  60.5 8.2 %shard_map.38 = f32[512,256]{1,0:T(8,128)} custom-call(s32[1]{0:T(128)} %bitcast.refs_0_.pix_ref, f32[136,128]{1,0:T(8,128)S(1)} %add.25.mine_ref, f32[136,128]{1,0:T(8,128)S(1)} %collective-permute-done.18.other_ref, f32[208,256]{1,0:T(8,128)S(1)} %get-tuple-element.60.refs_0_, f32[192,256]{1,0:T(8,128)S(1)} %get-tuple-element.61.refs_1_, ...), custom_call_target="tpu_custom_call" | custom-call | tf_op jit(solution)/shard_map/pallas_call | solution.py:370
  (22 shorter events, 0.4 us)
Async XLA Ops:
  4.6 3.8 %collective-permute-start = (f32[256,1024]{1,0:T(8,128)S(1)}, f32[256,1024]{1,0:T(8,128)S(1)}, u32[]{:S(2)}, u32[]{:S(2)}) collective-permute-start(f32[256,1024]{1,0:T(8,128)S(1)} %shard_map.28.after_ref.refs_3_), channel_id=1, source_target_pairs={{0,1},{1,0},{2,3},{3,2},{4,5},{5,4},{6,7},{7,6},{8,9},{9,8},{10,11... | collective-permute-start | bytes 3145736 | tf_op jit(solution)/shard_map/ppermute | solution.py:399
  10.0 13.3 %collective-permute-start.5 = (bf16[4,208,256]{2,1,0:T(8,128)(2,1)S(1)}, bf16[4,208,256]{2,1,0:T(8,128)(2,1)S(1)}, u32[]{:S(2)}, u32[]{:S(2)}) collective-permute-start(bf16[4,208,256]{2,1,0:T(8,128)(2,1)S(1)} %bitcast.6), channel_id=1, source_target_pairs={{0,2},{2,0},{4,6},{6,4},{8,10},{10,8},{12,14},{14,12},{1,3},{3,1},... | collective-permute-start | bytes 1277960 | tf_op jit(solution)/shard_map/ppermute | solution.py:405
  12.6 19.1 %collective-permute-start.1 = (bf16[4,192,256]{2,1,0:T(8,128)(2,1)S(1)}, bf16[4,192,256]{2,1,0:T(8,128)(2,1)S(1)}, u32[]{:S(2)}, u32[]{:S(2)}) collective-permute-start(bf16[4,192,256]{2,1,0:T(8,128)(2,1)S(1)} %bitcast.7), channel_id=1, source_target_pairs={{0,2},{2,0},{4,6},{6,4},{8,10},{10,8},{12,14},{14,12},{1,3},{3,1},... | collective-permute-start | bytes 1179656 | tf_op jit(solution)/shard_map/ppermute | solution.py:405
  12.7 15.3 %collective-permute-start.10 = (bf16[224,256]{1,0:T(8,128)(2,1)S(1)}, bf16[224,256]{1,0:T(8,128)(2,1)S(1)}, u32[]{:S(2)}, u32[]{:S(2)}) collective-permute-start(bf16[224,256]{1,0:T(8,128)(2,1)S(1)} %get-tuple-element.52), channel_id=1, source_target_pairs={{0,8},{2,10},{4,12},{6,14},{8,0},{10,2},{12,4},{14,6},{1,9},{3,11}... | collective-permute-start | bytes 344072 | tf_op jit(solution)/shard_map/ppermute | solution.py:410
  15.7 12.3 %collective-permute-start.11 = (bf16[224,256]{1,0:T(8,128)(2,1)S(1)}, bf16[224,256]{1,0:T(8,128)(2,1)S(1)}, u32[]{:S(2)}, u32[]{:S(2)}) collective-permute-start(bf16[224,256]{1,0:T(8,128)(2,1)S(1)} %get-tuple-element.53), channel_id=1, source_target_pairs={{0,4},{2,6},{4,0},{6,2},{8,12},{10,14},{12,8},{14,10},{1,5},{3,7},... | collective-permute-start | bytes 344072 | tf_op jit(solution)/shard_map/ppermute | solution.py:410
  17.3 10.7 %collective-permute-start.9 = (bf16[224,256]{1,0:T(8,128)(2,1)S(1)}, bf16[224,256]{1,0:T(8,128)(2,1)S(1)}, u32[]{:S(2)}, u32[]{:S(2)}) collective-permute-start(bf16[224,256]{1,0:T(8,128)(2,1)S(1)} %get-tuple-element.51), channel_id=1, source_target_pairs={{0,12},{2,14},{4,8},{6,10},{8,4},{10,6},{12,0},{14,2},{1,13},{3,15... | collective-permute-start | bytes 344072 | tf_op jit(solution)/shard_map/ppermute | solution.py:410
  23.9 12.5 %collective-permute-start.6 = (bf16[208,256]{1,0:T(8,128)(2,1)S(1)}, bf16[208,256]{1,0:T(8,128)(2,1)S(1)}, u32[]{:S(2)}, u32[]{:S(2)}) collective-permute-start(bf16[208,256]{1,0:T(8,128)(2,1)S(1)} %get-tuple-element.47), channel_id=1, source_target_pairs={{0,12},{2,14},{4,8},{6,10},{8,4},{10,6},{12,0},{14,2},{1,13},{3,15... | collective-permute-start | bytes 319496 | tf_op jit(solution)/shard_map/ppermute | solution.py:410
  28.1 8.3 %collective-permute-start.12 = (bf16[112,256]{1,0:T(8,128)(2,1)S(1)}, bf16[112,256]{1,0:T(8,128)(2,1)S(1)}, u32[]{:S(2)}, u32[]{:S(2)}) collective-permute-start(bf16[112,256]{1,0:T(8,128)(2,1)S(1)} %get-tuple-element.55), channel_id=1, source_target_pairs={{0,2},{2,0},{4,6},{6,4},{8,10},{10,8},{12,14},{14,12},{1,3},{3,1},... | collective-permute-start | bytes 172040 | tf_op jit(solution)/shard_map/ppermute | solution.py:417
  29.7 11.0 %collective-permute-start.7 = (bf16[208,256]{1,0:T(8,128)(2,1)S(1)}, bf16[208,256]{1,0:T(8,128)(2,1)S(1)}, u32[]{:S(2)}, u32[]{:S(2)}) collective-permute-start(bf16[208,256]{1,0:T(8,128)(2,1)S(1)} %get-tuple-element.48), channel_id=1, source_target_pairs={{0,8},{2,10},{4,12},{6,14},{8,0},{10,2},{12,4},{14,6},{1,9},{3,11}... | collective-permute-start | bytes 319496 | tf_op jit(solution)/shard_map/ppermute | solution.py:410
  30.6 10.1 %collective-permute-start.8 = (bf16[208,256]{1,0:T(8,128)(2,1)S(1)}, bf16[208,256]{1,0:T(8,128)(2,1)S(1)}, u32[]{:S(2)}, u32[]{:S(2)}) collective-permute-start(bf16[208,256]{1,0:T(8,128)(2,1)S(1)} %get-tuple-element.49), channel_id=1, source_target_pairs={{0,4},{2,6},{4,0},{6,2},{8,12},{10,14},{12,8},{14,10},{1,5},{3,7},... | collective-permute-start | bytes 319496 | tf_op jit(solution)/shard_map/ppermute | solution.py:410
  32.4 8.8 %collective-permute-start.2 = (bf16[192,256]{1,0:T(8,128)(2,1)S(1)}, bf16[192,256]{1,0:T(8,128)(2,1)S(1)}, u32[]{:S(2)}, u32[]{:S(2)}) collective-permute-start(bf16[192,256]{1,0:T(8,128)(2,1)S(1)} %get-tuple-element.41), channel_id=1, source_target_pairs={{0,12},{2,14},{4,8},{6,10},{8,4},{10,6},{12,0},{14,2},{1,13},{3,15... | collective-permute-start | bytes 294920 | tf_op jit(solution)/shard_map/ppermute | solution.py:410
  36.5 8.4 %collective-permute-start.3 = (bf16[192,256]{1,0:T(8,128)(2,1)S(1)}, bf16[192,256]{1,0:T(8,128)(2,1)S(1)}, u32[]{:S(2)}, u32[]{:S(2)}) collective-permute-start(bf16[192,256]{1,0:T(8,128)(2,1)S(1)} %get-tuple-element.42), channel_id=1, source_target_pairs={{0,8},{2,10},{4,12},{6,14},{8,0},{10,2},{12,4},{14,6},{1,9},{3,11}... | collective-permute-start | bytes 294920 | tf_op jit(solution)/shard_map/ppermute | solution.py:410
  36.5 8.4 %collective-permute-start.4 = (bf16[192,256]{1,0:T(8,128)(2,1)S(1)}, bf16[192,256]{1,0:T(8,128)(2,1)S(1)}, u32[]{:S(2)}, u32[]{:S(2)}) collective-permute-start(bf16[192,256]{1,0:T(8,128)(2,1)S(1)} %get-tuple-element.43), channel_id=1, source_target_pairs={{0,4},{2,6},{4,0},{6,2},{8,12},{10,14},{12,8},{14,10},{1,5},{3,7},... | collective-permute-start | bytes 294920 | tf_op jit(solution)/shard_map/ppermute | solution.py:410
  45.3 1.3 %collective-permute-start.13 = (f32[136,128]{1,0:T(8,128)S(1)}, f32[136,128]{1,0:T(8,128)S(1)}, u32[]{:S(2)}, u32[]{:S(2)}) collective-permute-start(f32[136,128]{1,0:T(8,128)S(1)} %get-tuple-element.59), channel_id=1, source_target_pairs={{0,1},{1,0},{2,3},{3,2},{4,5},{5,4},{6,7},{7,6},{8,9},{9,8},{10,11... | collective-permute-start | bytes 208904 | tf_op jit(solution)/shard_map/ppermute | solution.py:430
  46.7 4.4 %collective-permute-start.14 = (f32[136,128]{1,0:T(8,128)S(1)}, f32[136,128]{1,0:T(8,128)S(1)}, u32[]{:S(2)}, u32[]{:S(2)}) collective-permute-start(f32[136,128]{1,0:T(8,128)S(1)} %add.21), channel_id=1, source_target_pairs={{0,2},{2,0},{4,6},{6,4},{8,10},{10,8},{12,14},{14,12},{1,3},{3,1},... | collective-permute-start | bytes 208904 | tf_op jit(solution)/shard_map/ppermute | solution.py:434
  48.2 4.7 %collective-permute-start.15 = (f32[136,128]{1,0:T(8,128)S(1)}, f32[136,128]{1,0:T(8,128)S(1)}, u32[]{:S(2)}, u32[]{:S(2)}) collective-permute-start(f32[136,128]{1,0:T(8,128)S(1)} %add.21), channel_id=1, source_target_pairs={{0,4},{2,6},{4,0},{6,2},{8,12},{10,14},{12,8},{14,10},{1,5},{3,7},... | collective-permute-start | bytes 208904 | tf_op jit(solution)/shard_map/ppermute | solution.py:434
  48.3 5.6 %collective-permute-start.16 = (f32[136,128]{1,0:T(8,128)S(1)}, f32[136,128]{1,0:T(8,128)S(1)}, u32[]{:S(2)}, u32[]{:S(2)}) collective-permute-start(f32[136,128]{1,0:T(8,128)S(1)} %add.21), channel_id=1, source_target_pairs={{0,6},{2,4},{4,2},{6,0},{8,14},{10,12},{12,10},{14,8},{1,7},{3,5},... | collective-permute-start | bytes 208904 | tf_op jit(solution)/shard_map/ppermute | solution.py:434
  53.9 5.3 %collective-permute-start.17 = (f32[136,128]{1,0:T(8,128)S(1)}, f32[136,128]{1,0:T(8,128)S(1)}, u32[]{:S(2)}, u32[]{:S(2)}) collective-permute-start(f32[136,128]{1,0:T(8,128)S(1)} %add_add_fusion), channel_id=1, source_target_pairs={{0,8},{2,10},{4,12},{6,14},{8,0},{10,2},{12,4},{14,6},{1,9},{3,11}... | collective-permute-start | bytes 208904 | tf_op jit(solution)/shard_map/ppermute | solution.py:437
  59.2 1.3 %collective-permute-start.18 = (f32[136,128]{1,0:T(8,128)S(1)}, f32[136,128]{1,0:T(8,128)S(1)}, u32[]{:S(2)}, u32[]{:S(2)}) collective-permute-start(f32[136,128]{1,0:T(8,128)S(1)} %add.25.mine_ref), channel_id=1, source_target_pairs={{0,1},{1,0},{2,3},{3,2},{4,5},{5,4},{6,7},{7,6},{8,9},{9,8},{10,11... | collective-permute-start | bytes 208904 | tf_op jit(solution)/shard_map/ppermute | solution.py:438

commit v7 on v6

--- a/solution.py
+++ b/solution.py
@@ -114,7 +114,7 @@
 
 def away_kernel(n, *refs):
     blocks, (mine_ref, got_ref, loadings_ref, *outs) = refs[:n], refs[n:]
-    loadings_ref[...] = (mine_ref[...] + got_ref[...]).T.astype(BF16)
+    loadings_ref[...] = (mine_ref[...] + got_ref[...]).astype(BF16).T
     products = [jnp.dot(x[...], loadings_ref[...], preferred_element_type=F32) for x in blocks]
     for product, out_ref in zip(products[:-1], outs):
         out_ref[...] = product.astype(BF16)
@@ -266,7 +266,7 @@
     )(*[pix] * last, own, *got, gram)
 
 
-def transposed_dot(a, b):
+def stacked_terms(a, b):
     def terms(x):
         high = x.astype(BF16)
         rest = x - high.astype(F32)
@@ -274,10 +274,7 @@
         return high, middle, (rest - middle.astype(F32)).astype(BF16)
 
     (a0, a1, a2), (b0, b1, b2) = terms(a), terms(b)
-    return lax.dot_general(
-        jnp.concatenate([a0, a0, a1, a1, a0, a2], 0), jnp.concatenate([b0, b1, b0, b1, b2, b0], 0),
-        (((0,), (0,)), ((), ())), preferred_element_type=F32,
-    )
+    return jnp.concatenate([a0, a0, a1, a1, a0, a2], 0).T, jnp.concatenate([b0, b1, b0, b1, b2, b0], 0)
 
 
 def wide(column, width):
@@ -324,9 +321,13 @@
         if end < n:
             base = end // 128 * 128
             rest = right[:, base - start:]
-            change = transposed_dot(rest, jnp.concatenate([rest, left], 1))[end - base:]
-            gram[end:n, base:n] -= change[:, :n - base]
-            inverse[end:n, :reach] -= change[:, n - base:]
+            turned, stacked = stacked_terms(rest, jnp.concatenate([rest, left], 1))
+            cuts = [end, min(end + WINDOW, n), n]
+            for low, high in zip(cuts, cuts[1:]):
+                if high > low:
+                    change = jnp.dot(turned[low - base:high - base], stacked, preferred_element_type=F32)
+                    gram[low:high, base:n] -= change[:, :n - base]
+                    inverse[low:high, :reach] -= change[:, n - base:]
 
 
 def basis_kernel(pixels, pix_ref, mine_ref, other_ref, *refs):

time: 68.8 us -> 68.8 us (level)
  no operation moved by 1% of the time
where the time goes in v7:
time: 68.8 us; the launch traced here: 68.7 us
  starting transfers between devices  25.9 us (38%)
  Pallas kernels  24.2 us (35%)
  waiting for transfers between devices  18.3 us (27%)
    ppermute x9, starting transfers between devices, along_z(): lax.ppermute(sends[d - 1], 'bins', xor_pairs(n_bins, 2 * d))  14.4 us
    pallas_call x1, Pallas kernels, basis_of(): pl.pallas_call(functools.partial(basis_kernel, pixels), in_specs=[SMEM] +...  8.15 us
    ppermute x9, waiting for transfers between devices, along_z(): lax.ppermute(sends[d - 1], 'bins', xor_pairs(n_bins, 2 * d))  6.83 us
    pallas_call x1, Pallas kernels, loadings_terms(): pl.pallas_call(loadings_kernel, in_specs=[HBM, HBM], out_specs=VMEM, out_...  4.61 us
    pallas_call x1, Pallas kernels, image_kept(): pl.pallas_call(functools.partial(kept_kernel, rows, sizes), in_specs=[SME...  4.03 us
    ppermute x3, waiting for transfers between devices, on_device(): lax.ppermute(mine, 'bins', xor_pairs(n_bins, k))  3.64 us
    ppermute x3, starting transfers between devices, on_device(): lax.ppermute(mine, 'bins', xor_pairs(n_bins, k))  3.55 us
    pallas_call x1, Pallas kernels, fetch_blocks(): pl.pallas_call(functools.partial(fetch_kernel, sizes), in_specs=[SMEM, HB...  3.17 us
  transfers between devices with their start and end apart: 19, of which 10 were waited for; matrix products, arithmetic and copies ran while one was open for 0% of the time, Pallas kernels for 14%

profile of v7, /device:TPU:0, one launch (start us, length us, event | category | flops | bytes accessed | tf_op | source)
XLA Modules:
  0.0 68.7 jit_solution(17615132315268492233)
XLA Ops:
  0.0 4.6 %shard_map.28.after_ref.refs_3_ = f32[256,1024]{1,0:T(8,128)S(1)} custom-call(bf16[4096,1024]{1,0:T(8,128)(2,1)} %spectra_hbm.5, bf16[4096,256]{1,0:T(8,128)(2,1)} %probes_hbm.1), custom_call_target="tpu_custom_call" | custom-call | flops 2147483648 | bytes 10485760 | tf_op jit(solution)/shard_map/pallas_call | solution.py:55
  4.6 0.5 collective-permute-start
  5.2 3.2 %shard_map.29 = (bf16[832,1024]{1,0:T(8,128)(2,1)S(1)}, bf16[768,1024]{1,0:T(8,128)(2,1)S(1)}, bf16[896,1024]{1,0:T(8,128)(2,1)S(1)}) custom-call(s32[2]{0:T(128)S(1)} %pad_add_fusion.idx_ref, bf16[4096,1024]{1,0:T(8,128)(2,1)} %spectra_hbm.5, f32[256,1024]{1,0:T(8,128)S(1)} %shard_map.28.after_ref.refs_3_), custom_call_target="tpu_custom_call" | custom-call | bytes 10223616 | tf_op jit(solution)/shard_map/pallas_call | solution.py:104
  8.4 1.7 %shard_map.30 = (bf16[1024,256]{1,0:T(8,128)(2,1)S(1)}, bf16[832,256]{1,0:T(8,128)(2,1)S(1)}, bf16[768,256]{1,0:T(8,128)(2,1)S(1)}, f32[224,256]{1,0:T(8,128)S(1...) custom-call(bf16[832,1024]{1,0:T(8,128)(2,1)S(1)} %get-tuple-element.34.refs_0_, ...), custom_call_target="tpu_custom_call" | custom-call | flops 1308622848 | bytes 2555904 | tf_op jit(solution)/shard_map/pallas_call | solution.py:133
  10.1 2.6 %collective-permute-start.5 = (bf16[4,208,256]{2,1,0:T(8,128)(2,1)S(1)}, bf16[4,208,256]{2,1,0:T(8,128)(2,1)S(1)}, u32[]{:S(2)}, u32[]{:S(2)}) collective-permute-start(bf16[4,208,256]{2,1,0:T(8,128)(2,1)S(1)} %bitcast.6), channel_id=1, source_target_pairs={{0,2},{2,0},{4,6},{6,4},{8,10},{10,8},{12,14},{14,12},{1,3},{3,1},... | collective-permute-start | bytes 1277960 | tf_op jit(solution)/shard_map/ppermute | solution.py:406
  12.8 3.0 %collective-permute-start.10 = (bf16[224,256]{1,0:T(8,128)(2,1)S(1)}, bf16[224,256]{1,0:T(8,128)(2,1)S(1)}, u32[]{:S(2)}, u32[]{:S(2)}) collective-permute-start(bf16[224,256]{1,0:T(8,128)(2,1)S(1)} %get-tuple-element.52), channel_id=1, source_target_pairs={{0,8},{2,10},{4,12},{6,14},{8,0},{10,2},{12,4},{14,6},{1,9},{3,11}... | collective-permute-start | bytes 344072 | tf_op jit(solution)/shard_map/ppermute | solution.py:411
  15.8 1.6 %collective-permute-start.11 = (bf16[224,256]{1,0:T(8,128)(2,1)S(1)}, bf16[224,256]{1,0:T(8,128)(2,1)S(1)}, u32[]{:S(2)}, u32[]{:S(2)}) collective-permute-start(bf16[224,256]{1,0:T(8,128)(2,1)S(1)} %get-tuple-element.53), channel_id=1, source_target_pairs={{0,4},{2,6},{4,0},{6,2},{8,12},{10,14},{12,8},{14,10},{1,5},{3,7},... | collective-permute-start | bytes 344072 | tf_op jit(solution)/shard_map/ppermute | solution.py:411
  17.4 4.0 %shard_map.31 = (f32[4,208,256]{2,1,0:T(8,128)S(1)}, f32[4,192,256]{2,1,0:T(8,128)S(1)}) custom-call(s32[2]{0:T(128)S(1)} %pad_add_fusion.idx_ref, bf16[4096,1024]{1,0:T(8,128)(2,1)} %spectra_hbm.5, bf16[1024,256]{1,0:T(8,128)(2,1)S(1)} %get-tuple-element.38.loadings_ref), custom_call_target="tpu_custom_call" | custom-call | flops 1073741824 | bytes 6291456 | tf_op jit(solution)/shard_map/pallas_call | solution.py:164
  21.4 2.0 %collective-permute-done.5.got_ref = bf16[4,208,256]{2,1,0:T(8,128)(2,1)S(1)} collective-permute-done((bf16[4,208,256]{2,1,0:T(8,128)(2,1)S(1)}, bf16[4,208,256]{2,1,0:T(8,128)(2,1)S(1)}, u32[]{:S(2)}, u32[]{:S(2)}) %collective-permute-start.5) | collective-permute-done | bytes 426016 | tf_op jit(solution)/shard_map/ppermute | solution.py:406
  23.3 0.6 shard_map.33
  24.0 4.1 %collective-permute-start.6 = (bf16[208,256]{1,0:T(8,128)(2,1)S(1)}, bf16[208,256]{1,0:T(8,128)(2,1)S(1)}, u32[]{:S(2)}, u32[]{:S(2)}) collective-permute-start(bf16[208,256]{1,0:T(8,128)(2,1)S(1)} %get-tuple-element.47), channel_id=1, source_target_pairs={{0,12},{2,14},{4,8},{6,10},{8,4},{10,6},{12,0},{14,2},{1,13},{3,15... | collective-permute-start | bytes 319496 | tf_op jit(solution)/shard_map/ppermute | solution.py:411
  28.1 1.6 %collective-permute-start.12 = (bf16[112,256]{1,0:T(8,128)(2,1)S(1)}, bf16[112,256]{1,0:T(8,128)(2,1)S(1)}, u32[]{:S(2)}, u32[]{:S(2)}) collective-permute-start(bf16[112,256]{1,0:T(8,128)(2,1)S(1)} %get-tuple-element.55), channel_id=1, source_target_pairs={{0,2},{2,0},{4,6},{6,4},{8,10},{10,8},{12,14},{14,12},{1,3},{3,1},... | collective-permute-start | bytes 172040 | tf_op jit(solution)/shard_map/ppermute | solution.py:418
  29.7 0.9 %collective-permute-start.7 = (bf16[208,256]{1,0:T(8,128)(2,1)S(1)}, bf16[208,256]{1,0:T(8,128)(2,1)S(1)}, u32[]{:S(2)}, u32[]{:S(2)}) collective-permute-start(bf16[208,256]{1,0:T(8,128)(2,1)S(1)} %get-tuple-element.48), channel_id=1, source_target_pairs={{0,8},{2,10},{4,12},{6,14},{8,0},{10,2},{12,4},{14,6},{1,9},{3,11}... | collective-permute-start | bytes 319496 | tf_op jit(solution)/shard_map/ppermute | solution.py:411
  30.7 1.1 %collective-permute-done.1.got_ref = bf16[4,192,256]{2,1,0:T(8,128)(2,1)S(1)} collective-permute-done((bf16[4,192,256]{2,1,0:T(8,128)(2,1)S(1)}, bf16[4,192,256]{2,1,0:T(8,128)(2,1)S(1)}, u32[]{:S(2)}, u32[]{:S(2)}) %collective-permute-start.1) | collective-permute-done | bytes 393248 | tf_op jit(solution)/shard_map/ppermute | solution.py:406
  31.8 0.6 shard_map.32
  32.4 4.1 %collective-permute-start.2 = (bf16[192,256]{1,0:T(8,128)(2,1)S(1)}, bf16[192,256]{1,0:T(8,128)(2,1)S(1)}, u32[]{:S(2)}, u32[]{:S(2)}) collective-permute-start(bf16[192,256]{1,0:T(8,128)(2,1)S(1)} %get-tuple-element.41), channel_id=1, source_target_pairs={{0,12},{2,14},{4,8},{6,10},{8,4},{10,6},{12,0},{14,2},{1,13},{3,15... | collective-permute-start | bytes 294920 | tf_op jit(solution)/shard_map/ppermute | solution.py:411
  36.5 0.7 collective-permute-start.4
  37.2 0.4 shard_map.35
  37.6 3.1 %collective-permute-done.7.refs_2_ = bf16[208,256]{1,0:T(8,128)(2,1)S(1)} collective-permute-done((bf16[208,256]{1,0:T(8,128)(2,1)S(1)}, bf16[208,256]{1,0:T(8,128)(2,1)S(1)}, u32[]{:S(2)}, u32[]{:S(2)}) %collective-permute-start.7) | collective-permute-done | bytes 106528 | tf_op jit(solution)/shard_map/ppermute | solution.py:411
  40.7 0.4 shard_map.36
  41.2 3.7 %collective-permute-done.3.refs_3_ = bf16[192,256]{1,0:T(8,128)(2,1)S(1)} collective-permute-done((bf16[192,256]{1,0:T(8,128)(2,1)S(1)}, bf16[192,256]{1,0:T(8,128)(2,1)S(1)}, u32[]{:S(2)}, u32[]{:S(2)}) %collective-permute-start.3) | collective-permute-done | bytes 98336 | tf_op jit(solution)/shard_map/ppermute | solution.py:411
  44.9 0.5 shard_map.37
  45.4 1.2 %collective-permute-done.13 = f32[136,128]{1,0:T(8,128)S(1)} collective-permute-done((f32[136,128]{1,0:T(8,128)S(1)}, f32[136,128]{1,0:T(8,128)S(1)}, u32[]{:S(2)}, u32[]{:S(2)}) %collective-permute-start.13) | collective-permute-done | bytes 69664 | tf_op jit(solution)/shard_map/ppermute | solution.py:431
  46.7 1.6 %collective-permute-start.14 = (f32[136,128]{1,0:T(8,128)S(1)}, f32[136,128]{1,0:T(8,128)S(1)}, u32[]{:S(2)}, u32[]{:S(2)}) collective-permute-start(f32[136,128]{1,0:T(8,128)S(1)} %add.21), channel_id=1, source_target_pairs={{0,2},{2,0},{4,6},{6,4},{8,10},{10,8},{12,14},{14,12},{1,3},{3,1},... | collective-permute-start | bytes 208904 | tf_op jit(solution)/shard_map/ppermute | solution.py:435
  48.3 2.0 %collective-permute-start.16 = (f32[136,128]{1,0:T(8,128)S(1)}, f32[136,128]{1,0:T(8,128)S(1)}, u32[]{:S(2)}, u32[]{:S(2)}) collective-permute-start(f32[136,128]{1,0:T(8,128)S(1)} %add.21), channel_id=1, source_target_pairs={{0,6},{2,4},{4,2},{6,0},{8,14},{10,12},{12,10},{14,8},{1,7},{3,5},... | collective-permute-start | bytes 208904 | tf_op jit(solution)/shard_map/ppermute | solution.py:435
  50.3 0.8 %collective-permute-done.14 = f32[136,128]{1,0:T(8,128)S(1)} collective-permute-done((f32[136,128]{1,0:T(8,128)S(1)}, f32[136,128]{1,0:T(8,128)S(1)}, u32[]{:S(2)}, u32[]{:S(2)}) %collective-permute-start.14) | collective-permute-done | bytes 69664 | tf_op jit(solution)/shard_map/ppermute | solution.py:435
  51.1 1.9 %collective-permute-done.15 = f32[136,128]{1,0:T(8,128)S(1)} collective-permute-done((f32[136,128]{1,0:T(8,128)S(1)}, f32[136,128]{1,0:T(8,128)S(1)}, u32[]{:S(2)}, u32[]{:S(2)}) %collective-permute-start.15) | collective-permute-done | bytes 69664 | tf_op jit(solution)/shard_map/ppermute | solution.py:435
  53.0 0.9 %collective-permute-done.16 = f32[136,128]{1,0:T(8,128)S(1)} collective-permute-done((f32[136,128]{1,0:T(8,128)S(1)}, f32[136,128]{1,0:T(8,128)S(1)}, u32[]{:S(2)}, u32[]{:S(2)}) %collective-permute-start.16) | collective-permute-done | bytes 69664 | tf_op jit(solution)/shard_map/ppermute | solution.py:435
  53.9 3.0 %collective-permute-start.17 = (f32[136,128]{1,0:T(8,128)S(1)}, f32[136,128]{1,0:T(8,128)S(1)}, u32[]{:S(2)}, u32[]{:S(2)}) collective-permute-start(f32[136,128]{1,0:T(8,128)S(1)} %add_add_fusion), channel_id=1, source_target_pairs={{0,8},{2,10},{4,12},{6,14},{8,0},{10,2},{12,4},{14,6},{1,9},{3,11}... | collective-permute-start | bytes 208904 | tf_op jit(solution)/shard_map/ppermute | solution.py:438
  56.9 2.3 %collective-permute-done.17 = f32[136,128]{1,0:T(8,128)S(1)} collective-permute-done((f32[136,128]{1,0:T(8,128)S(1)}, f32[136,128]{1,0:T(8,128)S(1)}, u32[]{:S(2)}, u32[]{:S(2)}) %collective-permute-start.17) | collective-permute-done | bytes 69664 | tf_op jit(solution)/shard_map/ppermute | solution.py:438
  59.3 1.2 %collective-permute-done.18.other_ref = f32[136,128]{1,0:T(8,128)S(1)} collective-permute-done((f32[136,128]{1,0:T(8,128)S(1)}, f32[136,128]{1,0:T(8,128)S(1)}, u32[]{:S(2)}, u32[]{:S(2)}) %collective-permute-start.18) | collective-permute-done | bytes 69664 | tf_op jit(solution)/shard_map/ppermute | solution.py:439
  60.5 8.1 %shard_map.38 = f32[512,256]{1,0:T(8,128)} custom-call(s32[1]{0:T(128)} %bitcast.refs_0_.pix_ref, f32[136,128]{1,0:T(8,128)S(1)} %add.25.mine_ref, f32[136,128]{1,0:T(8,128)S(1)} %collective-permute-done.18.other_ref, f32[208,256]{1,0:T(8,128)S(1)} %get-tuple-element.60.refs_0_, f32[192,256]{1,0:T(8,128)S(1)} %get-tuple-element.61.refs_1_, ...), custom_call_target="tpu_custom_call" | custom-call | tf_op jit(solution)/shard_map/pallas_call | solution.py:371
  (22 shorter events, 0.4 us)
Async XLA Ops:
  4.6 3.8 %collective-permute-start = (f32[256,1024]{1,0:T(8,128)S(1)}, f32[256,1024]{1,0:T(8,128)S(1)}, u32[]{:S(2)}, u32[]{:S(2)}) collective-permute-start(f32[256,1024]{1,0:T(8,128)S(1)} %shard_map.28.after_ref.refs_3_), channel_id=1, source_target_pairs={{0,1},{1,0},{2,3},{3,2},{4,5},{5,4},{6,7},{7,6},{8,9},{9,8},{10,11... | collective-permute-start | bytes 3145736 | tf_op jit(solution)/shard_map/ppermute | solution.py:400
  10.1 13.3 %collective-permute-start.5 = (bf16[4,208,256]{2,1,0:T(8,128)(2,1)S(1)}, bf16[4,208,256]{2,1,0:T(8,128)(2,1)S(1)}, u32[]{:S(2)}, u32[]{:S(2)}) collective-permute-start(bf16[4,208,256]{2,1,0:T(8,128)(2,1)S(1)} %bitcast.6), channel_id=1, source_target_pairs={{0,2},{2,0},{4,6},{6,4},{8,10},{10,8},{12,14},{14,12},{1,3},{3,1},... | collective-permute-start | bytes 1277960 | tf_op jit(solution)/shard_map/ppermute | solution.py:406
  12.7 19.1 %collective-permute-start.1 = (bf16[4,192,256]{2,1,0:T(8,128)(2,1)S(1)}, bf16[4,192,256]{2,1,0:T(8,128)(2,1)S(1)}, u32[]{:S(2)}, u32[]{:S(2)}) collective-permute-start(bf16[4,192,256]{2,1,0:T(8,128)(2,1)S(1)} %bitcast.7), channel_id=1, source_target_pairs={{0,2},{2,0},{4,6},{6,4},{8,10},{10,8},{12,14},{14,12},{1,3},{3,1},... | collective-permute-start | bytes 1179656 | tf_op jit(solution)/shard_map/ppermute | solution.py:406
  12.8 15.3 %collective-permute-start.10 = (bf16[224,256]{1,0:T(8,128)(2,1)S(1)}, bf16[224,256]{1,0:T(8,128)(2,1)S(1)}, u32[]{:S(2)}, u32[]{:S(2)}) collective-permute-start(bf16[224,256]{1,0:T(8,128)(2,1)S(1)} %get-tuple-element.52), channel_id=1, source_target_pairs={{0,8},{2,10},{4,12},{6,14},{8,0},{10,2},{12,4},{14,6},{1,9},{3,11}... | collective-permute-start | bytes 344072 | tf_op jit(solution)/shard_map/ppermute | solution.py:411
  15.8 12.3 %collective-permute-start.11 = (bf16[224,256]{1,0:T(8,128)(2,1)S(1)}, bf16[224,256]{1,0:T(8,128)(2,1)S(1)}, u32[]{:S(2)}, u32[]{:S(2)}) collective-permute-start(bf16[224,256]{1,0:T(8,128)(2,1)S(1)} %get-tuple-element.53), channel_id=1, source_target_pairs={{0,4},{2,6},{4,0},{6,2},{8,12},{10,14},{12,8},{14,10},{1,5},{3,7},... | collective-permute-start | bytes 344072 | tf_op jit(solution)/shard_map/ppermute | solution.py:411
  17.3 10.7 %collective-permute-start.9 = (bf16[224,256]{1,0:T(8,128)(2,1)S(1)}, bf16[224,256]{1,0:T(8,128)(2,1)S(1)}, u32[]{:S(2)}, u32[]{:S(2)}) collective-permute-start(bf16[224,256]{1,0:T(8,128)(2,1)S(1)} %get-tuple-element.51), channel_id=1, source_target_pairs={{0,12},{2,14},{4,8},{6,10},{8,4},{10,6},{12,0},{14,2},{1,13},{3,15... | collective-permute-start | bytes 344072 | tf_op jit(solution)/shard_map/ppermute | solution.py:411
  24.0 12.5 %collective-permute-start.6 = (bf16[208,256]{1,0:T(8,128)(2,1)S(1)}, bf16[208,256]{1,0:T(8,128)(2,1)S(1)}, u32[]{:S(2)}, u32[]{:S(2)}) collective-permute-start(bf16[208,256]{1,0:T(8,128)(2,1)S(1)} %get-tuple-element.47), channel_id=1, source_target_pairs={{0,12},{2,14},{4,8},{6,10},{8,4},{10,6},{12,0},{14,2},{1,13},{3,15... | collective-permute-start | bytes 319496 | tf_op jit(solution)/shard_map/ppermute | solution.py:411
  28.1 8.3 %collective-permute-start.12 = (bf16[112,256]{1,0:T(8,128)(2,1)S(1)}, bf16[112,256]{1,0:T(8,128)(2,1)S(1)}, u32[]{:S(2)}, u32[]{:S(2)}) collective-permute-start(bf16[112,256]{1,0:T(8,128)(2,1)S(1)} %get-tuple-element.55), channel_id=1, source_target_pairs={{0,2},{2,0},{4,6},{6,4},{8,10},{10,8},{12,14},{14,12},{1,3},{3,1},... | collective-permute-start | bytes 172040 | tf_op jit(solution)/shard_map/ppermute | solution.py:418
  29.7 11.0 %collective-permute-start.7 = (bf16[208,256]{1,0:T(8,128)(2,1)S(1)}, bf16[208,256]{1,0:T(8,128)(2,1)S(1)}, u32[]{:S(2)}, u32[]{:S(2)}) collective-permute-start(bf16[208,256]{1,0:T(8,128)(2,1)S(1)} %get-tuple-element.48), channel_id=1, source_target_pairs={{0,8},{2,10},{4,12},{6,14},{8,0},{10,2},{12,4},{14,6},{1,9},{3,11}... | collective-permute-start | bytes 319496 | tf_op jit(solution)/shard_map/ppermute | solution.py:411
  30.7 10.1 %collective-permute-start.8 = (bf16[208,256]{1,0:T(8,128)(2,1)S(1)}, bf16[208,256]{1,0:T(8,128)(2,1)S(1)}, u32[]{:S(2)}, u32[]{:S(2)}) collective-permute-start(bf16[208,256]{1,0:T(8,128)(2,1)S(1)} %get-tuple-element.49), channel_id=1, source_target_pairs={{0,4},{2,6},{4,0},{6,2},{8,12},{10,14},{12,8},{14,10},{1,5},{3,7},... | collective-permute-start | bytes 319496 | tf_op jit(solution)/shard_map/ppermute | solution.py:411
  32.4 8.8 %collective-permute-start.2 = (bf16[192,256]{1,0:T(8,128)(2,1)S(1)}, bf16[192,256]{1,0:T(8,128)(2,1)S(1)}, u32[]{:S(2)}, u32[]{:S(2)}) collective-permute-start(bf16[192,256]{1,0:T(8,128)(2,1)S(1)} %get-tuple-element.41), channel_id=1, source_target_pairs={{0,12},{2,14},{4,8},{6,10},{8,4},{10,6},{12,0},{14,2},{1,13},{3,15... | collective-permute-start | bytes 294920 | tf_op jit(solution)/shard_map/ppermute | solution.py:411
  36.5 8.4 %collective-permute-start.3 = (bf16[192,256]{1,0:T(8,128)(2,1)S(1)}, bf16[192,256]{1,0:T(8,128)(2,1)S(1)}, u32[]{:S(2)}, u32[]{:S(2)}) collective-permute-start(bf16[192,256]{1,0:T(8,128)(2,1)S(1)} %get-tuple-element.42), channel_id=1, source_target_pairs={{0,8},{2,10},{4,12},{6,14},{8,0},{10,2},{12,4},{14,6},{1,9},{3,11}... | collective-permute-start | bytes 294920 | tf_op jit(solution)/shard_map/ppermute | solution.py:411
  36.5 8.4 %collective-permute-start.4 = (bf16[192,256]{1,0:T(8,128)(2,1)S(1)}, bf16[192,256]{1,0:T(8,128)(2,1)S(1)}, u32[]{:S(2)}, u32[]{:S(2)}) collective-permute-start(bf16[192,256]{1,0:T(8,128)(2,1)S(1)} %get-tuple-element.43), channel_id=1, source_target_pairs={{0,4},{2,6},{4,0},{6,2},{8,12},{10,14},{12,8},{14,10},{1,5},{3,7},... | collective-permute-start | bytes 294920 | tf_op jit(solution)/shard_map/ppermute | solution.py:411
  45.4 1.3 %collective-permute-start.13 = (f32[136,128]{1,0:T(8,128)S(1)}, f32[136,128]{1,0:T(8,128)S(1)}, u32[]{:S(2)}, u32[]{:S(2)}) collective-permute-start(f32[136,128]{1,0:T(8,128)S(1)} %get-tuple-element.59), channel_id=1, source_target_pairs={{0,1},{1,0},{2,3},{3,2},{4,5},{5,4},{6,7},{7,6},{8,9},{9,8},{10,11... | collective-permute-start | bytes 208904 | tf_op jit(solution)/shard_map/ppermute | solution.py:431
  46.7 4.4 %collective-permute-start.14 = (f32[136,128]{1,0:T(8,128)S(1)}, f32[136,128]{1,0:T(8,128)S(1)}, u32[]{:S(2)}, u32[]{:S(2)}) collective-permute-start(f32[136,128]{1,0:T(8,128)S(1)} %add.21), channel_id=1, source_target_pairs={{0,2},{2,0},{4,6},{6,4},{8,10},{10,8},{12,14},{14,12},{1,3},{3,1},... | collective-permute-start | bytes 208904 | tf_op jit(solution)/shard_map/ppermute | solution.py:435
  48.3 4.7 %collective-permute-start.15 = (f32[136,128]{1,0:T(8,128)S(1)}, f32[136,128]{1,0:T(8,128)S(1)}, u32[]{:S(2)}, u32[]{:S(2)}) collective-permute-start(f32[136,128]{1,0:T(8,128)S(1)} %add.21), channel_id=1, source_target_pairs={{0,4},{2,6},{4,0},{6,2},{8,12},{10,14},{12,8},{14,10},{1,5},{3,7},... | collective-permute-start | bytes 208904 | tf_op jit(solution)/shard_map/ppermute | solution.py:435
  48.3 5.6 %collective-permute-start.16 = (f32[136,128]{1,0:T(8,128)S(1)}, f32[136,128]{1,0:T(8,128)S(1)}, u32[]{:S(2)}, u32[]{:S(2)}) collective-permute-start(f32[136,128]{1,0:T(8,128)S(1)} %add.21), channel_id=1, source_target_pairs={{0,6},{2,4},{4,2},{6,0},{8,14},{10,12},{12,10},{14,8},{1,7},{3,5},... | collective-permute-start | bytes 208904 | tf_op jit(solution)/shard_map/ppermute | solution.py:435
  53.9 5.3 %collective-permute-start.17 = (f32[136,128]{1,0:T(8,128)S(1)}, f32[136,128]{1,0:T(8,128)S(1)}, u32[]{:S(2)}, u32[]{:S(2)}) collective-permute-start(f32[136,128]{1,0:T(8,128)S(1)} %add_add_fusion), channel_id=1, source_target_pairs={{0,8},{2,10},{4,12},{6,14},{8,0},{10,2},{12,4},{14,6},{1,9},{3,11}... | collective-permute-start | bytes 208904 | tf_op jit(solution)/shard_map/ppermute | solution.py:438
  59.2 1.3 %collective-permute-start.18 = (f32[136,128]{1,0:T(8,128)S(1)}, f32[136,128]{1,0:T(8,128)S(1)}, u32[]{:S(2)}, u32[]{:S(2)}) collective-permute-start(f32[136,128]{1,0:T(8,128)S(1)} %add.25.mine_ref), channel_id=1, source_target_pairs={{0,1},{1,0},{2,3},{3,2},{4,5},{5,4},{6,7},{7,6},{8,9},{9,8},{10,11... | collective-permute-start | bytes 208904 | tf_op jit(solution)/shard_map/ppermute | solution.py:439

commit v8 on v7

--- a/solution.py
+++ b/solution.py
@@ -227,9 +227,7 @@
     for g in got:
         x = x + g[...].astype(F32)
     x_ref[...] = x
-    gram = gram_in[...] + lax.dot_general(
-        x, x, (((0,), (0,)), ((), ())), precision=lax.Precision.HIGHEST, preferred_element_type=F32
-    )
+    gram = gram_in[...] + jnp.dot(*stacked_terms(x, x), preferred_element_type=F32)
     if not last:
         out[0][...] = gram
         return

time: 68.8 us -> 68.8 us (level)
  transfers between devices with their start and end apart: 19 -> 19, of which waited for: 10 -> 10; matrix products, arithmetic and copies ran while one was open for 0% -> 0% of each run, Pallas kernels for 14% -> 13%
where the time goes in v8:
time: 68.8 us; the launch traced here: 68.6 us
  starting transfers between devices  25.9 us (38%)
  Pallas kernels  24.1 us (35%)
  waiting for transfers between devices  18.4 us (27%)
    ppermute x9, starting transfers between devices, along_z(): lax.ppermute(sends[d - 1], 'bins', xor_pairs(n_bins, 2 * d))  14.4 us
    pallas_call x1, Pallas kernels, basis_of(): pl.pallas_call(functools.partial(basis_kernel, pixels), in_specs=[SMEM] +...  8.15 us
    ppermute x9, waiting for transfers between devices, along_z(): lax.ppermute(sends[d - 1], 'bins', xor_pairs(n_bins, 2 * d))  6.95 us
    pallas_call x1, Pallas kernels, loadings_terms(): pl.pallas_call(loadings_kernel, in_specs=[HBM, HBM], out_specs=VMEM, out_...  4.61 us
    pallas_call x1, Pallas kernels, image_kept(): pl.pallas_call(functools.partial(kept_kernel, rows, sizes), in_specs=[SME...  4.03 us
    ppermute x3, waiting for transfers between devices, on_device(): lax.ppermute(mine, 'bins', xor_pairs(n_bins, k))  3.64 us
    ppermute x3, starting transfers between devices, on_device(): lax.ppermute(mine, 'bins', xor_pairs(n_bins, k))  3.55 us
    pallas_call x1, Pallas kernels, fetch_blocks(): pl.pallas_call(functools.partial(fetch_kernel, sizes), in_specs=[SMEM, HB...  3.17 us
  transfers between devices with their start and end apart: 19, of which 10 were waited for; matrix products, arithmetic and copies ran while one was open for 0% of the time, Pallas kernels for 13%

profile of v8, /device:TPU:0, one launch (start us, length us, event | category | flops | bytes accessed | tf_op | source)
XLA Modules:
  0.0 68.6 jit_solution(11230908188101181105)
XLA Ops:
  0.0 4.6 %shard_map.28.after_ref.refs_3_ = f32[256,1024]{1,0:T(8,128)S(1)} custom-call(bf16[4096,1024]{1,0:T(8,128)(2,1)} %spectra_hbm.5, bf16[4096,256]{1,0:T(8,128)(2,1)} %probes_hbm.1), custom_call_target="tpu_custom_call" | custom-call | flops 2147483648 | bytes 10485760 | tf_op jit(solution)/shard_map/pallas_call | solution.py:55
  4.6 0.5 collective-permute-start
  5.2 3.2 %shard_map.29 = (bf16[832,1024]{1,0:T(8,128)(2,1)S(1)}, bf16[768,1024]{1,0:T(8,128)(2,1)S(1)}, bf16[896,1024]{1,0:T(8,128)(2,1)S(1)}) custom-call(s32[2]{0:T(128)S(1)} %pad_add_fusion.idx_ref, bf16[4096,1024]{1,0:T(8,128)(2,1)} %spectra_hbm.5, f32[256,1024]{1,0:T(8,128)S(1)} %shard_map.28.after_ref.refs_3_), custom_call_target="tpu_custom_call" | custom-call | bytes 10223616 | tf_op jit(solution)/shard_map/pallas_call | solution.py:104
  8.4 1.7 %shard_map.30 = (bf16[1024,256]{1,0:T(8,128)(2,1)S(1)}, bf16[832,256]{1,0:T(8,128)(2,1)S(1)}, bf16[768,256]{1,0:T(8,128)(2,1)S(1)}, f32[224,256]{1,0:T(8,128)S(1...) custom-call(bf16[832,1024]{1,0:T(8,128)(2,1)S(1)} %get-tuple-element.34.refs_0_, ...), custom_call_target="tpu_custom_call" | custom-call | flops 1308622848 | bytes 2555904 | tf_op jit(solution)/shard_map/pallas_call | solution.py:133
  10.1 2.6 %collective-permute-start.5 = (bf16[4,208,256]{2,1,0:T(8,128)(2,1)S(1)}, bf16[4,208,256]{2,1,0:T(8,128)(2,1)S(1)}, u32[]{:S(2)}, u32[]{:S(2)}) collective-permute-start(bf16[4,208,256]{2,1,0:T(8,128)(2,1)S(1)} %bitcast.6), channel_id=1, source_target_pairs={{0,2},{2,0},{4,6},{6,4},{8,10},{10,8},{12,14},{14,12},{1,3},{3,1},... | collective-permute-start | bytes 1277960 | tf_op jit(solution)/shard_map/ppermute | solution.py:404
  12.8 3.0 %collective-permute-start.10 = (bf16[224,256]{1,0:T(8,128)(2,1)S(1)}, bf16[224,256]{1,0:T(8,128)(2,1)S(1)}, u32[]{:S(2)}, u32[]{:S(2)}) collective-permute-start(bf16[224,256]{1,0:T(8,128)(2,1)S(1)} %get-tuple-element.52), channel_id=1, source_target_pairs={{0,8},{2,10},{4,12},{6,14},{8,0},{10,2},{12,4},{14,6},{1,9},{3,11}... | collective-permute-start | bytes 344072 | tf_op jit(solution)/shard_map/ppermute | solution.py:409
  15.8 1.6 %collective-permute-start.11 = (bf16[224,256]{1,0:T(8,128)(2,1)S(1)}, bf16[224,256]{1,0:T(8,128)(2,1)S(1)}, u32[]{:S(2)}, u32[]{:S(2)}) collective-permute-start(bf16[224,256]{1,0:T(8,128)(2,1)S(1)} %get-tuple-element.53), channel_id=1, source_target_pairs={{0,4},{2,6},{4,0},{6,2},{8,12},{10,14},{12,8},{14,10},{1,5},{3,7},... | collective-permute-start | bytes 344072 | tf_op jit(solution)/shard_map/ppermute | solution.py:409
  17.4 4.0 %shard_map.31 = (f32[4,208,256]{2,1,0:T(8,128)S(1)}, f32[4,192,256]{2,1,0:T(8,128)S(1)}) custom-call(s32[2]{0:T(128)S(1)} %pad_add_fusion.idx_ref, bf16[4096,1024]{1,0:T(8,128)(2,1)} %spectra_hbm.5, bf16[1024,256]{1,0:T(8,128)(2,1)S(1)} %get-tuple-element.38.loadings_ref), custom_call_target="tpu_custom_call" | custom-call | flops 1073741824 | bytes 6291456 | tf_op jit(solution)/shard_map/pallas_call | solution.py:164
  21.4 2.0 %collective-permute-done.5.got_ref = bf16[4,208,256]{2,1,0:T(8,128)(2,1)S(1)} collective-permute-done((bf16[4,208,256]{2,1,0:T(8,128)(2,1)S(1)}, bf16[4,208,256]{2,1,0:T(8,128)(2,1)S(1)}, u32[]{:S(2)}, u32[]{:S(2)}) %collective-permute-start.5) | collective-permute-done | bytes 426016 | tf_op jit(solution)/shard_map/ppermute | solution.py:404
  23.3 0.6 shard_map.33
  24.0 4.1 %collective-permute-start.6 = (bf16[208,256]{1,0:T(8,128)(2,1)S(1)}, bf16[208,256]{1,0:T(8,128)(2,1)S(1)}, u32[]{:S(2)}, u32[]{:S(2)}) collective-permute-start(bf16[208,256]{1,0:T(8,128)(2,1)S(1)} %get-tuple-element.47), channel_id=1, source_target_pairs={{0,12},{2,14},{4,8},{6,10},{8,4},{10,6},{12,0},{14,2},{1,13},{3,15... | collective-permute-start | bytes 319496 | tf_op jit(solution)/shard_map/ppermute | solution.py:409
  28.1 1.6 %collective-permute-start.12 = (bf16[112,256]{1,0:T(8,128)(2,1)S(1)}, bf16[112,256]{1,0:T(8,128)(2,1)S(1)}, u32[]{:S(2)}, u32[]{:S(2)}) collective-permute-start(bf16[112,256]{1,0:T(8,128)(2,1)S(1)} %get-tuple-element.55), channel_id=1, source_target_pairs={{0,2},{2,0},{4,6},{6,4},{8,10},{10,8},{12,14},{14,12},{1,3},{3,1},... | collective-permute-start | bytes 172040 | tf_op jit(solution)/shard_map/ppermute | solution.py:416
  29.7 0.9 %collective-permute-start.7 = (bf16[208,256]{1,0:T(8,128)(2,1)S(1)}, bf16[208,256]{1,0:T(8,128)(2,1)S(1)}, u32[]{:S(2)}, u32[]{:S(2)}) collective-permute-start(bf16[208,256]{1,0:T(8,128)(2,1)S(1)} %get-tuple-element.48), channel_id=1, source_target_pairs={{0,8},{2,10},{4,12},{6,14},{8,0},{10,2},{12,4},{14,6},{1,9},{3,11}... | collective-permute-start | bytes 319496 | tf_op jit(solution)/shard_map/ppermute | solution.py:409
  30.7 1.1 %collective-permute-done.1.got_ref = bf16[4,192,256]{2,1,0:T(8,128)(2,1)S(1)} collective-permute-done((bf16[4,192,256]{2,1,0:T(8,128)(2,1)S(1)}, bf16[4,192,256]{2,1,0:T(8,128)(2,1)S(1)}, u32[]{:S(2)}, u32[]{:S(2)}) %collective-permute-start.1) | collective-permute-done | bytes 393248 | tf_op jit(solution)/shard_map/ppermute | solution.py:404
  31.8 0.6 shard_map.32
  32.4 4.1 %collective-permute-start.2 = (bf16[192,256]{1,0:T(8,128)(2,1)S(1)}, bf16[192,256]{1,0:T(8,128)(2,1)S(1)}, u32[]{:S(2)}, u32[]{:S(2)}) collective-permute-start(bf16[192,256]{1,0:T(8,128)(2,1)S(1)} %get-tuple-element.41), channel_id=1, source_target_pairs={{0,12},{2,14},{4,8},{6,10},{8,4},{10,6},{12,0},{14,2},{1,13},{3,15... | collective-permute-start | bytes 294920 | tf_op jit(solution)/shard_map/ppermute | solution.py:409
  36.5 0.7 collective-permute-start.4
  37.2 0.3 shard_map.35
  37.5 3.2 %collective-permute-done.7.refs_2_ = bf16[208,256]{1,0:T(8,128)(2,1)S(1)} collective-permute-done((bf16[208,256]{1,0:T(8,128)(2,1)S(1)}, bf16[208,256]{1,0:T(8,128)(2,1)S(1)}, u32[]{:S(2)}, u32[]{:S(2)}) %collective-permute-start.7) | collective-permute-done | bytes 106528 | tf_op jit(solution)/shard_map/ppermute | solution.py:409
  40.7 0.4 shard_map.36
  41.2 3.7 %collective-permute-done.3.refs_3_ = bf16[192,256]{1,0:T(8,128)(2,1)S(1)} collective-permute-done((bf16[192,256]{1,0:T(8,128)(2,1)S(1)}, bf16[192,256]{1,0:T(8,128)(2,1)S(1)}, u32[]{:S(2)}, u32[]{:S(2)}) %collective-permute-start.3) | collective-permute-done | bytes 98336 | tf_op jit(solution)/shard_map/ppermute | solution.py:409
  44.9 0.4 shard_map.37
  45.4 1.2 %collective-permute-done.13 = f32[136,128]{1,0:T(8,128)S(1)} collective-permute-done((f32[136,128]{1,0:T(8,128)S(1)}, f32[136,128]{1,0:T(8,128)S(1)}, u32[]{:S(2)}, u32[]{:S(2)}) %collective-permute-start.13) | collective-permute-done | bytes 69664 | tf_op jit(solution)/shard_map/ppermute | solution.py:429
  46.6 1.6 %collective-permute-start.14 = (f32[136,128]{1,0:T(8,128)S(1)}, f32[136,128]{1,0:T(8,128)S(1)}, u32[]{:S(2)}, u32[]{:S(2)}) collective-permute-start(f32[136,128]{1,0:T(8,128)S(1)} %add.21), channel_id=1, source_target_pairs={{0,2},{2,0},{4,6},{6,4},{8,10},{10,8},{12,14},{14,12},{1,3},{3,1},... | collective-permute-start | bytes 208904 | tf_op jit(solution)/shard_map/ppermute | solution.py:433
  48.2 2.0 %collective-permute-start.16 = (f32[136,128]{1,0:T(8,128)S(1)}, f32[136,128]{1,0:T(8,128)S(1)}, u32[]{:S(2)}, u32[]{:S(2)}) collective-permute-start(f32[136,128]{1,0:T(8,128)S(1)} %add.21), channel_id=1, source_target_pairs={{0,6},{2,4},{4,2},{6,0},{8,14},{10,12},{12,10},{14,8},{1,7},{3,5},... | collective-permute-start | bytes 208904 | tf_op jit(solution)/shard_map/ppermute | solution.py:433
  50.2 0.8 %collective-permute-done.14 = f32[136,128]{1,0:T(8,128)S(1)} collective-permute-done((f32[136,128]{1,0:T(8,128)S(1)}, f32[136,128]{1,0:T(8,128)S(1)}, u32[]{:S(2)}, u32[]{:S(2)}) %collective-permute-start.14) | collective-permute-done | bytes 69664 | tf_op jit(solution)/shard_map/ppermute | solution.py:433
  51.0 1.9 %collective-permute-done.15 = f32[136,128]{1,0:T(8,128)S(1)} collective-permute-done((f32[136,128]{1,0:T(8,128)S(1)}, f32[136,128]{1,0:T(8,128)S(1)}, u32[]{:S(2)}, u32[]{:S(2)}) %collective-permute-start.15) | collective-permute-done | bytes 69664 | tf_op jit(solution)/shard_map/ppermute | solution.py:433
  52.9 0.9 %collective-permute-done.16 = f32[136,128]{1,0:T(8,128)S(1)} collective-permute-done((f32[136,128]{1,0:T(8,128)S(1)}, f32[136,128]{1,0:T(8,128)S(1)}, u32[]{:S(2)}, u32[]{:S(2)}) %collective-permute-start.16) | collective-permute-done | bytes 69664 | tf_op jit(solution)/shard_map/ppermute | solution.py:433
  53.9 3.0 %collective-permute-start.17 = (f32[136,128]{1,0:T(8,128)S(1)}, f32[136,128]{1,0:T(8,128)S(1)}, u32[]{:S(2)}, u32[]{:S(2)}) collective-permute-start(f32[136,128]{1,0:T(8,128)S(1)} %add_add_fusion), channel_id=1, source_target_pairs={{0,8},{2,10},{4,12},{6,14},{8,0},{10,2},{12,4},{14,6},{1,9},{3,11}... | collective-permute-start | bytes 208904 | tf_op jit(solution)/shard_map/ppermute | solution.py:436
  56.8 2.3 %collective-permute-done.17 = f32[136,128]{1,0:T(8,128)S(1)} collective-permute-done((f32[136,128]{1,0:T(8,128)S(1)}, f32[136,128]{1,0:T(8,128)S(1)}, u32[]{:S(2)}, u32[]{:S(2)}) %collective-permute-start.17) | collective-permute-done | bytes 69664 | tf_op jit(solution)/shard_map/ppermute | solution.py:436
  59.2 1.2 %collective-permute-done.18.other_ref = f32[136,128]{1,0:T(8,128)S(1)} collective-permute-done((f32[136,128]{1,0:T(8,128)S(1)}, f32[136,128]{1,0:T(8,128)S(1)}, u32[]{:S(2)}, u32[]{:S(2)}) %collective-permute-start.18) | collective-permute-done | bytes 69664 | tf_op jit(solution)/shard_map/ppermute | solution.py:437
  60.5 8.2 %shard_map.38 = f32[512,256]{1,0:T(8,128)} custom-call(s32[1]{0:T(128)} %bitcast.refs_0_.pix_ref, f32[136,128]{1,0:T(8,128)S(1)} %add.25.mine_ref, f32[136,128]{1,0:T(8,128)S(1)} %collective-permute-done.18.other_ref, f32[208,256]{1,0:T(8,128)S(1)} %get-tuple-element.60.refs_0_, f32[192,256]{1,0:T(8,128)S(1)} %get-tuple-element.61.refs_1_, ...), custom_call_target="tpu_custom_call" | custom-call | tf_op jit(solution)/shard_map/pallas_call | solution.py:369
  (22 shorter events, 0.4 us)
Async XLA Ops:
  4.6 3.8 %collective-permute-start = (f32[256,1024]{1,0:T(8,128)S(1)}, f32[256,1024]{1,0:T(8,128)S(1)}, u32[]{:S(2)}, u32[]{:S(2)}) collective-permute-start(f32[256,1024]{1,0:T(8,128)S(1)} %shard_map.28.after_ref.refs_3_), channel_id=1, source_target_pairs={{0,1},{1,0},{2,3},{3,2},{4,5},{5,4},{6,7},{7,6},{8,9},{9,8},{10,11... | collective-permute-start | bytes 3145736 | tf_op jit(solution)/shard_map/ppermute | solution.py:398
  10.1 13.3 %collective-permute-start.5 = (bf16[4,208,256]{2,1,0:T(8,128)(2,1)S(1)}, bf16[4,208,256]{2,1,0:T(8,128)(2,1)S(1)}, u32[]{:S(2)}, u32[]{:S(2)}) collective-permute-start(bf16[4,208,256]{2,1,0:T(8,128)(2,1)S(1)} %bitcast.6), channel_id=1, source_target_pairs={{0,2},{2,0},{4,6},{6,4},{8,10},{10,8},{12,14},{14,12},{1,3},{3,1},... | collective-permute-start | bytes 1277960 | tf_op jit(solution)/shard_map/ppermute | solution.py:404
  12.7 19.1 %collective-permute-start.1 = (bf16[4,192,256]{2,1,0:T(8,128)(2,1)S(1)}, bf16[4,192,256]{2,1,0:T(8,128)(2,1)S(1)}, u32[]{:S(2)}, u32[]{:S(2)}) collective-permute-start(bf16[4,192,256]{2,1,0:T(8,128)(2,1)S(1)} %bitcast.7), channel_id=1, source_target_pairs={{0,2},{2,0},{4,6},{6,4},{8,10},{10,8},{12,14},{14,12},{1,3},{3,1},... | collective-permute-start | bytes 1179656 | tf_op jit(solution)/shard_map/ppermute | solution.py:404
  12.8 15.3 %collective-permute-start.10 = (bf16[224,256]{1,0:T(8,128)(2,1)S(1)}, bf16[224,256]{1,0:T(8,128)(2,1)S(1)}, u32[]{:S(2)}, u32[]{:S(2)}) collective-permute-start(bf16[224,256]{1,0:T(8,128)(2,1)S(1)} %get-tuple-element.52), channel_id=1, source_target_pairs={{0,8},{2,10},{4,12},{6,14},{8,0},{10,2},{12,4},{14,6},{1,9},{3,11}... | collective-permute-start | bytes 344072 | tf_op jit(solution)/shard_map/ppermute | solution.py:409
  15.8 12.3 %collective-permute-start.11 = (bf16[224,256]{1,0:T(8,128)(2,1)S(1)}, bf16[224,256]{1,0:T(8,128)(2,1)S(1)}, u32[]{:S(2)}, u32[]{:S(2)}) collective-permute-start(bf16[224,256]{1,0:T(8,128)(2,1)S(1)} %get-tuple-element.53), channel_id=1, source_target_pairs={{0,4},{2,6},{4,0},{6,2},{8,12},{10,14},{12,8},{14,10},{1,5},{3,7},... | collective-permute-start | bytes 344072 | tf_op jit(solution)/shard_map/ppermute | solution.py:409
  17.3 10.7 %collective-permute-start.9 = (bf16[224,256]{1,0:T(8,128)(2,1)S(1)}, bf16[224,256]{1,0:T(8,128)(2,1)S(1)}, u32[]{:S(2)}, u32[]{:S(2)}) collective-permute-start(bf16[224,256]{1,0:T(8,128)(2,1)S(1)} %get-tuple-element.51), channel_id=1, source_target_pairs={{0,12},{2,14},{4,8},{6,10},{8,4},{10,6},{12,0},{14,2},{1,13},{3,15... | collective-permute-start | bytes 344072 | tf_op jit(solution)/shard_map/ppermute | solution.py:409
  24.0 12.5 %collective-permute-start.6 = (bf16[208,256]{1,0:T(8,128)(2,1)S(1)}, bf16[208,256]{1,0:T(8,128)(2,1)S(1)}, u32[]{:S(2)}, u32[]{:S(2)}) collective-permute-start(bf16[208,256]{1,0:T(8,128)(2,1)S(1)} %get-tuple-element.47), channel_id=1, source_target_pairs={{0,12},{2,14},{4,8},{6,10},{8,4},{10,6},{12,0},{14,2},{1,13},{3,15... | collective-permute-start | bytes 319496 | tf_op jit(solution)/shard_map/ppermute | solution.py:409
  28.1 8.3 %collective-permute-start.12 = (bf16[112,256]{1,0:T(8,128)(2,1)S(1)}, bf16[112,256]{1,0:T(8,128)(2,1)S(1)}, u32[]{:S(2)}, u32[]{:S(2)}) collective-permute-start(bf16[112,256]{1,0:T(8,128)(2,1)S(1)} %get-tuple-element.55), channel_id=1, source_target_pairs={{0,2},{2,0},{4,6},{6,4},{8,10},{10,8},{12,14},{14,12},{1,3},{3,1},... | collective-permute-start | bytes 172040 | tf_op jit(solution)/shard_map/ppermute | solution.py:416
  29.7 11.0 %collective-permute-start.7 = (bf16[208,256]{1,0:T(8,128)(2,1)S(1)}, bf16[208,256]{1,0:T(8,128)(2,1)S(1)}, u32[]{:S(2)}, u32[]{:S(2)}) collective-permute-start(bf16[208,256]{1,0:T(8,128)(2,1)S(1)} %get-tuple-element.48), channel_id=1, source_target_pairs={{0,8},{2,10},{4,12},{6,14},{8,0},{10,2},{12,4},{14,6},{1,9},{3,11}... | collective-permute-start | bytes 319496 | tf_op jit(solution)/shard_map/ppermute | solution.py:409
  30.7 10.1 %collective-permute-start.8 = (bf16[208,256]{1,0:T(8,128)(2,1)S(1)}, bf16[208,256]{1,0:T(8,128)(2,1)S(1)}, u32[]{:S(2)}, u32[]{:S(2)}) collective-permute-start(bf16[208,256]{1,0:T(8,128)(2,1)S(1)} %get-tuple-element.49), channel_id=1, source_target_pairs={{0,4},{2,6},{4,0},{6,2},{8,12},{10,14},{12,8},{14,10},{1,5},{3,7},... | collective-permute-start | bytes 319496 | tf_op jit(solution)/shard_map/ppermute | solution.py:409
  32.4 8.8 %collective-permute-start.2 = (bf16[192,256]{1,0:T(8,128)(2,1)S(1)}, bf16[192,256]{1,0:T(8,128)(2,1)S(1)}, u32[]{:S(2)}, u32[]{:S(2)}) collective-permute-start(bf16[192,256]{1,0:T(8,128)(2,1)S(1)} %get-tuple-element.41), channel_id=1, source_target_pairs={{0,12},{2,14},{4,8},{6,10},{8,4},{10,6},{12,0},{14,2},{1,13},{3,15... | collective-permute-start | bytes 294920 | tf_op jit(solution)/shard_map/ppermute | solution.py:409
  36.5 8.4 %collective-permute-start.3 = (bf16[192,256]{1,0:T(8,128)(2,1)S(1)}, bf16[192,256]{1,0:T(8,128)(2,1)S(1)}, u32[]{:S(2)}, u32[]{:S(2)}) collective-permute-start(bf16[192,256]{1,0:T(8,128)(2,1)S(1)} %get-tuple-element.42), channel_id=1, source_target_pairs={{0,8},{2,10},{4,12},{6,14},{8,0},{10,2},{12,4},{14,6},{1,9},{3,11}... | collective-permute-start | bytes 294920 | tf_op jit(solution)/shard_map/ppermute | solution.py:409
  36.5 8.4 %collective-permute-start.4 = (bf16[192,256]{1,0:T(8,128)(2,1)S(1)}, bf16[192,256]{1,0:T(8,128)(2,1)S(1)}, u32[]{:S(2)}, u32[]{:S(2)}) collective-permute-start(bf16[192,256]{1,0:T(8,128)(2,1)S(1)} %get-tuple-element.43), channel_id=1, source_target_pairs={{0,4},{2,6},{4,0},{6,2},{8,12},{10,14},{12,8},{14,10},{1,5},{3,7},... | collective-permute-start | bytes 294920 | tf_op jit(solution)/shard_map/ppermute | solution.py:409
  45.3 1.3 %collective-permute-start.13 = (f32[136,128]{1,0:T(8,128)S(1)}, f32[136,128]{1,0:T(8,128)S(1)}, u32[]{:S(2)}, u32[]{:S(2)}) collective-permute-start(f32[136,128]{1,0:T(8,128)S(1)} %get-tuple-element.59), channel_id=1, source_target_pairs={{0,1},{1,0},{2,3},{3,2},{4,5},{5,4},{6,7},{7,6},{8,9},{9,8},{10,11... | collective-permute-start | bytes 208904 | tf_op jit(solution)/shard_map/ppermute | solution.py:429
  46.6 4.4 %collective-permute-start.14 = (f32[136,128]{1,0:T(8,128)S(1)}, f32[136,128]{1,0:T(8,128)S(1)}, u32[]{:S(2)}, u32[]{:S(2)}) collective-permute-start(f32[136,128]{1,0:T(8,128)S(1)} %add.21), channel_id=1, source_target_pairs={{0,2},{2,0},{4,6},{6,4},{8,10},{10,8},{12,14},{14,12},{1,3},{3,1},... | collective-permute-start | bytes 208904 | tf_op jit(solution)/shard_map/ppermute | solution.py:433
  48.2 4.7 %collective-permute-start.15 = (f32[136,128]{1,0:T(8,128)S(1)}, f32[136,128]{1,0:T(8,128)S(1)}, u32[]{:S(2)}, u32[]{:S(2)}) collective-permute-start(f32[136,128]{1,0:T(8,128)S(1)} %add.21), channel_id=1, source_target_pairs={{0,4},{2,6},{4,0},{6,2},{8,12},{10,14},{12,8},{14,10},{1,5},{3,7},... | collective-permute-start | bytes 208904 | tf_op jit(solution)/shard_map/ppermute | solution.py:433
  48.2 5.6 %collective-permute-start.16 = (f32[136,128]{1,0:T(8,128)S(1)}, f32[136,128]{1,0:T(8,128)S(1)}, u32[]{:S(2)}, u32[]{:S(2)}) collective-permute-start(f32[136,128]{1,0:T(8,128)S(1)} %add.21), channel_id=1, source_target_pairs={{0,6},{2,4},{4,2},{6,0},{8,14},{10,12},{12,10},{14,8},{1,7},{3,5},... | collective-permute-start | bytes 208904 | tf_op jit(solution)/shard_map/ppermute | solution.py:433
  53.9 5.3 %collective-permute-start.17 = (f32[136,128]{1,0:T(8,128)S(1)}, f32[136,128]{1,0:T(8,128)S(1)}, u32[]{:S(2)}, u32[]{:S(2)}) collective-permute-start(f32[136,128]{1,0:T(8,128)S(1)} %add_add_fusion), channel_id=1, source_target_pairs={{0,8},{2,10},{4,12},{6,14},{8,0},{10,2},{12,4},{14,6},{1,9},{3,11}... | collective-permute-start | bytes 208904 | tf_op jit(solution)/shard_map/ppermute | solution.py:436
  59.1 1.3 %collective-permute-start.18 = (f32[136,128]{1,0:T(8,128)S(1)}, f32[136,128]{1,0:T(8,128)S(1)}, u32[]{:S(2)}, u32[]{:S(2)}) collective-permute-start(f32[136,128]{1,0:T(8,128)S(1)} %add.25.mine_ref), channel_id=1, source_target_pairs={{0,1},{1,0},{2,3},{3,2},{4,5},{5,4},{6,7},{7,6},{8,9},{9,8},{10,11... | collective-permute-start | bytes 208904 | tf_op jit(solution)/shard_map/ppermute | solution.py:437
